TPU v7x, 512 devices: a whole 4x8x8 slice. The times are simulated.
512 devices in a mesh: tm: 64 (over y_lo, z, core), head: 8 (over y_hi, x).
Axes of the slice: x: 4, y: 8 (y_hi: 2, y_lo: 4; y = y_hi * 4 + y_lo), z: 8, core: 2. Of those that a mesh axis runs over, the one named last changes fastest.
Arguments:
- queries: bfloat16 [32768, 2048], P('tm', 'head'), may hold values from -12 to 12
- keys: bfloat16 [32768, 2048], P('tm', 'head'), may hold values from -6 to 6
- values: bfloat16 [32768, 2048], P('tm', 'head'), may hold values from -6 to 6
- outputs: bfloat16 [32768, 2048], P('tm', 'head'), may hold values from -4 to 4
- out_cotangent: bfloat16 [32768, 2048], P('tm', 'head'), may hold values from -256 to 256
- out_weight: bfloat16 [2048, 2048], P(None, 'head'), may hold values from -0.125 to 0.125
- block_pick: int32 [64, 5], P('tm'), may hold values from 0 to 1
Outputs:
- query_grad: bfloat16 [32768, 2048], P('tm', 'head')
- key_grad: bfloat16 [32768, 2048], P('tm', 'head')
- value_grad: bfloat16 [32768, 2048], P('tm', 'head')
- weight_grad: float32 [2048, 2048], P('tm', 'head')
All inputs are finite; a program needn't handle non-finite values.
Results may differ from a plain program's by a relative error of at most 0.02.
Values may be sent and summed in bfloat16 or wider, within the bound.
No kernel may reach another device: no remote copies, remote signals or barrier semaphores. Data moves between devices by JAX's collectives and lax.ppermute only.
A program may use at most 64 MiB of HBM per device.

v0:
```python
import jax
import jax.numpy as jnp
from jax import lax
from jax.sharding import PartitionSpec as P

HD = 128
WIN = 256
BLK = 128
LEVELS = 5


def from_behind(block, axis, distance):
    devices = range(lax.axis_size(axis))
    route = [(i - distance, i) for i in devices if i - distance in devices]
    return lax.ppermute(block, axis, route)


def contract(left, right):
    return lax.dot_general(
        left, right, (((1,), (1,)), ((), ())), preferred_element_type=jnp.float32
    )


def on_device(queries, keys, values, outputs, out_cotangent, out_weight, block_pick):
    rows = queries.shape[0]
    width = queries.shape[1]
    heads_here = width // HD
    scale = HD ** (-0.5)
    shard = lax.axis_index("tm")
    shards = lax.axis_size("tm")
    gathered = lax.all_gather(out_cotangent, "head", axis=1, tiled=True)
    d_out = jnp.dot(gathered, out_weight, preferred_element_type=jnp.float32).astype(jnp.bfloat16)
    weight_grad = lax.psum_scatter(
        lax.dot_general(
            gathered, outputs, (((0,), (0,)), ((), ())), preferred_element_type=jnp.float32
        ),
        "tm",
        scatter_dimension=0,
        tiled=True,
    ) * (rows * shards) ** (-0.5)
    delta = jnp.sum(
        (d_out.astype(jnp.float32) * outputs.astype(jnp.float32)).reshape(rows, heads_here, HD),
        axis=2,
    )
    prev_keys, prev_values = from_behind((keys[rows - WIN :], values[rows - WIN :]), "tm", 1)
    far_key_list = []
    far_value_list = []
    far_flags = []
    for level in range(LEVELS):
        first = block_pick[0, level] * BLK
        block_keys = lax.dynamic_slice_in_dim(keys, first, BLK, 0)
        block_values = lax.dynamic_slice_in_dim(values, first, BLK, 0)
        got_keys, got_values = from_behind((block_keys, block_values), "tm", 2**level)
        far_key_list.append(got_keys)
        far_value_list.append(got_values)
        far_flags.append(jnp.full((BLK,), shard >= 2**level))
    far_keys = jnp.concatenate(far_key_list, axis=0)
    far_values = jnp.concatenate(far_value_list, axis=0)
    far_valid = jnp.concatenate(far_flags)
    near_keys = jnp.concatenate([prev_keys, keys], axis=0)
    near_values = jnp.concatenate([prev_values, values], axis=0)
    block = min(256, rows)
    dq_heads, dk_near, dv_near, dk_far, dv_far, lse_heads = ([], [], [], [], [], [])
    for head_no in range(heads_here):
        low = head_no * HD
        high = low + HD
        grad_q_parts = []
        lse_parts = []
        near_k_acc = jnp.zeros((WIN + rows, HD), jnp.float32)
        near_v_acc = jnp.zeros((WIN + rows, HD), jnp.float32)
        far_k_acc = jnp.zeros((LEVELS * BLK, HD), jnp.float32)
        far_v_acc = jnp.zeros((LEVELS * BLK, HD), jnp.float32)
        for first_row in range(0, rows, block):
            q_rows = queries[first_row : first_row + block, low:high]
            do_rows = d_out[first_row : first_row + block, low:high]
            delta_rows = delta[first_row : first_row + block, head_no]
            key_rows = jnp.concatenate(
                [near_keys[first_row : first_row + block + WIN, low:high], far_keys[:, low:high]],
                axis=0,
            )
            value_rows = jnp.concatenate(
                [
                    near_values[first_row : first_row + block + WIN, low:high],
                    far_values[:, low:high],
                ],
                axis=0,
            )
            qpos = first_row + jnp.arange(block)
            kpos = first_row - WIN + jnp.arange(block + WIN)
            dist = qpos[:, None] - kpos[None, :]
            window_ok = (dist >= 0) & (dist < WIN) & ((kpos >= 0) | (shard > 0))[None, :]
            mask = jnp.concatenate(
                [window_ok, jnp.broadcast_to(far_valid[None, :], (block, LEVELS * BLK))], axis=1
            )
            scores = contract(q_rows, key_rows) * scale
            masked = jnp.where(mask, scores, jnp.float32(-1e30))
            top = jnp.max(masked, axis=1)
            lse = top + jnp.log(jnp.sum(jnp.exp(masked - top[:, None]), axis=1))
            probs = jnp.exp(masked - lse[:, None])
            probs_b = probs.astype(jnp.bfloat16)
            dprobs = contract(do_rows, value_rows)
            dscores = (probs * (dprobs - delta_rows[:, None])).astype(jnp.bfloat16)
            grad_q_parts.append(
                jnp.dot(dscores, key_rows, preferred_element_type=jnp.float32) * scale
            )
            lse_parts.append(lse)
            dk_rows = jnp.dot(dscores.T, q_rows, preferred_element_type=jnp.float32) * scale
            dv_rows = jnp.dot(probs_b.T, do_rows, preferred_element_type=jnp.float32)
            near_k_acc = near_k_acc.at[first_row : first_row + block + WIN].add(
                dk_rows[: block + WIN]
            )
            near_v_acc = near_v_acc.at[first_row : first_row + block + WIN].add(
                dv_rows[: block + WIN]
            )
            far_k_acc = far_k_acc + dk_rows[block + WIN :]
            far_v_acc = far_v_acc + dv_rows[block + WIN :]
        dq_heads.append(jnp.concatenate(grad_q_parts, axis=0))
        lse_heads.append(jnp.concatenate(lse_parts, axis=0))
        dk_near.append(near_k_acc)
        dv_near.append(near_v_acc)
        dk_far.append(far_k_acc)
        dv_far.append(far_v_acc)
    query_grad = jnp.concatenate(dq_heads, axis=1).astype(jnp.bfloat16)
    near_k_all = jnp.concatenate(dk_near, axis=1)
    near_v_all = jnp.concatenate(dv_near, axis=1)
    far_k_all = jnp.concatenate(dk_far, axis=1)
    far_v_all = jnp.concatenate(dv_far, axis=1)
    own_k = near_k_all[WIN:]
    own_v = near_v_all[WIN:]
    back_k, back_v = from_behind((near_k_all[:WIN], near_v_all[:WIN]), "tm", -1)
    own_k = own_k.at[rows - WIN :].add(back_k)
    own_v = own_v.at[rows - WIN :].add(back_v)
    for level in range(LEVELS):
        got_k, got_v = from_behind(
            (
                far_k_all[level * BLK : (level + 1) * BLK],
                far_v_all[level * BLK : (level + 1) * BLK],
            ),
            "tm",
            -(2**level),
        )
        first = block_pick[0, level] * BLK
        own_k = lax.dynamic_update_slice_in_dim(
            own_k, lax.dynamic_slice_in_dim(own_k, first, BLK, 0) + got_k, first, 0
        )
        own_v = lax.dynamic_update_slice_in_dim(
            own_v, lax.dynamic_slice_in_dim(own_v, first, BLK, 0) + got_v, first, 0
        )
    return (query_grad, own_k.astype(jnp.bfloat16), own_v.astype(jnp.bfloat16), weight_grad)


def solution(mesh):
    placed = (
        P("tm", "head"),
        P("tm", "head"),
        P("tm", "head"),
        P("tm", "head"),
        P("tm", "head"),
        P(None, "head"),
        P("tm", None),
    )
    return jax.shard_map(
        on_device,
        mesh=mesh,
        in_specs=placed,
        out_specs=(P("tm", "head"), P("tm", "head"), P("tm", "head"), P("tm", "head")),
        check_vma=False,
    )
```

profile of v0, /device:TPU:1, one launch (start us, length us, event | category | flops | bytes accessed | tf_op | source)
XLA Modules:
  0.0 416.3 jit_solution(15605434833366984832)
XLA Ops:
  9.6 5.4 %collective-permute-start.6 = (bf16[256,256]{1,0:T(8,128)(2,1)}, bf16[256,256]{1,0:T(8,128)(2,1)}, u32[]{:S(2)}, u32[]{:S(2)}) collective-permute-start(bf16[256,256]{1,0:T(8,128)(2,1)} %slice.386), channel_id=1, source_target_pairs={{0,8},{8,16},{16,24},{24,32},{32,40},{40,48},{48,56},{56,64},{64,7... | collective-permute-start | bytes 393224 | tf_op jit(solution)/shard_map/ppermute | solution.py:15
  16.5 1.9 collective-permute-start
  24.3 3.2 collective-permute-start.11
  27.6 9.7 %collective-permute-start.10 = (bf16[128,256]{1,0:T(8,128)(2,1)S(1)}, bf16[128,256]{1,0:T(8,128)(2,1)S(1)}, u32[]{:S(2)}, u32[]{:S(2)}) collective-permute-start(bf16[128,256]{1,0:T(8,128)(2,1)S(1)} %get-tuple-element.155), channel_id=1, source_target_pairs={{0,64},{8,72},{16,80},{24,88},{32,96},{40,104},{48,112},{56,120},{... | collective-permute-start | bytes 196616 | tf_op jit(solution)/shard_map/ppermute | solution.py:15
  37.4 4.0 collective-permute-start.1
  45.8 3.1 collective-permute-start.2
  50.2 3.9 collective-permute-start.3
  55.4 7.1 %collective-permute-start.4 = (bf16[128,256]{1,0:T(8,128)(2,1)S(1)}, bf16[128,256]{1,0:T(8,128)(2,1)S(1)}, u32[]{:S(2)}, u32[]{:S(2)}) collective-permute-start(bf16[128,256]{1,0:T(8,128)(2,1)S(1)} %get-tuple-element.160), channel_id=1, source_target_pairs={{0,64},{8,72},{16,80},{24,88},{32,96},{40,104},{48,112},{56,120},{... | collective-permute-start | bytes 196616 | tf_op jit(solution)/shard_map/ppermute | solution.py:15
  63.8 12.0 %collective-permute-start.5 = (bf16[128,256]{1,0:T(8,128)(2,1)S(1)}, bf16[128,256]{1,0:T(8,128)(2,1)S(1)}, u32[]{:S(2)}, u32[]{:S(2)}) collective-permute-start(bf16[128,256]{1,0:T(8,128)(2,1)S(1)} %get-tuple-element.159), channel_id=1, source_target_pairs={{0,128},{8,136},{16,144},{24,152},{32,160},{40,168},{48,176},{56,1... | collective-permute-start | bytes 196616 | tf_op jit(solution)/shard_map/ppermute | solution.py:15
  77.1 5.8 %collective-permute-start.7 = (bf16[128,256]{1,0:T(8,128)(2,1)S(1)}, bf16[128,256]{1,0:T(8,128)(2,1)S(1)}, u32[]{:S(2)}, u32[]{:S(2)}) collective-permute-start(bf16[128,256]{1,0:T(8,128)(2,1)S(1)} %get-tuple-element.158), channel_id=1, source_target_pairs={{0,8},{8,16},{16,24},{24,32},{32,40},{40,48},{48,56},{56,64},{64,7... | collective-permute-start | bytes 196616 | tf_op jit(solution)/shard_map/ppermute | solution.py:15
  85.8 1.8 collective-permute-start.8
  89.0 5.0 %collective-permute-start.9 = (bf16[128,256]{1,0:T(8,128)(2,1)S(1)}, bf16[128,256]{1,0:T(8,128)(2,1)S(1)}, u32[]{:S(2)}, u32[]{:S(2)}) collective-permute-start(bf16[128,256]{1,0:T(8,128)(2,1)S(1)} %get-tuple-element.156), channel_id=1, source_target_pairs={{0,32},{8,40},{16,48},{24,56},{32,64},{40,72},{48,80},{56,88},{64,... | collective-permute-start | bytes 196616 | tf_op jit(solution)/shard_map/ppermute | solution.py:15
  103.2 2.4 bitcast_reduce_fusion
  118.1 2.1 fusion.107
  120.2 4.9 %collective-permute-start.12 = (f32[256,256]{0,1:T(8,128)}, f32[256,256]{0,1:T(8,128)S(1)}, u32[]{:S(2)}, u32[]{:S(2)}) collective-permute-start(f32[256,256]{0,1:T(8,128)} %pad_maximum_fusion.13), channel_id=1, source_target_pairs={{8,0},{16,8},{24,16},{32,24},{40,32},{48,40},{56,48},{64,56},{72,6... | collective-permute-start | bytes 786440 | tf_op jit(solution)/shard_map/ppermute | solution.py:15
  132.2 1.9 collective-permute-start.13
  135.4 1.9 collective-permute-start.18
  139.5 5.4 %collective-permute-done.18 = f32[256,256]{0,1:T(8,128)S(1)} collective-permute-done((f32[256,256]{0,1:T(8,128)S(1)}, f32[256,256]{0,1:T(8,128)S(1)}, u32[]{:S(2)}, u32[]{:S(2)}) %collective-permute-start.18) | collective-permute-done | bytes 262176 | tf_op jit(solution)/shard_map/ppermute | solution.py:15
  147.6 1.9 collective-permute-start.19
  149.5 3.3 collective-permute-done.15
  154.2 6.6 %collective-permute-done.16 = f32[128,256]{0,1:T(8,128)S(1)} collective-permute-done((f32[128,256]{0,1:T(8,128)S(1)}, f32[128,256]{0,1:T(8,128)S(1)}, u32[]{:S(2)}, u32[]{:S(2)}) %collective-permute-start.16) | collective-permute-done | bytes 131104 | tf_op jit(solution)/shard_map/ppermute | solution.py:15
  163.5 12.5 %collective-permute-done.21 = f32[128,256]{0,1:T(8,128)S(1)} collective-permute-done((f32[128,256]{0,1:T(8,128)S(1)}, f32[128,256]{0,1:T(8,128)S(1)}, u32[]{:S(2)}, u32[]{:S(2)}) %collective-permute-start.21) | collective-permute-done | bytes 131104 | tf_op jit(solution)/shard_map/ppermute | solution.py:15
  176.0 3.7 collective-permute-done.22
  181.7 226.5 %reduce-scatter.2.cloned.1.call-done = f32[32,256]{1,0:T(8,128)} async-done(((f32[2048,256]{1,0:T(8,128)}), f32[32,256]{1,0:T(8,128)}) %reduce-scatter.2.cloned.1.call-update) | async-done | bytes 32784 | tf_op jit(solution)/shard_map/reduce_scatter | solution.py:33
  (236 shorter events, 61.8 us)
Async XLA Ops:
  7.2 96.0 %all-gather.2.cloned.1.call-start = ((), (), s32[]{:S(2)}) async-start(), calls=%async_computation.1 | async-start | bytes 2359296 | tf_op jit(solution)/shard_map/all_gather | solution.py:31
  7.9 400.2 %reduce-scatter.2.cloned.1.call-start = ((), (), s32[]{:S(2)}) async-start(), calls=%async_computation.2 | async-start | bytes 2129920 | tf_op jit(solution)/shard_map/reduce_scatter | solution.py:33
  9.6 88.4 %collective-permute-start.6 = (bf16[256,256]{1,0:T(8,128)(2,1)}, bf16[256,256]{1,0:T(8,128)(2,1)}, u32[]{:S(2)}, u32[]{:S(2)}) collective-permute-start(bf16[256,256]{1,0:T(8,128)(2,1)} %slice.386), channel_id=1, source_target_pairs={{0,8},{8,16},{16,24},{24,32},{32,40},{40,48},{48,56},{56,64},{64,7... | collective-permute-start | bytes 393224 | tf_op jit(solution)/shard_map/ppermute | solution.py:15
  16.5 80.5 %collective-permute-start = (bf16[256,256]{1,0:T(8,128)(2,1)}, bf16[256,256]{1,0:T(8,128)(2,1)}, u32[]{:S(2)}, u32[]{:S(2)}) collective-permute-start(bf16[256,256]{1,0:T(8,128)(2,1)} %slice.376), channel_id=1, source_target_pairs={{0,8},{8,16},{16,24},{24,32},{32,40},{40,48},{48,56},{56,64},{64,7... | collective-permute-start | bytes 393224 | tf_op jit(solution)/shard_map/ppermute | solution.py:15
  24.3 71.0 %collective-permute-start.11 = (bf16[128,256]{1,0:T(8,128)(2,1)S(1)}, bf16[128,256]{1,0:T(8,128)(2,1)S(1)}, u32[]{:S(2)}, u32[]{:S(2)}) collective-permute-start(bf16[128,256]{1,0:T(8,128)(2,1)S(1)} %get-tuple-element.154), channel_id=1, source_target_pairs={{0,128},{8,136},{16,144},{24,152},{32,160},{40,168},{48,176},{56,1... | collective-permute-start | bytes 196616 | tf_op jit(solution)/shard_map/ppermute | solution.py:15
  27.6 67.8 %collective-permute-start.10 = (bf16[128,256]{1,0:T(8,128)(2,1)S(1)}, bf16[128,256]{1,0:T(8,128)(2,1)S(1)}, u32[]{:S(2)}, u32[]{:S(2)}) collective-permute-start(bf16[128,256]{1,0:T(8,128)(2,1)S(1)} %get-tuple-element.155), channel_id=1, source_target_pairs={{0,64},{8,72},{16,80},{24,88},{32,96},{40,104},{48,112},{56,120},{... | collective-permute-start | bytes 196616 | tf_op jit(solution)/shard_map/ppermute | solution.py:15
  37.4 8.4 %collective-permute-start.1 = (bf16[128,256]{1,0:T(8,128)(2,1)S(1)}, bf16[128,256]{1,0:T(8,128)(2,1)S(1)}, u32[]{:S(2)}, u32[]{:S(2)}) collective-permute-start(bf16[128,256]{1,0:T(8,128)(2,1)S(1)} %get-tuple-element.163), channel_id=1, source_target_pairs={{0,8},{8,16},{16,24},{24,32},{32,40},{40,48},{48,56},{56,64},{64,7... | collective-permute-start | bytes 196616 | tf_op jit(solution)/shard_map/ppermute | solution.py:15
  50.2 5.2 %collective-permute-start.3 = (bf16[128,256]{1,0:T(8,128)(2,1)S(1)}, bf16[128,256]{1,0:T(8,128)(2,1)S(1)}, u32[]{:S(2)}, u32[]{:S(2)}) collective-permute-start(bf16[128,256]{1,0:T(8,128)(2,1)S(1)} %get-tuple-element.161), channel_id=1, source_target_pairs={{0,32},{8,40},{16,48},{24,56},{32,64},{40,72},{48,80},{56,88},{64,... | collective-permute-start | bytes 196616 | tf_op jit(solution)/shard_map/ppermute | solution.py:15
  55.4 8.4 %collective-permute-start.4 = (bf16[128,256]{1,0:T(8,128)(2,1)S(1)}, bf16[128,256]{1,0:T(8,128)(2,1)S(1)}, u32[]{:S(2)}, u32[]{:S(2)}) collective-permute-start(bf16[128,256]{1,0:T(8,128)(2,1)S(1)} %get-tuple-element.160), channel_id=1, source_target_pairs={{0,64},{8,72},{16,80},{24,88},{32,96},{40,104},{48,112},{56,120},{... | collective-permute-start | bytes 196616 | tf_op jit(solution)/shard_map/ppermute | solution.py:15
  63.8 13.3 %collective-permute-start.5 = (bf16[128,256]{1,0:T(8,128)(2,1)S(1)}, bf16[128,256]{1,0:T(8,128)(2,1)S(1)}, u32[]{:S(2)}, u32[]{:S(2)}) collective-permute-start(bf16[128,256]{1,0:T(8,128)(2,1)S(1)} %get-tuple-element.159), channel_id=1, source_target_pairs={{0,128},{8,136},{16,144},{24,152},{32,160},{40,168},{48,176},{56,1... | collective-permute-start | bytes 196616 | tf_op jit(solution)/shard_map/ppermute | solution.py:15
  77.1 8.7 %collective-permute-start.7 = (bf16[128,256]{1,0:T(8,128)(2,1)S(1)}, bf16[128,256]{1,0:T(8,128)(2,1)S(1)}, u32[]{:S(2)}, u32[]{:S(2)}) collective-permute-start(bf16[128,256]{1,0:T(8,128)(2,1)S(1)} %get-tuple-element.158), channel_id=1, source_target_pairs={{0,8},{8,16},{16,24},{24,32},{32,40},{40,48},{48,56},{56,64},{64,7... | collective-permute-start | bytes 196616 | tf_op jit(solution)/shard_map/ppermute | solution.py:15
  89.0 6.4 %collective-permute-start.9 = (bf16[128,256]{1,0:T(8,128)(2,1)S(1)}, bf16[128,256]{1,0:T(8,128)(2,1)S(1)}, u32[]{:S(2)}, u32[]{:S(2)}) collective-permute-start(bf16[128,256]{1,0:T(8,128)(2,1)S(1)} %get-tuple-element.156), channel_id=1, source_target_pairs={{0,32},{8,40},{16,48},{24,56},{32,64},{40,72},{48,80},{56,88},{64,... | collective-permute-start | bytes 196616 | tf_op jit(solution)/shard_map/ppermute | solution.py:15
  120.2 17.9 %collective-permute-start.12 = (f32[256,256]{0,1:T(8,128)}, f32[256,256]{0,1:T(8,128)S(1)}, u32[]{:S(2)}, u32[]{:S(2)}) collective-permute-start(f32[256,256]{0,1:T(8,128)} %pad_maximum_fusion.13), channel_id=1, source_target_pairs={{8,0},{16,8},{24,16},{32,24},{40,32},{48,40},{56,48},{64,56},{72,6... | collective-permute-start | bytes 786440 | tf_op jit(solution)/shard_map/ppermute | solution.py:15
  130.9 48.9 %collective-permute-start.17 = (f32[128,256]{0,1:T(8,128)S(1)}, f32[128,256]{0,1:T(8,128)S(1)}, u32[]{:S(2)}, u32[]{:S(2)}) collective-permute-start(f32[128,256]{0,1:T(8,128)S(1)} %get-tuple-element.137), channel_id=1, source_target_pairs={{128,0},{136,8},{144,16},{152,24},{160,32},{168,40},{176,48},{184,... | collective-permute-start | bytes 393224 | tf_op jit(solution)/shard_map/ppermute | solution.py:15
  132.2 14.0 %collective-permute-start.13 = (f32[128,256]{0,1:T(8,128)S(1)}, f32[128,256]{0,1:T(8,128)S(1)}, u32[]{:S(2)}, u32[]{:S(2)}) collective-permute-start(f32[128,256]{0,1:T(8,128)S(1)} %get-tuple-element.138), channel_id=1, source_target_pairs={{8,0},{16,8},{24,16},{32,24},{40,32},{48,40},{56,48},{64,56},{72,6... | collective-permute-start | bytes 393224 | tf_op jit(solution)/shard_map/ppermute | solution.py:15
  134.1 13.5 %collective-permute-start.14 = (f32[128,256]{0,1:T(8,128)S(1)}, f32[128,256]{0,1:T(8,128)S(1)}, u32[]{:S(2)}, u32[]{:S(2)}) collective-permute-start(f32[128,256]{0,1:T(8,128)S(1)} %get-tuple-element.139), channel_id=1, source_target_pairs={{16,0},{24,8},{32,16},{40,24},{48,32},{56,40},{64,48},{72,56},{80,... | collective-permute-start | bytes 393224 | tf_op jit(solution)/shard_map/ppermute | solution.py:15
  135.4 9.5 %collective-permute-start.18 = (f32[256,256]{0,1:T(8,128)S(1)}, f32[256,256]{0,1:T(8,128)S(1)}, u32[]{:S(2)}, u32[]{:S(2)}) collective-permute-start(f32[256,256]{0,1:T(8,128)S(1)} %pad_maximum_fusion.12), channel_id=1, source_target_pairs={{8,0},{16,8},{24,16},{32,24},{40,32},{48,40},{56,48},{64,56},{72,6... | collective-permute-start | bytes 786440 | tf_op jit(solution)/shard_map/ppermute | solution.py:15
  138.1 14.7 %collective-permute-start.15 = (f32[128,256]{0,1:T(8,128)S(1)}, f32[128,256]{0,1:T(8,128)S(1)}, u32[]{:S(2)}, u32[]{:S(2)}) collective-permute-start(f32[128,256]{0,1:T(8,128)S(1)} %get-tuple-element.140), channel_id=1, source_target_pairs={{32,0},{40,8},{48,16},{56,24},{64,32},{72,40},{80,48},{88,56},{96,... | collective-permute-start | bytes 393224 | tf_op jit(solution)/shard_map/ppermute | solution.py:15
  144.9 15.9 %collective-permute-start.16 = (f32[128,256]{0,1:T(8,128)S(1)}, f32[128,256]{0,1:T(8,128)S(1)}, u32[]{:S(2)}, u32[]{:S(2)}) collective-permute-start(f32[128,256]{0,1:T(8,128)S(1)} %get-tuple-element.141), channel_id=1, source_target_pairs={{64,0},{72,8},{80,16},{88,24},{96,32},{104,40},{112,48},{120,56},{... | collective-permute-start | bytes 393224 | tf_op jit(solution)/shard_map/ppermute | solution.py:15
  146.2 33.6 %collective-permute-start.23 = (f32[128,256]{0,1:T(8,128)S(1)}, f32[128,256]{0,1:T(8,128)S(1)}, u32[]{:S(2)}, u32[]{:S(2)}) collective-permute-start(f32[128,256]{0,1:T(8,128)S(1)} %get-tuple-element.132), channel_id=1, source_target_pairs={{128,0},{136,8},{144,16},{152,24},{160,32},{168,40},{176,48},{184,... | collective-permute-start | bytes 393224 | tf_op jit(solution)/shard_map/ppermute | solution.py:15
  147.6 14.5 %collective-permute-start.19 = (f32[128,256]{0,1:T(8,128)S(1)}, f32[128,256]{0,1:T(8,128)S(1)}, u32[]{:S(2)}, u32[]{:S(2)}) collective-permute-start(f32[128,256]{0,1:T(8,128)S(1)} %get-tuple-element.133), channel_id=1, source_target_pairs={{8,0},{16,8},{24,16},{32,24},{40,32},{48,40},{56,48},{64,56},{72,6... | collective-permute-start | bytes 393224 | tf_op jit(solution)/shard_map/ppermute | solution.py:15
  152.8 10.6 %collective-permute-start.20 = (f32[128,256]{0,1:T(8,128)S(1)}, f32[128,256]{0,1:T(8,128)S(1)}, u32[]{:S(2)}, u32[]{:S(2)}) collective-permute-start(f32[128,256]{0,1:T(8,128)S(1)} %get-tuple-element.134), channel_id=1, source_target_pairs={{16,0},{24,8},{32,16},{40,24},{48,32},{56,40},{64,48},{72,56},{80,... | collective-permute-start | bytes 393224 | tf_op jit(solution)/shard_map/ppermute | solution.py:15
  160.8 15.2 %collective-permute-start.21 = (f32[128,256]{0,1:T(8,128)S(1)}, f32[128,256]{0,1:T(8,128)S(1)}, u32[]{:S(2)}, u32[]{:S(2)}) collective-permute-start(f32[128,256]{0,1:T(8,128)S(1)} %get-tuple-element.135), channel_id=1, source_target_pairs={{32,0},{40,8},{48,16},{56,24},{64,32},{72,40},{80,48},{88,56},{96,... | collective-permute-start | bytes 393224 | tf_op jit(solution)/shard_map/ppermute | solution.py:15
  162.1 17.6 %collective-permute-start.22 = (f32[128,256]{0,1:T(8,128)S(1)}, f32[128,256]{0,1:T(8,128)S(1)}, u32[]{:S(2)}, u32[]{:S(2)}) collective-permute-start(f32[128,256]{0,1:T(8,128)S(1)} %get-tuple-element.136), channel_id=1, source_target_pairs={{64,0},{72,8},{80,16},{88,24},{96,32},{104,40},{112,48},{120,56},{... | collective-permute-start | bytes 393224 | tf_op jit(solution)/shard_map/ppermute | solution.py:15
  (52 other events, 402.9 us)
Sparse Core Ops, SparseCore 0:
  11.1 80.4 all-gather.1
  120.4 287.7 reduce-scatter.1
where the time goes:
time: 423 us; the launch traced here: 416 us
  waiting for transfers between devices  268 us (63%)
  starting transfers between devices  83.9 us (20%)
  local copies, waits for them, and re-layouts  22.4 us (5%)
  between operations  18.5 us (4%)
  matrix products  14.7 us (3%)
  other arithmetic  8.68 us (2%)
    reduce_scatter x1, waiting for transfers between devices, on_device(): lax.psum_scatter(lax.dot_general(gathered, outputs, (((0,), (0,)), ((), (...  226 us
    ppermute x24, starting transfers between devices, from_behind(): return lax.ppermute(block, axis, route)  83.9 us
    ppermute x24, waiting for transfers between devices, from_behind(): return lax.ppermute(block, axis, route)  40.9 us
    unnamed x117, local copies, waits for them, and re-layouts  13.5 us
  transfers between devices with their start and end apart: 26, of which 13 were waited for; matrix products, arithmetic and copies ran while one was open for 6% of the time, Pallas kernels for 0%

commit v1 on v0

v1 whole, which is shorter than its diff:
```python
import functools

import jax
import jax.numpy as jnp
from jax import lax
from jax.experimental import pallas as pl
from jax.experimental.pallas import tpu as pltpu
from jax.sharding import PartitionSpec as P

HD = 128
WIN = 256
BLK = 128
LEVELS = 5
BF = jnp.bfloat16
F32 = jnp.float32
NX, NZ, NYL = 4, 8, 4
VMEM = pl.BlockSpec(memory_space=pltpu.VMEM)
SMEM = pl.BlockSpec(memory_space=pltpu.SMEM)


def params():
    return pltpu.CompilerParams(vmem_limit_bytes=40 * 1024 * 1024)


def dot(a, b, ca, cb):
    return lax.dot_general(a, b, (((ca,), (cb,)), ((), ())), preferred_element_type=F32)


def pack_kernel(info, k_ref, v_ref, near_ref, *far_refs):
    near_ref[0:WIN, :] = k_ref[512 - WIN :, :]
    near_ref[WIN : 2 * WIN, :] = v_ref[512 - WIN :, :]
    for level in range(LEVELS):
        first = pl.multiple_of(info[2 + level] * BLK, BLK)
        ref, at = (near_ref, 2 * WIN) if level == 0 else (far_refs[level - 1], 0)
        ref[at : at + BLK, :] = k_ref[pl.ds(first, BLK), :]
        ref[at + BLK : at + 2 * BLK, :] = v_ref[pl.ds(first, BLK), :]


def pack(info, keys, values):
    return pl.pallas_call(
        pack_kernel,
        out_shape=[jax.ShapeDtypeStruct((2 * WIN + 2 * BLK, 256), BF)]
        + [jax.ShapeDtypeStruct((2 * BLK, 256), BF)] * (LEVELS - 1),
        in_specs=[SMEM, VMEM, VMEM],
        out_specs=[VMEM] * LEVELS,
        compiler_params=params(),
        name="pack",
    )(info, keys, values)


def project_kernel(info, *refs):
    pieces = refs[:8]
    w_ref, o_ref, dout_ref, keep_ref, send_ref = refs[8:]
    core, head = info[0] % 2, info[1]
    yh, x = head // NX, head % NX
    o = o_ref[...]
    acc = jnp.zeros((512, 256), F32)
    for at in range(8):
        src = (yh ^ (at // NX)) * NX + (x + NX - at % NX) % NX
        cot = pieces[at][...]
        acc = acc + dot(cot, w_ref[pl.ds(pl.multiple_of(src * 256, 256), 256), :], 1, 0)
        term = dot(cot, o, 0, 0).astype(BF)
        yl, z0 = src // 2, (src % 2) * 4
        for sub in range(4):
            rows = pl.ds(pl.multiple_of((z0 + sub) * 128 + yl * 32, 32), 32)
            low = term[sub * 64 : sub * 64 + 32, :]
            high = term[sub * 64 + 32 : sub * 64 + 64, :]
            keep_ref[rows, :] = jnp.where(core == 0, low, high)
            send_ref[rows, :] = jnp.where(core == 0, high, low)
    dout_ref[...] = acc.astype(BF)


def project(info, pieces, out_weight, outputs):
    half = jax.ShapeDtypeStruct((1024, 256), BF)
    return pl.pallas_call(
        project_kernel,
        out_shape=[jax.ShapeDtypeStruct((512, 256), BF), half, half],
        in_specs=[SMEM] + [VMEM] * 10,
        out_specs=[VMEM] * 3,
        compiler_params=params(),
        name="project",
    )(info, *pieces, out_weight, outputs)


def attend_kernel(
    info, q_ref, k_ref, v_ref, o_ref, do_ref, near_ref, f1, f2, f3, f4,
    dq_ref, own_k, own_v, back_near, b1, b2, b3, b4,
    nk, nv, fk, fv,
):
    scale = HD ** (-0.5)
    shard = info[0]
    fars = (near_ref, f1, f2, f3, f4)
    neg = jnp.float32(-1e30)
    row = lax.broadcasted_iota(jnp.int32, (256, 256), 0)
    col = lax.broadcasted_iota(jnp.int32, (256, 256), 1)
    earlier = row > col
    level_of = lax.broadcasted_iota(jnp.int32, (LEVELS * BLK, 256), 0) // BLK
    far_ok = shard >= (1 << level_of)
    for head in range(2):
        lanes = slice(head * HD, (head + 1) * HD)
        k_far = jnp.concatenate(
            [r[(2 * WIN if i == 0 else 0) :, lanes][:BLK] for i, r in enumerate(fars)], axis=0
        )
        v_far = jnp.concatenate(
            [r[(2 * WIN if i == 0 else 0) + BLK :, lanes] for i, r in enumerate(fars)], axis=0
        )
        fk_acc = fv_acc = None
        mid = None
        for blk in range(2):
            rows = slice(blk * 256, (blk + 1) * 256)
            q = q_ref[rows, lanes]
            do = do_ref[rows, lanes]
            k_here, v_here = k_ref[rows, lanes], v_ref[rows, lanes]
            if blk == 0:
                k_prev, v_prev = near_ref[0:WIN, lanes], near_ref[WIN : 2 * WIN, lanes]
            else:
                k_prev, v_prev = k_ref[0:256, lanes], v_ref[0:256, lanes]
            delta = jnp.sum(
                do.astype(F32) * o_ref[rows, lanes].astype(F32), axis=1, keepdims=True
            )
            delta = jnp.transpose(jnp.broadcast_to(delta, (256, 128)))[0:1, :]
            s_prev = dot(k_prev, q, 1, 1)
            s_here = dot(k_here, q, 1, 1)
            s_far = dot(k_far, q, 1, 1)
            if blk == 0:
                s_prev = jnp.where(shard > 0, s_prev * scale, neg)
            else:
                s_prev = s_prev * scale
            s_near = jnp.where(earlier, s_prev, s_here * scale)
            s_far = jnp.where(far_ok, s_far * scale, neg)
            top = jnp.maximum(
                jnp.max(s_near, axis=0, keepdims=True), jnp.max(s_far, axis=0, keepdims=True)
            )
            e_near, e_far = jnp.exp(s_near - top), jnp.exp(s_far - top)
            inv = 1.0 / (
                jnp.sum(e_near, axis=0, keepdims=True) + jnp.sum(e_far, axis=0, keepdims=True)
            )
            p_near, p_far = e_near * inv, e_far * inv
            dp_near = jnp.where(earlier, dot(v_prev, do, 1, 1), dot(v_here, do, 1, 1))
            dp_far = dot(v_far, do, 1, 1)
            ds_near = p_near * (dp_near - delta)
            ds_far = (p_far * (dp_far - delta)).astype(BF)
            zero = jnp.zeros((), F32)
            ds_prev = jnp.where(earlier, ds_near, zero).astype(BF)
            ds_here = jnp.where(earlier, zero, ds_near).astype(BF)
            p_prev = jnp.where(earlier, p_near, zero).astype(BF)
            p_here = jnp.where(earlier, zero, p_near).astype(BF)
            p_far = p_far.astype(BF)
            dq = dot(ds_prev, k_prev, 0, 0) + dot(ds_here, k_here, 0, 0) + dot(ds_far, k_far, 0, 0)
            dq_ref[rows, lanes] = (dq * scale).astype(BF)
            dk_prev, dv_prev = dot(ds_prev, q, 1, 0) * scale, dot(p_prev, do, 1, 0)
            dk_here, dv_here = dot(ds_here, q, 1, 0) * scale, dot(p_here, do, 1, 0)
            dk_far, dv_far = dot(ds_far, q, 1, 0) * scale, dot(p_far, do, 1, 0)
            if blk == 0:
                back_near[0:WIN, lanes] = dk_prev.astype(BF)
                back_near[WIN : 2 * WIN, lanes] = dv_prev.astype(BF)
                own_k[0:256, lanes] = dk_here
                own_v[0:256, lanes] = dv_here
                fk[...] = dk_far
                fv[...] = dv_far
            else:
                own_k[0:256, lanes] += dk_prev
                own_v[0:256, lanes] += dv_prev
                own_k[256:512, lanes] = dk_here
                own_v[256:512, lanes] = dv_here
                for i, r in enumerate((back_near, b1, b2, b3, b4)):
                    at = 2 * WIN if i == 0 else 0
                    part = slice(i * BLK, (i + 1) * BLK)
                    r[at : at + BLK, lanes] = (fk[part, :] + dk_far[part]).astype(BF)
                    r[at + BLK : at + 2 * BLK, lanes] = (fv[part, :] + dv_far[part]).astype(BF)


def attend(info, queries, keys, values, outputs, d_out, got):
    f32s = jax.ShapeDtypeStruct((512, 256), F32)
    far = jax.ShapeDtypeStruct((2 * BLK, 256), BF)
    return pl.pallas_call(
        attend_kernel,
        out_shape=[
            jax.ShapeDtypeStruct((512, 256), BF), f32s, f32s,
            jax.ShapeDtypeStruct((2 * WIN + 2 * BLK, 256), BF), far, far, far, far,
        ],
        in_specs=[SMEM] + [VMEM] * 10,
        out_specs=[VMEM] * 8,
        scratch_shapes=[
            pltpu.VMEM((8, 128), F32), pltpu.VMEM((8, 128), F32),
            pltpu.VMEM((LEVELS * BLK, HD), F32), pltpu.VMEM((LEVELS * BLK, HD), F32),
        ],
        compiler_params=params(),
        name="attend",
    )(info, queries, keys, values, outputs, d_out, *got)


def finish_kernel(info, own_k, own_v, near_ref, f1, f2, f3, f4, dk_ref, dv_ref, tk, tv):
    for ref, acc, at in ((own_k, tk, 0), (own_v, tv, 1)):
        acc[0:256, :] = ref[0:256, :]
        acc[256:512, :] = ref[256:512, :] + near_ref[at * WIN : (at + 1) * WIN, :].astype(F32)
        for level, far in enumerate((near_ref, f1, f2, f3, f4)):
            low = (2 * WIN if level == 0 else 0) + at * BLK
            rows = pl.ds(pl.multiple_of(info[2 + level] * BLK, BLK), BLK)
            acc[rows, :] += far[low : low + BLK, :].astype(F32)
    dk_ref[...] = tk[...].astype(BF)
    dv_ref[...] = tv[...].astype(BF)


def finish(info, own_k, own_v, got):
    out = jax.ShapeDtypeStruct((512, 256), BF)
    return pl.pallas_call(
        finish_kernel,
        out_shape=[out, out],
        in_specs=[SMEM] + [VMEM] * 7,
        out_specs=[VMEM] * 2,
        scratch_shapes=[pltpu.VMEM((512, 256), F32)] * 2,
        compiler_params=params(),
        name="finish",
    )(info, own_k, own_v, *got)


def shift(block, distance):
    return lax.ppermute(
        block, "tm", [(i, i + distance) for i in range(64) if 0 <= i + distance < 64]
    )


def turn_x(block, offset):
    return lax.ppermute(
        block, "head", [(h, h // NX * NX + (h % NX + offset) % NX) for h in range(2 * NX)]
    )


def on_device(queries, keys, values, outputs, out_cotangent, out_weight, block_pick):
    shard = lax.axis_index("tm")
    info = jnp.concatenate(
        [
            shard.astype(jnp.int32)[None],
            lax.axis_index("head").astype(jnp.int32)[None],
            block_pick[0],
        ]
    )
    other = lax.ppermute(out_cotangent, "head", [(h, (h + NX) % (2 * NX)) for h in range(2 * NX)])
    mine = [out_cotangent] + [turn_x(out_cotangent, o) for o in range(1, NX)]
    packed = pack(info, keys, values)
    got = [shift(b, 2**level) for level, b in enumerate(packed)]
    theirs = [other] + [turn_x(other, o) for o in range(1, NX)]
    d_out, keep, send = project(info, mine + theirs, out_weight, outputs)
    received = lax.ppermute(send, "tm", [(i, i ^ 1) for i in range(64)])
    dq, own_k, own_v, *back = attend(info, queries, keys, values, outputs, d_out, got)
    back = [shift(b, -(2**level)) for level, b in enumerate(back)]
    half = (keep.astype(F32) + received.astype(F32)).astype(BF).reshape(NZ, NYL * 32, 256)
    z_groups = [[yl * 16 + z * 2 + c for z in range(NZ)] for yl in range(NYL) for c in range(2)]
    half = lax.all_to_all(half, "tm", 0, 0, axis_index_groups=z_groups)
    part = jnp.sum(half.astype(F32), axis=0).astype(BF).reshape(NYL, 32, 256)
    y_groups = [[yl * 16 + zc for yl in range(NYL)] for zc in range(16)]
    part = lax.all_to_all(part, "tm", 0, 0, axis_index_groups=y_groups)
    weight_grad = jnp.sum(part.astype(F32), axis=0) * (512 * 64) ** (-0.5)
    dk, dv = finish(info, own_k, own_v, back)
    return dq, dk, dv, weight_grad


def solution(mesh):
    placed = (P("tm", "head"),) * 5 + (P(None, "head"), P("tm", None))
    return jax.shard_map(
        on_device,
        mesh=mesh,
        in_specs=placed,
        out_specs=(P("tm", "head"),) * 4,
        check_vma=False,
    )
```

time: 423 us -> 135 us (0.32)
  waiting for transfers between devices: 268 us -> 27.2 us
  local copies, waits for them, and re-layouts: 22.4 us -> 3.79 us
  between operations: 18.5 us -> 0.91 us
  matrix products: 14.7 us -> 0 us
  Pallas kernels: 0 us -> 10 us
  other arithmetic: 8.68 us -> 2.36 us
  starting transfers between devices: 83.9 us -> 88.2 us
    reduce_scatter x1 -> x0, waiting for transfers between devices: 226 us -> none  [on_device(): lax.psum_scatter(lax.dot_general(gathered, outputs, (((0,), (0,)), ((), (...]
    all_to_all x0 -> x2, starting transfers between devices: none -> 32.6 us  [the longest x1 22.5 us: on_device(): part = lax.all_to_all(part, 'tm', 0, 0, axis_index_groups=y_groups)]
    ppermute x24 -> x18, starting transfers between devices: 83.9 us -> 55.6 us  [the longest x10 26.3 us: shift(): lax.ppermute(block, 'tm', [(i, i + distance) for i in range(64) if 0 <= i...]
    ppermute x24 -> x18, waiting for transfers between devices: 40.9 us -> 20 us  [the longest x6 13.7 us: turn_x(): lax.ppermute(block, 'head', [(h, h // NX * NX + (h % NX + offset) % NX) f...]
    dot_general x22 -> x0, matrix products: 14.7 us -> none  [the longest x8 3.8 us: contract(): lax.dot_general(left, right, (((1,), (1,)), ((), ())), preferred_element_...]
    pallas_call x0 -> x4, Pallas kernels: none -> 10 us  [the longest x1 6.04 us: attend(): pl.pallas_call(attend_kernel, out_shape=[jax.ShapeDtypeStruct((512, 256),...]
    unnamed x117 -> x16, local copies, waits for them, and re-layouts: 13.5 us -> 3.79 us
    slice x10 -> x0, local copies, waits for them, and re-layouts: 7.59 us -> none  [the longest x1 1.6 us: on_device(): values[rows - WIN:]]
  transfers between devices with their start and end apart: 26 -> 20, of which waited for: 13 -> 9; matrix products, arithmetic and copies ran while one was open for 6% -> 1% of each run, Pallas kernels for 0% -> 6%
where the time goes in v1:
time: 135 us; the launch traced here: 132 us
  starting transfers between devices  88.2 us (65%)
  waiting for transfers between devices  27.2 us (20%)
  Pallas kernels  10 us (7%)
  local copies, waits for them, and re-layouts  3.79 us (3%)
  other arithmetic  2.36 us (2%)
    ppermute x10, starting transfers between devices, shift(): lax.ppermute(block, 'tm', [(i, i + distance) for i in range(64) if 0 <= i...  26.3 us
    all_to_all x1, starting transfers between devices, on_device(): part = lax.all_to_all(part, 'tm', 0, 0, axis_index_groups=y_groups)  22.5 us
    ppermute x6, starting transfers between devices, turn_x(): lax.ppermute(block, 'head', [(h, h // NX * NX + (h % NX + offset) % NX) f...  18.4 us
    ppermute x6, waiting for transfers between devices, turn_x(): lax.ppermute(block, 'head', [(h, h // NX * NX + (h % NX + offset) % NX) f...  13.7 us
    all_to_all x1, starting transfers between devices, on_device(): half = lax.all_to_all(half, 'tm', 0, 0, axis_index_groups=z_groups)  10.2 us
    ppermute x1, starting transfers between devices, on_device(): lax.ppermute(out_cotangent, 'head', [(h, (h + NX) % (2 * NX)) for h in ra...  8.28 us
    all_to_all x1, waiting for transfers between devices, on_device(): part = lax.all_to_all(part, 'tm', 0, 0, axis_index_groups=y_groups)  7.21 us
    pallas_call x1, Pallas kernels, attend(): pl.pallas_call(attend_kernel, out_shape=[jax.ShapeDtypeStruct((512, 256),...  6.04 us
  transfers between devices with their start and end apart: 20, of which 9 were waited for; matrix products, arithmetic and copies ran while one was open for 1% of the time, Pallas kernels for 6%

profile of v1, /device:TPU:1, one launch (start us, length us, event | category | flops | bytes accessed | tf_op | source)
XLA Modules:
  0.0 132.5 jit_solution(15595063234966110799)
XLA Ops:
  0.6 8.3 %collective-permute-start.3 = (bf16[512,256]{1,0:T(8,128)(2,1)}, bf16[512,256]{1,0:T(8,128)(2,1)S(1)}, u32[]{:S(2)}, u32[]{:S(2)}) collective-permute-start(bf16[512,256]{1,0:T(8,128)(2,1)} %refs_0_.1), channel_id=1, source_target_pairs={{0,4},{1,5},{2,6},{3,7},{4,0},{5,1},{6,2},{7,3},{8,12},{9,13},{10,... | collective-permute-start | bytes 786440 | tf_op jit(solution)/shard_map/ppermute | solution.py:239
  8.9 4.4 %collective-permute-start.2 = (bf16[512,256]{1,0:T(8,128)(2,1)}, bf16[512,256]{1,0:T(8,128)(2,1)S(1)}, u32[]{:S(2)}, u32[]{:S(2)}) collective-permute-start(bf16[512,256]{1,0:T(8,128)(2,1)} %refs_0_.1), channel_id=1, source_target_pairs={{0,3},{1,0},{2,1},{3,2},{4,7},{5,4},{6,5},{7,6},{8,11},{9,8},{10,9... | collective-permute-start | bytes 786440 | tf_op jit(solution)/shard_map/ppermute | solution.py:225
  13.3 2.4 %collective-permute-start.1 = (bf16[512,256]{1,0:T(8,128)(2,1)}, bf16[512,256]{1,0:T(8,128)(2,1)S(1)}, u32[]{:S(2)}, u32[]{:S(2)}) collective-permute-start(bf16[512,256]{1,0:T(8,128)(2,1)} %refs_0_.1), channel_id=1, source_target_pairs={{0,2},{1,3},{2,0},{3,1},{4,6},{5,7},{6,4},{7,5},{8,10},{9,11},{10,... | collective-permute-start | bytes 786440 | tf_op jit(solution)/shard_map/ppermute | solution.py:225
  15.8 2.5 %collective-permute-start = (bf16[512,256]{1,0:T(8,128)(2,1)}, bf16[512,256]{1,0:T(8,128)(2,1)S(1)}, u32[]{:S(2)}, u32[]{:S(2)}) collective-permute-start(bf16[512,256]{1,0:T(8,128)(2,1)} %refs_0_.1), channel_id=1, source_target_pairs={{0,1},{1,2},{2,3},{3,0},{4,5},{5,6},{6,7},{7,4},{8,9},{9,10},{10,1... | collective-permute-start | bytes 786440 | tf_op jit(solution)/shard_map/ppermute | solution.py:225
  18.3 4.0 %collective-permute-start.6 = (bf16[512,256]{1,0:T(8,128)(2,1)S(1)}, bf16[512,256]{1,0:T(8,128)(2,1)S(1)}, u32[]{:S(2)}, u32[]{:S(2)}) collective-permute-start(bf16[512,256]{1,0:T(8,128)(2,1)S(1)} %collective-permute-done.3.refs_4_), channel_id=1, source_target_pairs={{0,3},{1,0},{2,1},{3,2},{4,7},{5,4},{6,5},{7,6},{8,11},{9,8},{10,9... | collective-permute-start | bytes 786440 | tf_op jit(solution)/shard_map/ppermute | solution.py:225
  22.3 3.1 %collective-permute-start.5 = (bf16[512,256]{1,0:T(8,128)(2,1)S(1)}, bf16[512,256]{1,0:T(8,128)(2,1)S(1)}, u32[]{:S(2)}, u32[]{:S(2)}) collective-permute-start(bf16[512,256]{1,0:T(8,128)(2,1)S(1)} %collective-permute-done.3.refs_4_), channel_id=1, source_target_pairs={{0,2},{1,3},{2,0},{3,1},{4,6},{5,7},{6,4},{7,5},{8,10},{9,11},{10,... | collective-permute-start | bytes 786440 | tf_op jit(solution)/shard_map/ppermute | solution.py:225
  25.4 1.9 %collective-permute-start.4 = (bf16[512,256]{1,0:T(8,128)(2,1)S(1)}, bf16[512,256]{1,0:T(8,128)(2,1)S(1)}, u32[]{:S(2)}, u32[]{:S(2)}) collective-permute-start(bf16[512,256]{1,0:T(8,128)(2,1)S(1)} %collective-permute-done.3.refs_4_), channel_id=1, source_target_pairs={{0,1},{1,2},{2,3},{3,0},{4,5},{5,6},{6,7},{7,4},{8,9},{9,10},{10,1... | collective-permute-start | bytes 786440 | tf_op jit(solution)/shard_map/ppermute | solution.py:225
  28.1 4.2 %collective-permute-done.refs_1_ = bf16[512,256]{1,0:T(8,128)(2,1)S(1)} collective-permute-done((bf16[512,256]{1,0:T(8,128)(2,1)}, bf16[512,256]{1,0:T(8,128)(2,1)S(1)}, u32[]{:S(2)}, u32[]{:S(2)}) %collective-permute-start) | collective-permute-done | bytes 262176 | tf_op jit(solution)/shard_map/ppermute | solution.py:225
  32.5 2.3 %collective-permute-done.5.refs_6_ = bf16[512,256]{1,0:T(8,128)(2,1)S(1)} collective-permute-done((bf16[512,256]{1,0:T(8,128)(2,1)S(1)}, bf16[512,256]{1,0:T(8,128)(2,1)S(1)}, u32[]{:S(2)}, u32[]{:S(2)}) %collective-permute-start.5) | collective-permute-done | bytes 262176 | tf_op jit(solution)/shard_map/ppermute | solution.py:225
  34.8 7.0 %collective-permute-done.4.refs_5_ = bf16[512,256]{1,0:T(8,128)(2,1)S(1)} collective-permute-done((bf16[512,256]{1,0:T(8,128)(2,1)S(1)}, bf16[512,256]{1,0:T(8,128)(2,1)S(1)}, u32[]{:S(2)}, u32[]{:S(2)}) %collective-permute-start.4) | collective-permute-done | bytes 262176 | tf_op jit(solution)/shard_map/ppermute | solution.py:225
  44.9 1.8 %project.1 = (bf16[512,256]{1,0:T(8,128)(2,1)S(1)}, bf16[1024,256]{1,0:T(8,128)(2,1)S(1)}, bf16[1024,256]{1,0:T(8,128)(2,1)S(1)}) custom-call(s32[7]{0:T(128)S(1)} %pad_add_fusion.info, bf16[512,256]{1,0:T(8,128)(2,1)S(1)} %copy-done.5, bf16[512,256]{1,0:T(8,128)(2,1)S(1)} %collective-permute-done.refs_1_, ...), custom_call_target="tpu_custom_call" | custom-call | tf_op jit(solution)/shard_map/project/pallas_call | solution.py:75
  46.8 2.6 %collective-permute-start.17 = (bf16[1024,256]{1,0:T(8,128)(2,1)S(1)}, bf16[1024,256]{1,0:T(8,128)(2,1)S(1)}, u32[]{:S(2)}, u32[]{:S(2)}) collective-permute-start(bf16[1024,256]{1,0:T(8,128)(2,1)S(1)} %get-tuple-element.39), channel_id=1, source_target_pairs={{0,8},{8,0},{16,24},{24,16},{32,40},{40,32},{48,56},{56,48},{64,72... | collective-permute-start | bytes 1572872 | tf_op jit(solution)/shard_map/ppermute | solution.py:245
  51.9 10.2 %all-to-all-start = ((bf16[8,128,256]{2,1,0:T(8,128)(2,1)}), bf16[8,128,256]{2,1,0:T(8,128)(2,1)S(1)}, u32[]{:S(2)}, u32[]{:S(2)}) async-start(bf16[8,128,256]{2,1,0:T(8,128)(2,1)} %bitcast.3), calls=%async_computation | async-start | bytes 1048576 | tf_op jit(solution)/shard_map/all_to_all | solution.py:250
  62.7 4.2 %collective-permute-start.7 = (bf16[768,256]{1,0:T(8,128)(2,1)S(1)}, bf16[768,256]{1,0:T(8,128)(2,1)S(1)}, u32[]{:S(2)}, u32[]{:S(2)}) collective-permute-start(bf16[768,256]{1,0:T(8,128)(2,1)S(1)} %get-tuple-element.23), channel_id=1, source_target_pairs={{0,8},{8,16},{16,24},{24,32},{32,40},{40,48},{48,56},{56,64},{64,7... | collective-permute-start | bytes 1179656 | tf_op jit(solution)/shard_map/ppermute | solution.py:219
  66.9 3.1 %collective-permute-start.8 = (bf16[256,256]{1,0:T(8,128)(2,1)S(1)}, bf16[256,256]{1,0:T(8,128)(2,1)S(1)}, u32[]{:S(2)}, u32[]{:S(2)}) collective-permute-start(bf16[256,256]{1,0:T(8,128)(2,1)S(1)} %get-tuple-element.24), channel_id=1, source_target_pairs={{0,16},{8,24},{16,32},{24,40},{32,48},{40,56},{48,64},{56,72},{64,... | collective-permute-start | bytes 393224 | tf_op jit(solution)/shard_map/ppermute | solution.py:219
  70.0 5.2 %collective-permute-start.9 = (bf16[256,256]{1,0:T(8,128)(2,1)S(1)}, bf16[256,256]{1,0:T(8,128)(2,1)S(1)}, u32[]{:S(2)}, u32[]{:S(2)}) collective-permute-start(bf16[256,256]{1,0:T(8,128)(2,1)S(1)} %get-tuple-element.25), channel_id=1, source_target_pairs={{0,32},{8,40},{16,48},{24,56},{32,64},{40,72},{48,80},{56,88},{64,... | collective-permute-start | bytes 393224 | tf_op jit(solution)/shard_map/ppermute | solution.py:219
  75.2 1.9 %collective-permute-start.10 = (bf16[256,256]{1,0:T(8,128)(2,1)S(1)}, bf16[256,256]{1,0:T(8,128)(2,1)S(1)}, u32[]{:S(2)}, u32[]{:S(2)}) collective-permute-start(bf16[256,256]{1,0:T(8,128)(2,1)S(1)} %get-tuple-element.26), channel_id=1, source_target_pairs={{0,64},{8,72},{16,80},{24,88},{32,96},{40,104},{48,112},{56,120},{... | collective-permute-start | bytes 393224 | tf_op jit(solution)/shard_map/ppermute | solution.py:219
  77.1 4.8 %collective-permute-start.11 = (bf16[256,256]{1,0:T(8,128)(2,1)S(1)}, bf16[256,256]{1,0:T(8,128)(2,1)S(1)}, u32[]{:S(2)}, u32[]{:S(2)}) collective-permute-start(bf16[256,256]{1,0:T(8,128)(2,1)S(1)} %get-tuple-element.27), channel_id=1, source_target_pairs={{0,128},{8,136},{16,144},{24,152},{32,160},{40,168},{48,176},{56,1... | collective-permute-start | bytes 393224 | tf_op jit(solution)/shard_map/ppermute | solution.py:219
  82.0 1.9 %collective-permute-done.8.f1 = bf16[256,256]{1,0:T(8,128)(2,1)S(1)} collective-permute-done((bf16[256,256]{1,0:T(8,128)(2,1)S(1)}, bf16[256,256]{1,0:T(8,128)(2,1)S(1)}, u32[]{:S(2)}, u32[]{:S(2)}) %collective-permute-start.8) | collective-permute-done | bytes 131104 | tf_op jit(solution)/shard_map/ppermute | solution.py:219
  86.7 6.0 %attend.1 = (bf16[512,256]{1,0:T(8,128)(2,1)}, f32[512,256]{1,0:T(8,128)S(1)}, f32[512,256]{1,0:T(8,128)S(1)}, bf16[768,256]{1,0:T(8,128)(2,1)S(1)}, bf16[256,25...) custom-call(s32[7]{0:T(128)S(1)} %pad_add_fusion.info, ...), custom_call_target="tpu_custom_call" | custom-call | tf_op jit(solution)/shard_map/attend/pallas_call | solution.py:176
  92.8 1.9 %collective-permute-start.12 = (bf16[768,256]{1,0:T(8,128)(2,1)S(1)}, bf16[768,256]{1,0:T(8,128)(2,1)S(1)}, u32[]{:S(2)}, u32[]{:S(2)}) collective-permute-start(bf16[768,256]{1,0:T(8,128)(2,1)S(1)} %get-tuple-element.31), channel_id=1, source_target_pairs={{8,0},{16,8},{24,16},{32,24},{40,32},{48,40},{56,48},{64,56},{72,6... | collective-permute-start | bytes 1179656 | tf_op jit(solution)/shard_map/ppermute | solution.py:219
  100.6 22.5 %all-to-all-start.1 = ((bf16[4,32,256]{2,1,0:T(8,128)(2,1)}), bf16[4,32,256]{2,1,0:T(8,128)(2,1)S(1)}, u32[]{:S(2)}, u32[]{:S(2)}) async-start(bf16[4,32,256]{2,1,0:T(8,128)(2,1)} %bitcast.4), calls=%async_computation.1 | async-start | bytes 131072 | tf_op jit(solution)/shard_map/all_to_all | solution.py:253
  123.1 1.6 %finish.1 = (bf16[512,256]{1,0:T(8,128)(2,1)}, bf16[512,256]{1,0:T(8,128)(2,1)}) custom-call(s32[7]{0:T(128)S(1)} %pad_add_fusion.info, f32[512,256]{1,0:T(8,128)S(1)} %get-tuple-element.29.own_k, f32[512,256]{1,0:T(8,128)S(1)} %get-tuple-element.30.own_v, bf16[768,256]{1,0:T(8,128)(2,1)S(1)} %collective-permute-done.12.near_ref, ...), custom_call_target="tpu_custom_call" | custom-call | tf_op jit(solution)/shard_map/finish/pallas_call | solution.py:207
  124.7 7.2 %all-to-all-done.1 = bf16[4,32,256]{2,1,0:T(8,128)(2,1)S(1)} async-done(((bf16[4,32,256]{2,1,0:T(8,128)(2,1)}), bf16[4,32,256]{2,1,0:T(8,128)(2,1)S(1)}, u32[]{:S(2)}, u32[]{:S(2)}) %all-to-all-start.1) | async-done | bytes 65568 | tf_op jit(solution)/shard_map/all_to_all | solution.py:253
  (41 shorter events, 16.5 us)
Async XLA Ops:
  0.6 17.7 %collective-permute-start.3 = (bf16[512,256]{1,0:T(8,128)(2,1)}, bf16[512,256]{1,0:T(8,128)(2,1)S(1)}, u32[]{:S(2)}, u32[]{:S(2)}) collective-permute-start(bf16[512,256]{1,0:T(8,128)(2,1)} %refs_0_.1), channel_id=1, source_target_pairs={{0,4},{1,5},{2,6},{3,7},{4,0},{5,1},{6,2},{7,3},{8,12},{9,13},{10,... | collective-permute-start | bytes 786440 | tf_op jit(solution)/shard_map/ppermute | solution.py:239
  8.9 16.5 %collective-permute-start.2 = (bf16[512,256]{1,0:T(8,128)(2,1)}, bf16[512,256]{1,0:T(8,128)(2,1)S(1)}, u32[]{:S(2)}, u32[]{:S(2)}) collective-permute-start(bf16[512,256]{1,0:T(8,128)(2,1)} %refs_0_.1), channel_id=1, source_target_pairs={{0,3},{1,0},{2,1},{3,2},{4,7},{5,4},{6,5},{7,6},{8,11},{9,8},{10,9... | collective-permute-start | bytes 786440 | tf_op jit(solution)/shard_map/ppermute | solution.py:225
  13.3 14.8 %collective-permute-start.1 = (bf16[512,256]{1,0:T(8,128)(2,1)}, bf16[512,256]{1,0:T(8,128)(2,1)S(1)}, u32[]{:S(2)}, u32[]{:S(2)}) collective-permute-start(bf16[512,256]{1,0:T(8,128)(2,1)} %refs_0_.1), channel_id=1, source_target_pairs={{0,2},{1,3},{2,0},{3,1},{4,6},{5,7},{6,4},{7,5},{8,10},{9,11},{10,... | collective-permute-start | bytes 786440 | tf_op jit(solution)/shard_map/ppermute | solution.py:225
  15.8 16.6 %collective-permute-start = (bf16[512,256]{1,0:T(8,128)(2,1)}, bf16[512,256]{1,0:T(8,128)(2,1)S(1)}, u32[]{:S(2)}, u32[]{:S(2)}) collective-permute-start(bf16[512,256]{1,0:T(8,128)(2,1)} %refs_0_.1), channel_id=1, source_target_pairs={{0,1},{1,2},{2,3},{3,0},{4,5},{5,6},{6,7},{7,4},{8,9},{9,10},{10,1... | collective-permute-start | bytes 786440 | tf_op jit(solution)/shard_map/ppermute | solution.py:225
  18.3 14.2 %collective-permute-start.6 = (bf16[512,256]{1,0:T(8,128)(2,1)S(1)}, bf16[512,256]{1,0:T(8,128)(2,1)S(1)}, u32[]{:S(2)}, u32[]{:S(2)}) collective-permute-start(bf16[512,256]{1,0:T(8,128)(2,1)S(1)} %collective-permute-done.3.refs_4_), channel_id=1, source_target_pairs={{0,3},{1,0},{2,1},{3,2},{4,7},{5,4},{6,5},{7,6},{8,11},{9,8},{10,9... | collective-permute-start | bytes 786440 | tf_op jit(solution)/shard_map/ppermute | solution.py:225
  22.3 12.5 %collective-permute-start.5 = (bf16[512,256]{1,0:T(8,128)(2,1)S(1)}, bf16[512,256]{1,0:T(8,128)(2,1)S(1)}, u32[]{:S(2)}, u32[]{:S(2)}) collective-permute-start(bf16[512,256]{1,0:T(8,128)(2,1)S(1)} %collective-permute-done.3.refs_4_), channel_id=1, source_target_pairs={{0,2},{1,3},{2,0},{3,1},{4,6},{5,7},{6,4},{7,5},{8,10},{9,11},{10,... | collective-permute-start | bytes 786440 | tf_op jit(solution)/shard_map/ppermute | solution.py:225
  25.4 16.4 %collective-permute-start.4 = (bf16[512,256]{1,0:T(8,128)(2,1)S(1)}, bf16[512,256]{1,0:T(8,128)(2,1)S(1)}, u32[]{:S(2)}, u32[]{:S(2)}) collective-permute-start(bf16[512,256]{1,0:T(8,128)(2,1)S(1)} %collective-permute-done.3.refs_4_), channel_id=1, source_target_pairs={{0,1},{1,2},{2,3},{3,0},{4,5},{5,6},{6,7},{7,4},{8,9},{9,10},{10,1... | collective-permute-start | bytes 786440 | tf_op jit(solution)/shard_map/ppermute | solution.py:225
  46.8 4.1 %collective-permute-start.17 = (bf16[1024,256]{1,0:T(8,128)(2,1)S(1)}, bf16[1024,256]{1,0:T(8,128)(2,1)S(1)}, u32[]{:S(2)}, u32[]{:S(2)}) collective-permute-start(bf16[1024,256]{1,0:T(8,128)(2,1)S(1)} %get-tuple-element.39), channel_id=1, source_target_pairs={{0,8},{8,0},{16,24},{24,16},{32,40},{40,32},{48,56},{56,48},{64,72... | collective-permute-start | bytes 1572872 | tf_op jit(solution)/shard_map/ppermute | solution.py:245
  51.9 10.2 %copy-start.2 = (bf16[512,256]{1,0:T(8,128)(2,1)S(1)}, bf16[512,256]{1,0:T(8,128)(2,1)}, u32[]{:S(2)}) copy-start(bf16[512,256]{1,0:T(8,128)(2,1)} %k_ref.3) | copy-start | bytes 786436
  51.9 10.2 %copy-start.3 = (bf16[512,256]{1,0:T(8,128)(2,1)S(1)}, bf16[512,256]{1,0:T(8,128)(2,1)}, u32[]{:S(2)}) copy-start(bf16[512,256]{1,0:T(8,128)(2,1)} %v_ref.3) | copy-start | bytes 786436
  51.9 48.0 %all-to-all-start = ((bf16[8,128,256]{2,1,0:T(8,128)(2,1)}), bf16[8,128,256]{2,1,0:T(8,128)(2,1)S(1)}, u32[]{:S(2)}, u32[]{:S(2)}) async-start(bf16[8,128,256]{2,1,0:T(8,128)(2,1)} %bitcast.3), calls=%async_computation | async-start | bytes 1048576 | tf_op jit(solution)/shard_map/all_to_all | solution.py:250
  62.1 24.7 %copy-start.1 = (bf16[512,256]{1,0:T(8,128)(2,1)S(1)}, bf16[512,256]{1,0:T(8,128)(2,1)}, u32[]{:S(2)}) copy-start(bf16[512,256]{1,0:T(8,128)(2,1)} %o_ref.1) | copy-start | bytes 786436
  62.1 24.6 %copy-start.6 = (bf16[512,256]{1,0:T(8,128)(2,1)S(1)}, bf16[512,256]{1,0:T(8,128)(2,1)}, u32[]{:S(2)}) copy-start(bf16[512,256]{1,0:T(8,128)(2,1)} %q_ref.1) | copy-start | bytes 786436
  62.7 24.0 %collective-permute-start.7 = (bf16[768,256]{1,0:T(8,128)(2,1)S(1)}, bf16[768,256]{1,0:T(8,128)(2,1)S(1)}, u32[]{:S(2)}, u32[]{:S(2)}) collective-permute-start(bf16[768,256]{1,0:T(8,128)(2,1)S(1)} %get-tuple-element.23), channel_id=1, source_target_pairs={{0,8},{8,16},{16,24},{24,32},{32,40},{40,48},{48,56},{56,64},{64,7... | collective-permute-start | bytes 1179656 | tf_op jit(solution)/shard_map/ppermute | solution.py:219
  66.9 17.0 %collective-permute-start.8 = (bf16[256,256]{1,0:T(8,128)(2,1)S(1)}, bf16[256,256]{1,0:T(8,128)(2,1)S(1)}, u32[]{:S(2)}, u32[]{:S(2)}) collective-permute-start(bf16[256,256]{1,0:T(8,128)(2,1)S(1)} %get-tuple-element.24), channel_id=1, source_target_pairs={{0,16},{8,24},{16,32},{24,40},{32,48},{40,56},{48,64},{56,72},{64,... | collective-permute-start | bytes 393224 | tf_op jit(solution)/shard_map/ppermute | solution.py:219
  70.0 15.3 %collective-permute-start.9 = (bf16[256,256]{1,0:T(8,128)(2,1)S(1)}, bf16[256,256]{1,0:T(8,128)(2,1)S(1)}, u32[]{:S(2)}, u32[]{:S(2)}) collective-permute-start(bf16[256,256]{1,0:T(8,128)(2,1)S(1)} %get-tuple-element.25), channel_id=1, source_target_pairs={{0,32},{8,40},{16,48},{24,56},{32,64},{40,72},{48,80},{56,88},{64,... | collective-permute-start | bytes 393224 | tf_op jit(solution)/shard_map/ppermute | solution.py:219
  75.2 11.5 %collective-permute-start.10 = (bf16[256,256]{1,0:T(8,128)(2,1)S(1)}, bf16[256,256]{1,0:T(8,128)(2,1)S(1)}, u32[]{:S(2)}, u32[]{:S(2)}) collective-permute-start(bf16[256,256]{1,0:T(8,128)(2,1)S(1)} %get-tuple-element.26), channel_id=1, source_target_pairs={{0,64},{8,72},{16,80},{24,88},{32,96},{40,104},{48,112},{56,120},{... | collective-permute-start | bytes 393224 | tf_op jit(solution)/shard_map/ppermute | solution.py:219
  77.1 9.6 %collective-permute-start.11 = (bf16[256,256]{1,0:T(8,128)(2,1)S(1)}, bf16[256,256]{1,0:T(8,128)(2,1)S(1)}, u32[]{:S(2)}, u32[]{:S(2)}) collective-permute-start(bf16[256,256]{1,0:T(8,128)(2,1)S(1)} %get-tuple-element.27), channel_id=1, source_target_pairs={{0,128},{8,136},{16,144},{24,152},{32,160},{40,168},{48,176},{56,1... | collective-permute-start | bytes 393224 | tf_op jit(solution)/shard_map/ppermute | solution.py:219
  92.8 30.3 %collective-permute-start.12 = (bf16[768,256]{1,0:T(8,128)(2,1)S(1)}, bf16[768,256]{1,0:T(8,128)(2,1)S(1)}, u32[]{:S(2)}, u32[]{:S(2)}) collective-permute-start(bf16[768,256]{1,0:T(8,128)(2,1)S(1)} %get-tuple-element.31), channel_id=1, source_target_pairs={{8,0},{16,8},{24,16},{32,24},{40,32},{48,40},{56,48},{64,56},{72,6... | collective-permute-start | bytes 1179656 | tf_op jit(solution)/shard_map/ppermute | solution.py:219
  94.7 28.4 %collective-permute-start.13 = (bf16[256,256]{1,0:T(8,128)(2,1)S(1)}, bf16[256,256]{1,0:T(8,128)(2,1)S(1)}, u32[]{:S(2)}, u32[]{:S(2)}) collective-permute-start(bf16[256,256]{1,0:T(8,128)(2,1)S(1)} %get-tuple-element.32), channel_id=1, source_target_pairs={{16,0},{24,8},{32,16},{40,24},{48,32},{56,40},{64,48},{72,56},{80,... | collective-permute-start | bytes 393224 | tf_op jit(solution)/shard_map/ppermute | solution.py:219
  96.0 27.1 %collective-permute-start.14 = (bf16[256,256]{1,0:T(8,128)(2,1)S(1)}, bf16[256,256]{1,0:T(8,128)(2,1)S(1)}, u32[]{:S(2)}, u32[]{:S(2)}) collective-permute-start(bf16[256,256]{1,0:T(8,128)(2,1)S(1)} %get-tuple-element.33), channel_id=1, source_target_pairs={{32,0},{40,8},{48,16},{56,24},{64,32},{72,40},{80,48},{88,56},{96,... | collective-permute-start | bytes 393224 | tf_op jit(solution)/shard_map/ppermute | solution.py:219
  97.3 25.8 %collective-permute-start.15 = (bf16[256,256]{1,0:T(8,128)(2,1)S(1)}, bf16[256,256]{1,0:T(8,128)(2,1)S(1)}, u32[]{:S(2)}, u32[]{:S(2)}) collective-permute-start(bf16[256,256]{1,0:T(8,128)(2,1)S(1)} %get-tuple-element.34), channel_id=1, source_target_pairs={{64,0},{72,8},{80,16},{88,24},{96,32},{104,40},{112,48},{120,56},{... | collective-permute-start | bytes 393224 | tf_op jit(solution)/shard_map/ppermute | solution.py:219
  98.6 24.5 %collective-permute-start.16 = (bf16[256,256]{1,0:T(8,128)(2,1)S(1)}, bf16[256,256]{1,0:T(8,128)(2,1)S(1)}, u32[]{:S(2)}, u32[]{:S(2)}) collective-permute-start(bf16[256,256]{1,0:T(8,128)(2,1)S(1)} %get-tuple-element.35), channel_id=1, source_target_pairs={{128,0},{136,8},{144,16},{152,24},{160,32},{168,40},{176,48},{184,... | collective-permute-start | bytes 393224 | tf_op jit(solution)/shard_map/ppermute | solution.py:219
  100.6 31.3 %all-to-all-start.1 = ((bf16[4,32,256]{2,1,0:T(8,128)(2,1)}), bf16[4,32,256]{2,1,0:T(8,128)(2,1)S(1)}, u32[]{:S(2)}, u32[]{:S(2)}) async-start(bf16[4,32,256]{2,1,0:T(8,128)(2,1)} %bitcast.4), calls=%async_computation.1 | async-start | bytes 131072 | tf_op jit(solution)/shard_map/all_to_all | solution.py:253
  (4 other events, 3.8 us)

commit v2 on v1

v2 whole, which is shorter than its diff:
```python
import functools

import functools

import jax
import jax.numpy as jnp
from jax import lax
from jax.experimental import pallas as pl
from jax.experimental.pallas import tpu as pltpu
from jax.sharding import PartitionSpec as P

HD = 128
WIN = 256
BLK = 128
LEVELS = 5
BF = jnp.bfloat16
F32 = jnp.float32
NX, NZ, NYL = 4, 8, 4
VMEM = pl.BlockSpec(memory_space=pltpu.VMEM)
ANY = pl.BlockSpec(memory_space=pl.ANY)
PROJECT_MIB = 60
AFTER = slice(0, 3)
SMEM = pl.BlockSpec(memory_space=pltpu.SMEM)


def params(mib=16):
    return pltpu.CompilerParams(vmem_limit_bytes=mib * 1024 * 1024)


def dot(a, b, ca, cb):
    return lax.dot_general(a, b, (((ca,), (cb,)), ((), ())), preferred_element_type=F32)


def pack_kernel(pick, k_ref, v_ref, near_ref, *far_refs):
    near_ref[0:WIN, :] = k_ref[512 - WIN :, :]
    near_ref[WIN : 2 * WIN, :] = v_ref[512 - WIN :, :]
    for level in range(LEVELS):
        first = pl.multiple_of(pick[0, level] * BLK, BLK)
        ref, at = (near_ref, 2 * WIN) if level == 0 else (far_refs[level - 1], 0)
        ref[at : at + BLK, :] = k_ref[pl.ds(first, BLK), :]
        ref[at + BLK : at + 2 * BLK, :] = v_ref[pl.ds(first, BLK), :]


def pack(pick, keys, values):
    return pl.pallas_call(
        pack_kernel,
        out_shape=[jax.ShapeDtypeStruct((2 * WIN + 2 * BLK, 256), BF)]
        + [jax.ShapeDtypeStruct((2 * BLK, 256), BF)] * (LEVELS - 1),
        in_specs=[SMEM, VMEM, VMEM],
        out_specs=[VMEM] * LEVELS,
        compiler_params=params(),
        name="pack",
    )(pick, keys, values)


def spread_kernel(n, b_ref, *refs):
    block = b_ref[...]
    for i in range(NX):
        refs[n][i] = block


def spread(block, *after):
    n = len(after)
    return pl.pallas_call(
        functools.partial(spread_kernel, n),
        out_shape=jax.ShapeDtypeStruct((NX, 512, 256), BF),
        in_specs=[VMEM] + [ANY] * n,
        out_specs=VMEM,
        compiler_params=params(),
        name="spread",
    )(block, *after)


def k_rows(near_ref, fars, lanes):
    return jnp.concatenate(
        [near_ref[2 * WIN : 2 * WIN + BLK, lanes]] + [r[0:BLK, lanes] for r in fars], axis=0
    )


def v_rows(near_ref, fars, lanes):
    return jnp.concatenate(
        [near_ref[2 * WIN + BLK :, lanes]] + [r[BLK:, lanes] for r in fars], axis=0
    )


def earlier_tile():
    row = lax.broadcasted_iota(jnp.int32, (256, 256), 0)
    col = lax.broadcasted_iota(jnp.int32, (256, 256), 1)
    return row > col


def weigh_kernel(
    q_ref, k_ref, near_ref, f1, f2, f3, f4, p_ref,
):
    scale = HD ** (-0.5)
    shard = lax.axis_index("tm")
    neg = jnp.float32(-1e30)
    earlier = earlier_tile()
    level_of = lax.broadcasted_iota(jnp.int32, (LEVELS * BLK, 256), 0) // BLK
    far_ok = shard >= (1 << level_of)
    for head in range(2):
        lanes = slice(head * HD, (head + 1) * HD)
        k_far = k_rows(near_ref, (f1, f2, f3, f4), lanes)
        for blk in range(2):
            rows = slice(blk * 256, (blk + 1) * 256)
            q = q_ref[rows, lanes]
            k_here = k_ref[rows, lanes]
            k_prev = near_ref[0:WIN, lanes] if blk == 0 else k_ref[0:256, lanes]
            s_prev = dot(k_prev, q, 1, 1) * scale
            s_here = dot(k_here, q, 1, 1) * scale
            s_far = dot(k_far, q, 1, 1) * scale
            if blk == 0:
                s_prev = jnp.where(shard > 0, s_prev, neg)
            s_near = jnp.where(earlier, s_prev, s_here)
            s_far = jnp.where(far_ok, s_far, neg)
            top = jnp.maximum(
                jnp.max(s_near, axis=0, keepdims=True), jnp.max(s_far, axis=0, keepdims=True)
            )
            e_near, e_far = jnp.exp(s_near - top), jnp.exp(s_far - top)
            inv = 1.0 / (
                jnp.sum(e_near, axis=0, keepdims=True) + jnp.sum(e_far, axis=0, keepdims=True)
            )
            p_ref[2 * head + blk, 0:256, :] = (e_near * inv).astype(BF)
            p_ref[2 * head + blk, 256:, :] = (e_far * inv).astype(BF)


def weigh(queries, keys, got):
    return pl.pallas_call(
        weigh_kernel,
        out_shape=jax.ShapeDtypeStruct((4, 256 + LEVELS * BLK, 256), BF),
        in_specs=[VMEM] * 7,
        out_specs=VMEM,
        compiler_params=params(),
        name="weigh",
    )(queries, keys, *got)


def project_kernel(
    mine_hbm, theirs_hbm, w_hbm, o_hbm, probs, dout_ref, keep_ref, send_ref,
    w_ref, cot_ref, o_ref, w_sems, cot_sems, o_sem,
):
    core, head = lax.axis_index("tm") % 2, lax.axis_index("head")
    yh = head // NX
    load_o = pltpu.make_async_copy(o_hbm, o_ref, o_sem)
    load_o.start()
    loads = []
    for at in range(2 * NX):
        src = (yh if at < NX else 1 - yh) * NX + at % NX
        rows = pl.ds(pl.multiple_of(src * 256, 256), 256)
        cots = mine_hbm if at < NX else theirs_hbm
        pair = (
            pltpu.make_async_copy(cots.at[at % NX], cot_ref.at[at], cot_sems.at[at]),
            pltpu.make_async_copy(w_hbm.at[rows, :], w_ref.at[at], w_sems.at[at]),
        )
        for load in pair:
            load.start()
        loads.append(pair)
    load_o.wait()
    acc = jnp.zeros((512, 256), F32)
    for at in range(2 * NX):
        src = (yh if at < NX else 1 - yh) * NX + at % NX
        loads[at][0].wait()
        cot = cot_ref[at]
        term = dot(cot, o_ref[...], 0, 0).astype(BF)
        for sub in range(4):
            rows = pl.ds(pl.multiple_of(src * 128 + sub * 32, 32), 32)
            low = term[sub * 64 : sub * 64 + 32, :]
            high = term[sub * 64 + 32 : sub * 64 + 64, :]
            keep_ref[rows, :] = jnp.where(core == 0, low, high)
            send_ref[rows, :] = jnp.where(core == 0, high, low)
        loads[at][1].wait()
        acc = acc + dot(cot, w_ref[at], 1, 0)
    dout_ref[...] = acc.astype(BF)


def project(mine, theirs, out_weight, outputs, probs):
    half = jax.ShapeDtypeStruct((1024, 256), BF)
    return pl.pallas_call(
        project_kernel,
        out_shape=[jax.ShapeDtypeStruct((512, 256), BF), half, half],
        in_specs=[ANY] * 5,
        out_specs=[VMEM] * 3,
        scratch_shapes=[
            pltpu.VMEM((2 * NX, 256, 256), BF),
            pltpu.VMEM((2 * NX, 512, 256), BF),
            pltpu.VMEM((512, 256), BF),
            pltpu.SemaphoreType.DMA((2 * NX,)),
            pltpu.SemaphoreType.DMA((2 * NX,)),
            pltpu.SemaphoreType.DMA,
        ],
        compiler_params=params(PROJECT_MIB),
        name="project",
    )(mine, theirs, out_weight, outputs, probs)


def attend_kernel(
    p_ref, q_ref, k_ref, v_ref, o_ref, do_ref, near_ref, f1, f2, f3, f4,
    dq_ref, own_k, own_v, back_near, b1, b2, b3, b4, fk, fv,
):
    scale = HD ** (-0.5)
    earlier = earlier_tile()
    zero = jnp.zeros((), F32)
    for head in range(2):
        lanes = slice(head * HD, (head + 1) * HD)
        k_far = k_rows(near_ref, (f1, f2, f3, f4), lanes)
        v_far = v_rows(near_ref, (f1, f2, f3, f4), lanes)
        for blk in range(2):
            rows = slice(blk * 256, (blk + 1) * 256)
            q = q_ref[rows, lanes]
            do = do_ref[rows, lanes]
            k_here, v_here = k_ref[rows, lanes], v_ref[rows, lanes]
            if blk == 0:
                k_prev, v_prev = near_ref[0:WIN, lanes], near_ref[WIN : 2 * WIN, lanes]
            else:
                k_prev, v_prev = k_ref[0:256, lanes], v_ref[0:256, lanes]
            delta = jnp.sum(
                do.astype(F32) * o_ref[rows, lanes].astype(F32), axis=1, keepdims=True
            )
            delta = jnp.transpose(jnp.broadcast_to(delta, (256, 128)))[0:1, :]
            p_near = p_ref[2 * head + blk, 0:256, :].astype(F32)
            p_far = p_ref[2 * head + blk, 256:, :]
            dp_near = jnp.where(earlier, dot(v_prev, do, 1, 1), dot(v_here, do, 1, 1))
            dp_far = dot(v_far, do, 1, 1)
            ds_near = p_near * (dp_near - delta)
            ds_far = (p_far.astype(F32) * (dp_far - delta)).astype(BF)
            ds_prev = jnp.where(earlier, ds_near, zero).astype(BF)
            ds_here = jnp.where(earlier, zero, ds_near).astype(BF)
            p_prev = jnp.where(earlier, p_near, zero).astype(BF)
            p_here = jnp.where(earlier, zero, p_near).astype(BF)
            dq = dot(ds_prev, k_prev, 0, 0) + dot(ds_here, k_here, 0, 0) + dot(ds_far, k_far, 0, 0)
            dq_ref[rows, lanes] = (dq * scale).astype(BF)
            dk_prev, dv_prev = dot(ds_prev, q, 1, 0) * scale, dot(p_prev, do, 1, 0)
            dk_here, dv_here = dot(ds_here, q, 1, 0) * scale, dot(p_here, do, 1, 0)
            dk_far, dv_far = dot(ds_far, q, 1, 0) * scale, dot(p_far, do, 1, 0)
            if blk == 0:
                back_near[0:WIN, lanes] = dk_prev.astype(BF)
                back_near[WIN : 2 * WIN, lanes] = dv_prev.astype(BF)
                own_k[0:256, lanes] = dk_here
                own_v[0:256, lanes] = dv_here
                fk[...] = dk_far
                fv[...] = dv_far
            else:
                own_k[0:256, lanes] += dk_prev
                own_v[0:256, lanes] += dv_prev
                own_k[256:512, lanes] = dk_here
                own_v[256:512, lanes] = dv_here
                for i, r in enumerate((back_near, b1, b2, b3, b4)):
                    at = 2 * WIN if i == 0 else 0
                    part = slice(i * BLK, (i + 1) * BLK)
                    r[at : at + BLK, lanes] = (fk[part, :] + dk_far[part]).astype(BF)
                    r[at + BLK : at + 2 * BLK, lanes] = (fv[part, :] + dv_far[part]).astype(BF)


def attend(probs, queries, keys, values, outputs, d_out, got):
    f32s = jax.ShapeDtypeStruct((512, 256), F32)
    far = jax.ShapeDtypeStruct((2 * BLK, 256), BF)
    return pl.pallas_call(
        attend_kernel,
        out_shape=[
            jax.ShapeDtypeStruct((512, 256), BF), f32s, f32s,
            jax.ShapeDtypeStruct((2 * WIN + 2 * BLK, 256), BF), far, far, far, far,
        ],
        in_specs=[VMEM] * 11,
        out_specs=[VMEM] * 8,
        scratch_shapes=[pltpu.VMEM((LEVELS * BLK, HD), F32)] * 2,
        compiler_params=params(),
        name="attend",
    )(probs, queries, keys, values, outputs, d_out, *got)


def finish_kernel(pick, own_k, own_v, near_ref, f1, f2, f3, f4, dk_ref, dv_ref, tk, tv):
    for ref, acc, at in ((own_k, tk, 0), (own_v, tv, 1)):
        acc[0:256, :] = ref[0:256, :]
        acc[256:512, :] = ref[256:512, :] + near_ref[at * WIN : (at + 1) * WIN, :].astype(F32)
        for level, far in enumerate((near_ref, f1, f2, f3, f4)):
            low = (2 * WIN if level == 0 else 0) + at * BLK
            rows = pl.ds(pl.multiple_of(pick[0, level] * BLK, BLK), BLK)
            acc[rows, :] += far[low : low + BLK, :].astype(F32)
    dk_ref[...] = tk[...].astype(BF)
    dv_ref[...] = tv[...].astype(BF)


def finish(pick, own_k, own_v, got):
    out = jax.ShapeDtypeStruct((512, 256), BF)
    return pl.pallas_call(
        finish_kernel,
        out_shape=[out, out],
        in_specs=[SMEM] + [VMEM] * 7,
        out_specs=[VMEM] * 2,
        scratch_shapes=[pltpu.VMEM((512, 256), F32)] * 2,
        compiler_params=params(),
        name="finish",
    )(pick, own_k, own_v, *got)


def shift(block, distance):
    return lax.ppermute(
        block, "tm", [(i, i + distance) for i in range(64) if 0 <= i + distance < 64]
    )


def to_row(blocks):
    rows = [[yh * NX + x for x in range(NX)] for yh in range(2)]
    return lax.all_to_all(blocks, "head", 0, 0, axis_index_groups=rows)


def on_device(queries, keys, values, outputs, out_cotangent, out_weight, block_pick):
    mine = to_row(spread(out_cotangent))
    other = lax.ppermute(out_cotangent, "head", [(h, (h + NX) % (2 * NX)) for h in range(2 * NX)])
    packed = pack(block_pick, keys, values)
    got = [shift(b, 2**level) for level, b in enumerate(packed)]
    theirs = to_row(spread(other, *got[AFTER]))
    probs = weigh(queries, keys, got)
    d_out, keep, send = project(mine, theirs, out_weight, outputs, probs)
    received = lax.ppermute(send, "tm", [(i, i ^ 1) for i in range(64)])
    dq, own_k, own_v, *back = attend(probs, queries, keys, values, outputs, d_out, got)
    back = [shift(b, -(2**level)) for level, b in enumerate(back)]
    half = (keep.astype(F32) + received.astype(F32)).astype(BF).reshape(NYL * NZ, 32, 256)
    groups = [[2 * i + c for i in range(NYL * NZ)] for c in range(2)]
    part = lax.all_to_all(half, "tm", 0, 0, axis_index_groups=groups)
    weight_grad = jnp.sum(part.astype(F32), axis=0) * (512 * 64) ** (-0.5)
    dk, dv = finish(block_pick, own_k, own_v, back)
    return dq, dk, dv, weight_grad


def solution(mesh):
    placed = (P("tm", "head"),) * 5 + (P(None, "head"), P("tm", None))
    return jax.shard_map(
        on_device,
        mesh=mesh,
        in_specs=placed,
        out_specs=(P("tm", "head"),) * 4,
        check_vma=False,
    )
```

time: 135 us -> 126 us (0.933)
  the two profiles are of different devices: /device:TPU:1 before, /device:TPU:2 now
where the time goes in v2:
time: 126 us; the launch traced here: 125 us
  starting transfers between devices  68 us (54%)
  waiting for transfers between devices  30.7 us (24%)
  Pallas kernels  16.9 us (13%)
  local copies, waits for them, and re-layouts  5.05 us (4%)
  other arithmetic  3.72 us (3%)
    ppermute x10, starting transfers between devices, shift(): lax.ppermute(block, 'tm', [(i, i + distance) for i in range(64) if 0 <= i...  36.1 us
    ppermute x10, waiting for transfers between devices, shift(): lax.ppermute(block, 'tm', [(i, i + distance) for i in range(64) if 0 <= i...  27.5 us
    all_to_all x2, starting transfers between devices, to_row(): return lax.all_to_all(blocks, 'head', 0, 0, axis_index_groups=rows)  14.2 us
    all_to_all x1, starting transfers between devices, on_device(): part = lax.all_to_all(half, 'tm', 0, 0, axis_index_groups=groups)  12.5 us
    pallas_call x1, Pallas kernels, project(): pl.pallas_call(project_kernel, out_shape=[jax.ShapeDtypeStruct((512, 256)...  6.59 us
    unnamed x30, local copies, waits for them, and re-layouts  5.05 us
    pallas_call x1, Pallas kernels, attend(): pl.pallas_call(attend_kernel, out_shape=[jax.ShapeDtypeStruct((512, 256),...  4.23 us
    ppermute x1, starting transfers between devices, on_device(): lax.ppermute(out_cotangent, 'head', [(h, (h + NX) % (2 * NX)) for h in ra...  3.17 us
  transfers between devices with their start and end apart: 15, of which 7 were waited for; matrix products, arithmetic and copies ran while one was open for 0% of the time, Pallas kernels for 7%

profile of v2, /device:TPU:2, one launch (start us, length us, event | category | flops | bytes accessed | tf_op | source)
XLA Modules:
  0.0 125.3 jit_solution(15671761409867591433)
XLA Ops:
  2.7 9.4 %all-to-all-start = ((bf16[4,512,256]{2,1,0:T(8,128)(2,1)}), bf16[4,512,256]{2,1,0:T(8,128)(2,1)S(1)}, u32[]{:S(2)}, u32[]{:S(2)}) async-start(bf16[4,512,256]{2,1,0:T(8,128)(2,1)} %spread.2), calls=%async_computation | async-start | bytes 2097152 | tf_op jit(solution)/shard_map/all_to_all | solution.py:304
  12.7 1.3 %collective-permute-start = (bf16[768,256]{1,0:T(8,128)(2,1)S(1)}, bf16[768,256]{1,0:T(8,128)(2,1)S(1)}, u32[]{:S(2)}, u32[]{:S(2)}) collective-permute-start(bf16[768,256]{1,0:T(8,128)(2,1)S(1)} %get-tuple-element.22), channel_id=1, source_target_pairs={{0,8},{8,16},{16,24},{24,32},{32,40},{40,48},{48,56},{56,64},{64,7... | collective-permute-start | bytes 1179656 | tf_op jit(solution)/shard_map/ppermute | solution.py:297
  14.1 3.2 %collective-permute-start.5 = (bf16[512,256]{1,0:T(8,128)(2,1)S(1)}, bf16[512,256]{1,0:T(8,128)(2,1)S(1)}, u32[]{:S(2)}, u32[]{:S(2)}) collective-permute-start(bf16[512,256]{1,0:T(8,128)(2,1)S(1)} %copy-done.11), channel_id=1, source_target_pairs={{0,4},{1,5},{2,6},{3,7},{4,0},{5,1},{6,2},{7,3},{8,12},{9,13},{10,... | collective-permute-start | bytes 786440 | tf_op jit(solution)/shard_map/ppermute | solution.py:309
  17.2 4.9 %collective-permute-start.1 = (bf16[256,256]{1,0:T(8,128)(2,1)S(1)}, bf16[256,256]{1,0:T(8,128)(2,1)S(1)}, u32[]{:S(2)}, u32[]{:S(2)}) collective-permute-start(bf16[256,256]{1,0:T(8,128)(2,1)S(1)} %get-tuple-element.23), channel_id=1, source_target_pairs={{0,16},{8,24},{16,32},{24,40},{32,48},{40,56},{48,64},{56,72},{64,... | collective-permute-start | bytes 393224 | tf_op jit(solution)/shard_map/ppermute | solution.py:297
  22.1 6.2 %collective-permute-start.2 = (bf16[256,256]{1,0:T(8,128)(2,1)S(1)}, bf16[256,256]{1,0:T(8,128)(2,1)S(1)}, u32[]{:S(2)}, u32[]{:S(2)}) collective-permute-start(bf16[256,256]{1,0:T(8,128)(2,1)S(1)} %get-tuple-element.24), channel_id=1, source_target_pairs={{0,32},{8,40},{16,48},{24,56},{32,64},{40,72},{48,80},{56,88},{64,... | collective-permute-start | bytes 393224 | tf_op jit(solution)/shard_map/ppermute | solution.py:297
  28.4 2.5 %collective-permute-done.2.f2.refs_2_ = bf16[256,256]{1,0:T(8,128)(2,1)S(1)} collective-permute-done((bf16[256,256]{1,0:T(8,128)(2,1)S(1)}, bf16[256,256]{1,0:T(8,128)(2,1)S(1)}, u32[]{:S(2)}, u32[]{:S(2)}) %collective-permute-start.2) | collective-permute-done | bytes 131104 | tf_op jit(solution)/shard_map/ppermute | solution.py:297
  33.0 4.8 %all-to-all-start.1 = ((bf16[4,512,256]{2,1,0:T(8,128)(2,1)}), bf16[4,512,256]{2,1,0:T(8,128)(2,1)}, u32[]{:S(2)}, u32[]{:S(2)}) async-start(bf16[4,512,256]{2,1,0:T(8,128)(2,1)} %spread.3), calls=%async_computation.1 | async-start | bytes 2097152 | tf_op jit(solution)/shard_map/all_to_all | solution.py:304
  37.8 13.5 %collective-permute-start.3 = (bf16[256,256]{1,0:T(8,128)(2,1)S(1)}, bf16[256,256]{1,0:T(8,128)(2,1)S(1)}, u32[]{:S(2)}, u32[]{:S(2)}) collective-permute-start(bf16[256,256]{1,0:T(8,128)(2,1)S(1)} %get-tuple-element.25), channel_id=1, source_target_pairs={{0,64},{8,72},{16,80},{24,88},{32,96},{40,104},{48,112},{56,120},{... | collective-permute-start | bytes 393224 | tf_op jit(solution)/shard_map/ppermute | solution.py:297
  51.3 3.7 %collective-permute-start.4 = (bf16[256,256]{1,0:T(8,128)(2,1)S(1)}, bf16[256,256]{1,0:T(8,128)(2,1)S(1)}, u32[]{:S(2)}, u32[]{:S(2)}) collective-permute-start(bf16[256,256]{1,0:T(8,128)(2,1)S(1)} %get-tuple-element.26), channel_id=1, source_target_pairs={{0,128},{8,136},{16,144},{24,152},{32,160},{40,168},{48,176},{56,1... | collective-permute-start | bytes 393224 | tf_op jit(solution)/shard_map/ppermute | solution.py:297
  55.1 3.1 %collective-permute-done.4.f4 = bf16[256,256]{1,0:T(8,128)(2,1)S(1)} collective-permute-done((bf16[256,256]{1,0:T(8,128)(2,1)S(1)}, bf16[256,256]{1,0:T(8,128)(2,1)S(1)}, u32[]{:S(2)}, u32[]{:S(2)}) %collective-permute-start.4) | collective-permute-done | bytes 131104 | tf_op jit(solution)/shard_map/ppermute | solution.py:297
  58.2 1.8 %weigh.1.probs.p_ref = bf16[4,896,256]{2,1,0:T(8,128)(2,1)S(1)} custom-call(bf16[512,256]{1,0:T(8,128)(2,1)S(1)} %copy-done.3, bf16[512,256]{1,0:T(8,128)(2,1)S(1)} %copy-done.2, bf16[768,256]{1,0:T(8,128)(2,1)S(1)} %collective-permute-done.near_ref.refs_0_, bf16[256,256]{1,0:T(8,128)(2,1)S(1)} %collective-permute-done.1.f1.refs_1_, ...), custom_call_target="tpu_custom_call" | custom-call | tf_op jit(solution)/shard_map/weigh/pallas_call | solution.py:128
  61.3 6.6 %project.1 = (bf16[512,256]{1,0:T(8,128)(2,1)}, bf16[1024,256]{1,0:T(8,128)(2,1)}, bf16[1024,256]{1,0:T(8,128)(2,1)}) custom-call(bf16[4,512,256]{2,1,0:T(8,128)(2,1)} %copy-done.14, bf16[4,512,256]{2,1,0:T(8,128)(2,1)} %all-to-all-done.1.theirs_hbm, bf16[2048,256]{1,0:T(8,128)(2,1)} %w_hbm.1, bf16[512,256]{1,0:T(8,128)(2,1)} %o_ref.1, ...), custom_call_target="tpu_custom_call" | custom-call | tf_op jit(solution)/shard_map/project/pallas_call | solution.py:178
  68.0 2.1 %collective-permute-start.11 = (bf16[1024,256]{1,0:T(8,128)(2,1)}, bf16[1024,256]{1,0:T(8,128)(2,1)S(1)}, u32[]{:S(2)}, u32[]{:S(2)}) collective-permute-start(bf16[1024,256]{1,0:T(8,128)(2,1)} %get-tuple-element.39), channel_id=1, source_target_pairs={{0,8},{8,0},{16,24},{24,16},{32,40},{40,32},{48,56},{56,48},{64,72... | collective-permute-start | bytes 1572872 | tf_op jit(solution)/shard_map/ppermute | solution.py:315
  70.0 2.1 %collective-permute-done.11 = bf16[1024,256]{1,0:T(8,128)(2,1)S(1)} collective-permute-done((bf16[1024,256]{1,0:T(8,128)(2,1)}, bf16[1024,256]{1,0:T(8,128)(2,1)S(1)}, u32[]{:S(2)}, u32[]{:S(2)}) %collective-permute-start.11) | collective-permute-done | bytes 524320 | tf_op jit(solution)/shard_map/ppermute | solution.py:315
  72.1 2.0 %add_convert_fusion = bf16[1024,256]{1,0:T(8,128)(2,1)} fusion(bf16[1024,256]{1,0:T(8,128)(2,1)S(1)} %collective-permute-done.11, bf16[1024,256]{1,0:T(8,128)(2,1)} %get-tuple-element.38), kind=kLoop, calls=%fused_computation.1 | loop fusion | flops 1048576 | bytes 1572864 | tf_op jit(solution)/shard_map/convert_element_type | solution.py:318
  74.1 12.5 %all-to-all-start.2 = ((bf16[32,32,256]{2,1,0:T(8,128)(2,1)}), bf16[32,32,256]{2,1,0:T(8,128)(2,1)}, u32[]{:S(2)}, u32[]{:S(2)}) async-start(bf16[32,32,256]{2,1,0:T(8,128)(2,1)} %bitcast.1), calls=%async_computation.2 | async-start | bytes 1048576 | tf_op jit(solution)/shard_map/all_to_all | solution.py:320
  89.3 4.2 %attend.1 = (bf16[512,256]{1,0:T(8,128)(2,1)}, f32[512,256]{1,0:T(8,128)S(1)}, f32[512,256]{1,0:T(8,128)S(1)}, bf16[768,256]{1,0:T(8,128)(2,1)S(1)}, bf16[256,25...) custom-call(bf16[4,896,256]{2,1,0:T(8,128)(2,1)S(1)} %copy-done.1, ...), custom_call_target="tpu_custom_call" | custom-call | tf_op jit(solution)/shard_map/attend/pallas_call | solution.py:257
  94.8 1.3 %collective-permute-start.10 = (bf16[256,256]{1,0:T(8,128)(2,1)S(1)}, bf16[256,256]{1,0:T(8,128)(2,1)S(1)}, u32[]{:S(2)}, u32[]{:S(2)}) collective-permute-start(bf16[256,256]{1,0:T(8,128)(2,1)S(1)} %get-tuple-element.35), channel_id=1, source_target_pairs={{128,0},{136,8},{144,16},{152,24},{160,32},{168,40},{176,48},{184,... | collective-permute-start | bytes 393224 | tf_op jit(solution)/shard_map/ppermute | solution.py:297
  96.1 1.3 %collective-permute-start.7 = (bf16[256,256]{1,0:T(8,128)(2,1)S(1)}, bf16[256,256]{1,0:T(8,128)(2,1)S(1)}, u32[]{:S(2)}, u32[]{:S(2)}) collective-permute-start(bf16[256,256]{1,0:T(8,128)(2,1)S(1)} %get-tuple-element.32), channel_id=1, source_target_pairs={{16,0},{24,8},{32,16},{40,24},{48,32},{56,40},{64,48},{72,56},{80,... | collective-permute-start | bytes 393224 | tf_op jit(solution)/shard_map/ppermute | solution.py:297
  97.4 1.3 %collective-permute-start.8 = (bf16[256,256]{1,0:T(8,128)(2,1)S(1)}, bf16[256,256]{1,0:T(8,128)(2,1)S(1)}, u32[]{:S(2)}, u32[]{:S(2)}) collective-permute-start(bf16[256,256]{1,0:T(8,128)(2,1)S(1)} %get-tuple-element.33), channel_id=1, source_target_pairs={{32,0},{40,8},{48,16},{56,24},{64,32},{72,40},{80,48},{88,56},{96,... | collective-permute-start | bytes 393224 | tf_op jit(solution)/shard_map/ppermute | solution.py:297
  100.0 10.2 %collective-permute-done.10.f4 = bf16[256,256]{1,0:T(8,128)(2,1)S(1)} collective-permute-done((bf16[256,256]{1,0:T(8,128)(2,1)S(1)}, bf16[256,256]{1,0:T(8,128)(2,1)S(1)}, u32[]{:S(2)}, u32[]{:S(2)}) %collective-permute-start.10) | collective-permute-done | bytes 131104 | tf_op jit(solution)/shard_map/ppermute | solution.py:297
  110.3 1.7 %collective-permute-done.7.f1 = bf16[256,256]{1,0:T(8,128)(2,1)S(1)} collective-permute-done((bf16[256,256]{1,0:T(8,128)(2,1)S(1)}, bf16[256,256]{1,0:T(8,128)(2,1)S(1)}, u32[]{:S(2)}, u32[]{:S(2)}) %collective-permute-start.7) | collective-permute-done | bytes 131104 | tf_op jit(solution)/shard_map/ppermute | solution.py:297
  112.0 9.9 %collective-permute-done.8.f2 = bf16[256,256]{1,0:T(8,128)(2,1)S(1)} collective-permute-done((bf16[256,256]{1,0:T(8,128)(2,1)S(1)}, bf16[256,256]{1,0:T(8,128)(2,1)S(1)}, u32[]{:S(2)}, u32[]{:S(2)}) %collective-permute-start.8) | collective-permute-done | bytes 131104 | tf_op jit(solution)/shard_map/ppermute | solution.py:297
  121.9 1.6 %finish.1 = (bf16[512,256]{1,0:T(8,128)(2,1)}, bf16[512,256]{1,0:T(8,128)(2,1)}) custom-call(s32[1,5]{1,0:T(1,128)S(1)} %copy-done.13, f32[512,256]{1,0:T(8,128)S(1)} %get-tuple-element.29.own_k, f32[512,256]{1,0:T(8,128)S(1)} %get-tuple-element.30.own_v, bf16[768,256]{1,0:T(8,128)(2,1)S(1)} %collective-permute-done.6.near_ref, ...), custom_call_target="tpu_custom_call" | custom-call | tf_op jit(solution)/shard_map/finish/pallas_call | solution.py:285
  (46 shorter events, 13.2 us)
Async XLA Ops:
  0.6 11.5 %copy-start.2 = (bf16[512,256]{1,0:T(8,128)(2,1)S(1)}, bf16[512,256]{1,0:T(8,128)(2,1)}, u32[]{:S(2)}) copy-start(bf16[512,256]{1,0:T(8,128)(2,1)} %k_ref.5) | copy-start | bytes 786436
  0.6 11.5 %copy-start.5 = (bf16[512,256]{1,0:T(8,128)(2,1)S(1)}, bf16[512,256]{1,0:T(8,128)(2,1)}, u32[]{:S(2)}) copy-start(bf16[512,256]{1,0:T(8,128)(2,1)} %v_ref.3) | copy-start | bytes 786436
  1.7 10.5 %copy-start.13 = (s32[1,5]{1,0:T(1,128)S(1)}, s32[1,5]{1,0:T(1,128)}, u32[]{:S(2)}) copy-start(s32[1,5]{1,0:T(1,128)} %pick.3) | copy-start | bytes 64
  1.7 12.4 %copy-start.11 = (bf16[512,256]{1,0:T(8,128)(2,1)S(1)}, bf16[512,256]{1,0:T(8,128)(2,1)}, u32[]{:S(2)}) copy-start(bf16[512,256]{1,0:T(8,128)(2,1)} %b_ref.1) | copy-start | bytes 786436
  2.7 30.3 %all-to-all-start = ((bf16[4,512,256]{2,1,0:T(8,128)(2,1)}), bf16[4,512,256]{2,1,0:T(8,128)(2,1)S(1)}, u32[]{:S(2)}, u32[]{:S(2)}) async-start(bf16[4,512,256]{2,1,0:T(8,128)(2,1)} %spread.2), calls=%async_computation | async-start | bytes 2097152 | tf_op jit(solution)/shard_map/all_to_all | solution.py:304
  12.7 19.2 %collective-permute-start = (bf16[768,256]{1,0:T(8,128)(2,1)S(1)}, bf16[768,256]{1,0:T(8,128)(2,1)S(1)}, u32[]{:S(2)}, u32[]{:S(2)}) collective-permute-start(bf16[768,256]{1,0:T(8,128)(2,1)S(1)} %get-tuple-element.22), channel_id=1, source_target_pairs={{0,8},{8,16},{16,24},{24,32},{32,40},{40,48},{48,56},{56,64},{64,7... | collective-permute-start | bytes 1179656 | tf_op jit(solution)/shard_map/ppermute | solution.py:297
  14.1 17.9 %collective-permute-start.5 = (bf16[512,256]{1,0:T(8,128)(2,1)S(1)}, bf16[512,256]{1,0:T(8,128)(2,1)S(1)}, u32[]{:S(2)}, u32[]{:S(2)}) collective-permute-start(bf16[512,256]{1,0:T(8,128)(2,1)S(1)} %copy-done.11), channel_id=1, source_target_pairs={{0,4},{1,5},{2,6},{3,7},{4,0},{5,1},{6,2},{7,3},{8,12},{9,13},{10,... | collective-permute-start | bytes 786440 | tf_op jit(solution)/shard_map/ppermute | solution.py:309
  17.2 11.1 %collective-permute-start.1 = (bf16[256,256]{1,0:T(8,128)(2,1)S(1)}, bf16[256,256]{1,0:T(8,128)(2,1)S(1)}, u32[]{:S(2)}, u32[]{:S(2)}) collective-permute-start(bf16[256,256]{1,0:T(8,128)(2,1)S(1)} %get-tuple-element.23), channel_id=1, source_target_pairs={{0,16},{8,24},{16,32},{24,40},{32,48},{40,56},{48,64},{56,72},{64,... | collective-permute-start | bytes 393224 | tf_op jit(solution)/shard_map/ppermute | solution.py:297
  22.1 36.1 %copy-start.3 = (bf16[512,256]{1,0:T(8,128)(2,1)S(1)}, bf16[512,256]{1,0:T(8,128)(2,1)}, u32[]{:S(2)}) copy-start(bf16[512,256]{1,0:T(8,128)(2,1)} %q_ref.3) | copy-start | bytes 786436
  22.1 8.7 %collective-permute-start.2 = (bf16[256,256]{1,0:T(8,128)(2,1)S(1)}, bf16[256,256]{1,0:T(8,128)(2,1)S(1)}, u32[]{:S(2)}, u32[]{:S(2)}) collective-permute-start(bf16[256,256]{1,0:T(8,128)(2,1)S(1)} %get-tuple-element.24), channel_id=1, source_target_pairs={{0,32},{8,40},{16,48},{24,56},{32,64},{40,72},{48,80},{56,88},{64,... | collective-permute-start | bytes 393224 | tf_op jit(solution)/shard_map/ppermute | solution.py:297
  33.0 27.0 %copy-start.14 = (bf16[4,512,256]{2,1,0:T(8,128)(2,1)}, bf16[4,512,256]{2,1,0:T(8,128)(2,1)S(1)}, u32[]{:S(2)}) copy-start(bf16[4,512,256]{2,1,0:T(8,128)(2,1)S(1)} %all-to-all-done.mine_hbm) | copy-start | bytes 3145732
  33.0 28.3 %all-to-all-start.1 = ((bf16[4,512,256]{2,1,0:T(8,128)(2,1)}), bf16[4,512,256]{2,1,0:T(8,128)(2,1)}, u32[]{:S(2)}, u32[]{:S(2)}) async-start(bf16[4,512,256]{2,1,0:T(8,128)(2,1)} %spread.3), calls=%async_computation.1 | async-start | bytes 2097152 | tf_op jit(solution)/shard_map/all_to_all | solution.py:304
  37.8 17.3 %collective-permute-start.3 = (bf16[256,256]{1,0:T(8,128)(2,1)S(1)}, bf16[256,256]{1,0:T(8,128)(2,1)S(1)}, u32[]{:S(2)}, u32[]{:S(2)}) collective-permute-start(bf16[256,256]{1,0:T(8,128)(2,1)S(1)} %get-tuple-element.25), channel_id=1, source_target_pairs={{0,64},{8,72},{16,80},{24,88},{32,96},{40,104},{48,112},{56,120},{... | collective-permute-start | bytes 393224 | tf_op jit(solution)/shard_map/ppermute | solution.py:297
  51.3 6.9 %collective-permute-start.4 = (bf16[256,256]{1,0:T(8,128)(2,1)S(1)}, bf16[256,256]{1,0:T(8,128)(2,1)S(1)}, u32[]{:S(2)}, u32[]{:S(2)}) collective-permute-start(bf16[256,256]{1,0:T(8,128)(2,1)S(1)} %get-tuple-element.26), channel_id=1, source_target_pairs={{0,128},{8,136},{16,144},{24,152},{32,160},{40,168},{48,176},{56,1... | collective-permute-start | bytes 393224 | tf_op jit(solution)/shard_map/ppermute | solution.py:297
  55.1 6.2 %copy-start.6 = (bf16[256,256]{1,0:T(8,128)(2,1)}, bf16[256,256]{1,0:T(8,128)(2,1)S(1)}, u32[]{:S(2)}) copy-start(bf16[256,256]{1,0:T(8,128)(2,1)S(1)} %collective-permute-done.3.f3) | copy-start | bytes 393220
  67.9 18.6 %copy-start.1 = (bf16[4,896,256]{2,1,0:T(8,128)(2,1)S(1)}, bf16[4,896,256]{2,1,0:T(8,128)(2,1)}, u32[]{:S(2)}) copy-start(bf16[4,896,256]{2,1,0:T(8,128)(2,1)} %copy-done) | copy-start | bytes 5505028
  67.9 18.6 %copy-start.4 = (bf16[512,256]{1,0:T(8,128)(2,1)S(1)}, bf16[512,256]{1,0:T(8,128)(2,1)}, u32[]{:S(2)}) copy-start(bf16[512,256]{1,0:T(8,128)(2,1)} %o_ref.1) | copy-start | bytes 786436
  68.0 4.1 %collective-permute-start.11 = (bf16[1024,256]{1,0:T(8,128)(2,1)}, bf16[1024,256]{1,0:T(8,128)(2,1)S(1)}, u32[]{:S(2)}, u32[]{:S(2)}) collective-permute-start(bf16[1024,256]{1,0:T(8,128)(2,1)} %get-tuple-element.39), channel_id=1, source_target_pairs={{0,8},{8,0},{16,24},{24,16},{32,40},{40,32},{48,56},{56,48},{64,72... | collective-permute-start | bytes 1572872 | tf_op jit(solution)/shard_map/ppermute | solution.py:315
  74.1 49.4 %all-to-all-start.2 = ((bf16[32,32,256]{2,1,0:T(8,128)(2,1)}), bf16[32,32,256]{2,1,0:T(8,128)(2,1)}, u32[]{:S(2)}, u32[]{:S(2)}) async-start(bf16[32,32,256]{2,1,0:T(8,128)(2,1)} %bitcast.1), calls=%async_computation.2 | async-start | bytes 1048576 | tf_op jit(solution)/shard_map/all_to_all | solution.py:320
  93.6 28.4 %collective-permute-start.6 = (bf16[768,256]{1,0:T(8,128)(2,1)S(1)}, bf16[768,256]{1,0:T(8,128)(2,1)S(1)}, u32[]{:S(2)}, u32[]{:S(2)}) collective-permute-start(bf16[768,256]{1,0:T(8,128)(2,1)S(1)} %get-tuple-element.31), channel_id=1, source_target_pairs={{8,0},{16,8},{24,16},{32,24},{40,32},{48,40},{56,48},{64,56},{72,6... | collective-permute-start | bytes 1179656 | tf_op jit(solution)/shard_map/ppermute | solution.py:297
  94.8 15.4 %collective-permute-start.10 = (bf16[256,256]{1,0:T(8,128)(2,1)S(1)}, bf16[256,256]{1,0:T(8,128)(2,1)S(1)}, u32[]{:S(2)}, u32[]{:S(2)}) collective-permute-start(bf16[256,256]{1,0:T(8,128)(2,1)S(1)} %get-tuple-element.35), channel_id=1, source_target_pairs={{128,0},{136,8},{144,16},{152,24},{160,32},{168,40},{176,48},{184,... | collective-permute-start | bytes 393224 | tf_op jit(solution)/shard_map/ppermute | solution.py:297
  96.1 15.9 %collective-permute-start.7 = (bf16[256,256]{1,0:T(8,128)(2,1)S(1)}, bf16[256,256]{1,0:T(8,128)(2,1)S(1)}, u32[]{:S(2)}, u32[]{:S(2)}) collective-permute-start(bf16[256,256]{1,0:T(8,128)(2,1)S(1)} %get-tuple-element.32), channel_id=1, source_target_pairs={{16,0},{24,8},{32,16},{40,24},{48,32},{56,40},{64,48},{72,56},{80,... | collective-permute-start | bytes 393224 | tf_op jit(solution)/shard_map/ppermute | solution.py:297
  97.4 24.5 %collective-permute-start.8 = (bf16[256,256]{1,0:T(8,128)(2,1)S(1)}, bf16[256,256]{1,0:T(8,128)(2,1)S(1)}, u32[]{:S(2)}, u32[]{:S(2)}) collective-permute-start(bf16[256,256]{1,0:T(8,128)(2,1)S(1)} %get-tuple-element.33), channel_id=1, source_target_pairs={{32,0},{40,8},{48,16},{56,24},{64,32},{72,40},{80,48},{88,56},{96,... | collective-permute-start | bytes 393224 | tf_op jit(solution)/shard_map/ppermute | solution.py:297
  98.7 23.2 %collective-permute-start.9 = (bf16[256,256]{1,0:T(8,128)(2,1)S(1)}, bf16[256,256]{1,0:T(8,128)(2,1)S(1)}, u32[]{:S(2)}, u32[]{:S(2)}) collective-permute-start(bf16[256,256]{1,0:T(8,128)(2,1)S(1)} %get-tuple-element.34), channel_id=1, source_target_pairs={{64,0},{72,8},{80,16},{88,24},{96,32},{104,40},{112,48},{120,56},{... | collective-permute-start | bytes 393224 | tf_op jit(solution)/shard_map/ppermute | solution.py:297
  (6 other events, 8.1 us)

commit v3 on v1

v3 whole, which is shorter than its diff:
```python
import jax
import jax.numpy as jnp
from jax import lax
from jax.experimental import pallas as pl
from jax.experimental.pallas import tpu as pltpu
from jax.sharding import PartitionSpec as P

HD = 128
WIN = 256
BLK = 128
LEVELS = 5
GATE_MIB = 60
ATTEND_MIB = 60
BF = jnp.bfloat16
F32 = jnp.float32
NX, NZ, NYL = 4, 8, 4
VMEM = pl.BlockSpec(memory_space=pltpu.VMEM)
PIECES = 1
ANY = pl.BlockSpec(memory_space=pl.ANY)
SMEM = pl.BlockSpec(memory_space=pltpu.SMEM)


def params(mib=16):
    return pltpu.CompilerParams(vmem_limit_bytes=mib * 1024 * 1024)


def dot(a, b, ca, cb):
    return lax.dot_general(a, b, (((ca,), (cb,)), ((), ())), preferred_element_type=F32)


def pack_kernel(pick, k_ref, v_ref, near_ref, *far_refs):
    near_ref[0:WIN, :] = k_ref[512 - WIN :, :]
    near_ref[WIN : 2 * WIN, :] = v_ref[512 - WIN :, :]
    for level in range(LEVELS):
        first = pl.multiple_of(pick[0, level] * BLK, BLK)
        ref, at = (near_ref, 2 * WIN) if level == 0 else (far_refs[level - 1], 0)
        ref[at : at + BLK, :] = k_ref[pl.ds(first, BLK), :]
        ref[at + BLK : at + 2 * BLK, :] = v_ref[pl.ds(first, BLK), :]


def pack(pick, keys, values):
    return pl.pallas_call(
        pack_kernel,
        out_shape=[jax.ShapeDtypeStruct((2 * WIN + 2 * BLK, 256), BF)]
        + [jax.ShapeDtypeStruct((2 * BLK, 256), BF)] * (LEVELS - 1),
        in_specs=[SMEM, VMEM, VMEM],
        out_specs=[VMEM] * LEVELS,
        compiler_params=params(),
        name="pack",
    )(pick, keys, values)


def k_rows(near_ref, fars, lanes):
    return jnp.concatenate(
        [near_ref[2 * WIN : 2 * WIN + BLK, lanes]] + [r[0:BLK, lanes] for r in fars], axis=0
    )


def v_rows(near_ref, fars, lanes):
    return jnp.concatenate(
        [near_ref[2 * WIN + BLK :, lanes]] + [r[BLK:, lanes] for r in fars], axis=0
    )


def earlier_tile():
    row = lax.broadcasted_iota(jnp.int32, (256, 256), 0)
    col = lax.broadcasted_iota(jnp.int32, (256, 256), 1)
    return row > col


def sources():
    head = lax.axis_index("head")
    yh = head // NX
    return [(yh if at < NX else 1 - yh) * NX + at % NX for at in range(2 * NX)]


def piece(refs, at):
    low = at // NX * 512
    return refs[0][at % NX, low : low + 512, :]


def gate_kernel(*refs):
    refs[-1][...] = jnp.zeros((8, 128), F32)


def gate(*got):
    return pl.pallas_call(
        gate_kernel,
        out_shape=jax.ShapeDtypeStruct((8, 128), F32),
        in_specs=[ANY] * len(got),
        out_specs=VMEM,
        compiler_params=params(GATE_MIB),
        cost_estimate=pl.CostEstimate(
            flops=13000000000, bytes_accessed=2**20, transcendentals=0
        ),
        name="gate",
    )(*got)


def project_kernel(*refs):
    pieces, (w_ref, o_ref, ready) = refs[:PIECES], refs[PIECES : PIECES + 3]
    dout_ref, keep_ref, send_ref = refs[PIECES + 3 :]
    core = lax.axis_index("tm") % 2
    o = o_ref[...]
    acc = jnp.zeros((512, 256), F32)
    for at, src in enumerate(sources()):
        cot = piece(pieces, at)
        acc = acc + dot(cot, w_ref[pl.ds(pl.multiple_of(src * 256, 256), 256), :], 1, 0)
        term = dot(cot, o, 0, 0).astype(BF)
        for sub in range(4):
            rows = pl.ds(pl.multiple_of(src * 128 + sub * 32, 32), 32)
            low = term[sub * 64 : sub * 64 + 32, :]
            high = term[sub * 64 + 32 : sub * 64 + 64, :]
            keep_ref[rows, :] = jnp.where(core == 0, low, high)
            send_ref[rows, :] = jnp.where(core == 0, high, low)
    dout_ref[...] = acc.astype(BF)


def project(pieces, out_weight, outputs, ready):
    half = jax.ShapeDtypeStruct((1024, 256), BF)
    return pl.pallas_call(
        project_kernel,
        out_shape=[jax.ShapeDtypeStruct((512, 256), BF), half, half],
        in_specs=[VMEM] * (PIECES + 2) + [ANY],
        out_specs=[VMEM] * 3,
        compiler_params=params(),
        name="project",
    )(*pieces, out_weight, outputs, ready)


def attend_kernel(
    q_hbm, k_hbm, v_hbm, o_hbm, do_hbm, near_hbm, f1, f2, f3, f4,
    dq_ref, own_k, own_v, back_near, b1, b2, b3, b4, token,
    q_ref, k_ref, v_ref, o_ref, do_ref, near_ref, f_ref, fk, fv, sems,
):
    token[...] = jnp.zeros((8, 128), F32)
    pairs = [(q_hbm, q_ref), (k_hbm, k_ref), (near_hbm, near_ref)]
    pairs += [(f, f_ref.at[i]) for i, f in enumerate((f1, f2, f3, f4))]
    pairs += [(v_hbm, v_ref), (do_hbm, do_ref), (o_hbm, o_ref)]
    loads = [pltpu.make_async_copy(src, dst, sems.at[i]) for i, (src, dst) in enumerate(pairs)]
    for load in loads:
        load.start()
    scale = HD ** (-0.5)
    shard = lax.axis_index("tm")
    neg = jnp.float32(-1e30)
    zero = jnp.zeros((), F32)
    earlier = earlier_tile()
    level_of = lax.broadcasted_iota(jnp.int32, (LEVELS * BLK, 256), 0) // BLK
    far_ok = shard >= (1 << level_of)
    fars = [f_ref.at[i] for i in range(LEVELS - 1)]
    for load in loads[: LEVELS + 2]:
        load.wait()
    for head in range(2):
        lanes = slice(head * HD, (head + 1) * HD)
        k_far = k_rows(near_ref, fars, lanes)
        v_far = v_rows(near_ref, fars, lanes)
        for blk in range(2):
            rows = slice(blk * 256, (blk + 1) * 256)
            q = q_ref[rows, lanes]
            k_here = k_ref[rows, lanes]
            k_prev = near_ref[0:WIN, lanes] if blk == 0 else k_ref[0:256, lanes]
            s_prev = dot(k_prev, q, 1, 1) * scale
            s_here = dot(k_here, q, 1, 1) * scale
            s_far = dot(k_far, q, 1, 1) * scale
            if blk == 0:
                s_prev = jnp.where(shard > 0, s_prev, neg)
            s_near = jnp.where(earlier, s_prev, s_here)
            s_far = jnp.where(far_ok, s_far, neg)
            top = jnp.maximum(
                jnp.max(s_near, axis=0, keepdims=True), jnp.max(s_far, axis=0, keepdims=True)
            )
            e_near, e_far = jnp.exp(s_near - top), jnp.exp(s_far - top)
            inv = 1.0 / (
                jnp.sum(e_near, axis=0, keepdims=True) + jnp.sum(e_far, axis=0, keepdims=True)
            )
            p_near, p_far = e_near * inv, e_far * inv
            if head == 0 and blk == 0:
                for load in loads[LEVELS + 2 :]:
                    load.wait()
            do = do_ref[rows, lanes]
            v_here = v_ref[rows, lanes]
            v_prev = near_ref[WIN : 2 * WIN, lanes] if blk == 0 else v_ref[0:256, lanes]
            delta = jnp.sum(
                do.astype(F32) * o_ref[rows, lanes].astype(F32), axis=1, keepdims=True
            )
            delta = jnp.transpose(jnp.broadcast_to(delta, (256, 128)))[0:1, :]
            dp_near = jnp.where(earlier, dot(v_prev, do, 1, 1), dot(v_here, do, 1, 1))
            dp_far = dot(v_far, do, 1, 1)
            ds_near = p_near * (dp_near - delta)
            ds_far = (p_far * (dp_far - delta)).astype(BF)
            ds_prev = jnp.where(earlier, ds_near, zero).astype(BF)
            ds_here = jnp.where(earlier, zero, ds_near).astype(BF)
            p_prev = jnp.where(earlier, p_near, zero).astype(BF)
            p_here = jnp.where(earlier, zero, p_near).astype(BF)
            p_far = p_far.astype(BF)
            dq = dot(ds_prev, k_prev, 0, 0) + dot(ds_here, k_here, 0, 0) + dot(ds_far, k_far, 0, 0)
            dq_ref[rows, lanes] = (dq * scale).astype(BF)
            dk_prev, dv_prev = dot(ds_prev, q, 1, 0) * scale, dot(p_prev, do, 1, 0)
            dk_here, dv_here = dot(ds_here, q, 1, 0) * scale, dot(p_here, do, 1, 0)
            dk_far, dv_far = dot(ds_far, q, 1, 0) * scale, dot(p_far, do, 1, 0)
            if blk == 0:
                back_near[0:WIN, lanes] = dk_prev.astype(BF)
                back_near[WIN : 2 * WIN, lanes] = dv_prev.astype(BF)
                own_k[0:256, lanes] = dk_here
                own_v[0:256, lanes] = dv_here
                fk[...] = dk_far
                fv[...] = dv_far
            else:
                own_k[0:256, lanes] += dk_prev
                own_v[0:256, lanes] += dv_prev
                own_k[256:512, lanes] = dk_here
                own_v[256:512, lanes] = dv_here
                for i, r in enumerate((back_near, b1, b2, b3, b4)):
                    at = 2 * WIN if i == 0 else 0
                    part = slice(i * BLK, (i + 1) * BLK)
                    r[at : at + BLK, lanes] = (fk[part, :] + dk_far[part]).astype(BF)
                    r[at + BLK : at + 2 * BLK, lanes] = (fv[part, :] + dv_far[part]).astype(BF)


def attend(queries, keys, values, outputs, d_out, got):
    f32s = jax.ShapeDtypeStruct((512, 256), F32)
    far = jax.ShapeDtypeStruct((2 * BLK, 256), BF)
    here = pltpu.VMEM((512, 256), BF)
    return pl.pallas_call(
        attend_kernel,
        out_shape=[
            jax.ShapeDtypeStruct((512, 256), BF), f32s, f32s,
            jax.ShapeDtypeStruct((2 * WIN + 2 * BLK, 256), BF), far, far, far, far,
            jax.ShapeDtypeStruct((8, 128), F32),
        ],
        in_specs=[ANY] * 10,
        out_specs=[VMEM] * 9,
        scratch_shapes=[
            here, here, here, here, here,
            pltpu.VMEM((2 * WIN + 2 * BLK, 256), BF),
            pltpu.VMEM((LEVELS - 1, 2 * BLK, 256), BF),
            pltpu.VMEM((LEVELS * BLK, HD), F32),
            pltpu.VMEM((LEVELS * BLK, HD), F32),
            pltpu.SemaphoreType.DMA((10,)),
        ],
        compiler_params=params(ATTEND_MIB),
        name="attend",
    )(queries, keys, values, outputs, d_out, *got)


def add_kernel(keep_ref, got_ref, out_ref):
    out_ref[...] = (keep_ref[...].astype(F32) + got_ref[...].astype(F32)).astype(BF)


def add(keep, received):
    return pl.pallas_call(
        add_kernel,
        out_shape=jax.ShapeDtypeStruct((1024, 256), BF),
        in_specs=[VMEM, VMEM],
        out_specs=VMEM,
        compiler_params=params(),
        name="add",
    )(keep, received)


def total_kernel(part_ref, out_ref):
    out_ref[...] = jnp.sum(part_ref[...].astype(F32), axis=0) * (512 * 64) ** (-0.5)


def total(part):
    return pl.pallas_call(
        total_kernel,
        out_shape=jax.ShapeDtypeStruct((32, 256), F32),
        in_specs=[VMEM],
        out_specs=VMEM,
        compiler_params=params(),
        name="total",
    )(part)


def finish_kernel(pick, own_k, own_v, near_ref, f1, f2, f3, f4, dk_ref, dv_ref, tk, tv):
    for ref, acc, at in ((own_k, tk, 0), (own_v, tv, 1)):
        acc[0:256, :] = ref[0:256, :]
        acc[256:512, :] = ref[256:512, :] + near_ref[at * WIN : (at + 1) * WIN, :].astype(F32)
        for level, far in enumerate((near_ref, f1, f2, f3, f4)):
            low = (2 * WIN if level == 0 else 0) + at * BLK
            rows = pl.ds(pl.multiple_of(pick[0, level] * BLK, BLK), BLK)
            acc[rows, :] += far[low : low + BLK, :].astype(F32)
    dk_ref[...] = tk[...].astype(BF)
    dv_ref[...] = tv[...].astype(BF)


def finish(pick, own_k, own_v, got):
    out = jax.ShapeDtypeStruct((512, 256), BF)
    return pl.pallas_call(
        finish_kernel,
        out_shape=[out, out],
        in_specs=[SMEM] + [VMEM] * 7,
        out_specs=[VMEM] * 2,
        scratch_shapes=[pltpu.VMEM((512, 256), F32)] * 2,
        compiler_params=params(),
        cost_estimate=pl.CostEstimate(
            flops=5000000000, bytes_accessed=2**20, transcendentals=0
        ),
        name="finish",
    )(pick, own_k, own_v, *got)


def shift(block, distance):
    return lax.ppermute(
        block, "tm", [(i, i + distance) for i in range(64) if 0 <= i + distance < 64]
    )


def spread_kernel(a_ref, b_ref, out_ref):
    for i in range(NX):
        out_ref[i, 0:512, :] = a_ref[...]
        out_ref[i, 512:1024, :] = b_ref[...]


def spread(block, other):
    return pl.pallas_call(
        spread_kernel,
        out_shape=jax.ShapeDtypeStruct((NX, 1024, 256), BF),
        in_specs=[VMEM] * 2,
        out_specs=VMEM,
        compiler_params=params(),
        name="spread",
    )(block, other)


def to_row(blocks):
    rows = [[yh * NX + x for x in range(NX)] for yh in range(2)]
    return lax.all_to_all(blocks, "head", 0, 0, axis_index_groups=rows)


def on_device(queries, keys, values, outputs, out_cotangent, out_weight, block_pick):
    other = lax.ppermute(out_cotangent, "head", [(h, (h + NX) % (2 * NX)) for h in range(2 * NX)])
    packed = pack(block_pick, keys, values)
    got = [shift(b, 2**level) for level, b in enumerate(packed)]
    pieces = [to_row(spread(out_cotangent, other))]
    ready = gate(got[0], got[1], got[2], got[3], got[4])
    d_out, keep, send = project(pieces, out_weight, outputs, ready)
    received = lax.ppermute(send, "tm", [(i, i ^ 1) for i in range(64)])
    dq, own_k, own_v, *back, token = attend(queries, keys, values, outputs, d_out, got)
    back = [shift(b, -(2**level)) for level, b in enumerate(back)]
    half = add(keep, received).reshape(NYL * NZ, 32, 256)
    groups = [[2 * i + c for i in range(NYL * NZ)] for c in range(2)]
    part = lax.all_to_all(half, "tm", 0, 0, axis_index_groups=groups)
    weight_grad = total(part)
    dk, dv = finish(block_pick, own_k, own_v, back)
    return dq, dk, dv, weight_grad


def solution(mesh):
    placed = (P("tm", "head"),) * 5 + (P(None, "head"), P("tm", None))
    return jax.shard_map(
        on_device,
        mesh=mesh,
        in_specs=placed,
        out_specs=(P("tm", "head"),) * 4,
        check_vma=False,
    )
```

time: 135 us -> 114 us (0.84)
  starting transfers between devices: 88.2 us -> 66.7 us
  waiting for transfers between devices: 27.2 us -> 20.9 us
  Pallas kernels: 10 us -> 15.7 us
  local copies, waits for them, and re-layouts: 3.79 us -> 7.62 us
  other arithmetic: 2.36 us -> 0 us
    ppermute x6 -> x0, starting transfers between devices: 18.4 us -> none  [turn_x(): lax.ppermute(block, 'head', [(h, h // NX * NX + (h % NX + offset) % NX) f...]
    all_to_all x2, starting transfers between devices: 32.6 us -> 17.3 us  [the longest x1 13.3 us: on_device(): part = lax.all_to_all(half, 'tm', 0, 0, axis_index_groups=groups)]
    ppermute x10, waiting for transfers between devices: 4.76 us -> 19.4 us  [shift(): lax.ppermute(block, 'tm', [(i, i + distance) for i in range(64) if 0 <= i...]
    ppermute x6 -> x0, waiting for transfers between devices: 13.7 us -> none  [turn_x(): lax.ppermute(block, 'head', [(h, h // NX * NX + (h % NX + offset) % NX) f...]
    all_to_all x2, waiting for transfers between devices: 7.21 us -> 0.01 us  [the longest x1 0.01 us: on_device(): part = lax.all_to_all(half, 'tm', 0, 0, axis_index_groups=groups)]
    ppermute x10, starting transfers between devices: 26.3 us -> 33.2 us  [shift(): lax.ppermute(block, 'tm', [(i, i + distance) for i in range(64) if 0 <= i...]
    ppermute x1, starting transfers between devices: 2.6 us -> 8.02 us  [on_device(): received = lax.ppermute(send, 'tm', [(i, i ^ 1) for i in range(64)])]
    unnamed x16 -> x30, local copies, waits for them, and re-layouts: 3.79 us -> 7.62 us
  transfers between devices with their start and end apart: 20 -> 14, of which waited for: 9 -> 6; matrix products, arithmetic and copies ran while one was open for 1% -> 0% of each run, Pallas kernels for 6% -> 11%
where the time goes in v3:
time: 114 us; the launch traced here: 112 us
  starting transfers between devices  66.7 us (59%)
  waiting for transfers between devices  20.9 us (18%)
  Pallas kernels  15.7 us (14%)
  local copies, waits for them, and re-layouts  7.62 us (7%)
    ppermute x10, starting transfers between devices, shift(): lax.ppermute(block, 'tm', [(i, i + distance) for i in range(64) if 0 <= i...  33.2 us
    ppermute x10, waiting for transfers between devices, shift(): lax.ppermute(block, 'tm', [(i, i + distance) for i in range(64) if 0 <= i...  19.4 us
    all_to_all x1, starting transfers between devices, on_device(): part = lax.all_to_all(half, 'tm', 0, 0, axis_index_groups=groups)  13.3 us
    ppermute x1, starting transfers between devices, on_device(): lax.ppermute(out_cotangent, 'head', [(h, (h + NX) % (2 * NX)) for h in ra...  8.28 us
    ppermute x1, starting transfers between devices, on_device(): received = lax.ppermute(send, 'tm', [(i, i ^ 1) for i in range(64)])  8.02 us
    pallas_call x1, Pallas kernels, attend(): pl.pallas_call(attend_kernel, out_shape=[jax.ShapeDtypeStruct((512, 256),...  7.73 us
    unnamed x30, local copies, waits for them, and re-layouts  7.62 us
    all_to_all x1, starting transfers between devices, to_row(): return lax.all_to_all(blocks, 'head', 0, 0, axis_index_groups=rows)  4.01 us
  transfers between devices with their start and end apart: 14, of which 6 were waited for; matrix products, arithmetic and copies ran while one was open for 0% of the time, Pallas kernels for 11%

profile of v3, /device:TPU:1, one launch (start us, length us, event | category | flops | bytes accessed | tf_op | source)
XLA Modules:
  0.0 111.9 jit_solution(13398315037102740965)
XLA Ops:
  0.6 8.3 %collective-permute-start = (bf16[512,256]{1,0:T(8,128)(2,1)}, bf16[512,256]{1,0:T(8,128)(2,1)S(1)}, u32[]{:S(2)}, u32[]{:S(2)}) collective-permute-start(bf16[512,256]{1,0:T(8,128)(2,1)} %a_ref.1), channel_id=1, source_target_pairs={{0,4},{1,5},{2,6},{3,7},{4,0},{5,1},{6,2},{7,3},{8,12},{9,13},{10,... | collective-permute-start | bytes 786440 | tf_op jit(solution)/shard_map/ppermute | solution.py:333
  11.5 1.5 %pack.1 = (bf16[768,256]{1,0:T(8,128)(2,1)}, bf16[256,256]{1,0:T(8,128)(2,1)}, bf16[256,256]{1,0:T(8,128)(2,1)}, bf16[256,256]{1,0:T(8,128)(2,1)}, bf16[256,256]{1,0:T(8,128)(2,1)S(1)}) custom-call(s32[1,5]{1,0:T(1,128)S(1)} %copy-done.7, bf16[512,256]{1,0:T(8,128)(2,1)S(1)} %copy-done, bf16[512,256]{1,0:T(8,128)(2,1)S(1)} %copy-done.1), custom_call_target="tpu_custom_call" | custom-call | tf_op jit(solution)/shard_map/pack/pallas_call | solution.py:42
  12.9 4.8 %collective-permute-start.1 = (bf16[768,256]{1,0:T(8,128)(2,1)}, bf16[768,256]{1,0:T(8,128)(2,1)}, u32[]{:S(2)}, u32[]{:S(2)}) collective-permute-start(bf16[768,256]{1,0:T(8,128)(2,1)} %get-tuple-element.22), channel_id=1, source_target_pairs={{0,8},{8,16},{16,24},{24,32},{32,40},{40,48},{48,56},{56,64},{64,7... | collective-permute-start | bytes 1179656 | tf_op jit(solution)/shard_map/ppermute | solution.py:305
  18.7 1.5 %spread.1 = bf16[4,1024,256]{2,1,0:T(8,128)(2,1)} custom-call(bf16[512,256]{1,0:T(8,128)(2,1)S(1)} %copy-done.4, bf16[512,256]{1,0:T(8,128)(2,1)S(1)} %collective-permute-done.b_ref), custom_call_target="tpu_custom_call" | custom-call | tf_op jit(solution)/shard_map/spread/pallas_call | solution.py:317
  20.2 4.0 %all-to-all-start = ((bf16[4,1024,256]{2,1,0:T(8,128)(2,1)}), bf16[4,1024,256]{2,1,0:T(8,128)(2,1)S(1)}, u32[]{:S(2)}, u32[]{:S(2)}) async-start(bf16[4,1024,256]{2,1,0:T(8,128)(2,1)} %spread.1), calls=%async_computation | async-start | bytes 4194304 | tf_op jit(solution)/shard_map/all_to_all | solution.py:329
  24.2 4.0 %collective-permute-start.2 = (bf16[256,256]{1,0:T(8,128)(2,1)}, bf16[256,256]{1,0:T(8,128)(2,1)S(1)}, u32[]{:S(2)}, u32[]{:S(2)}) collective-permute-start(bf16[256,256]{1,0:T(8,128)(2,1)} %get-tuple-element.23), channel_id=1, source_target_pairs={{0,16},{8,24},{16,32},{24,40},{32,48},{40,56},{48,64},{56,72},{64,... | collective-permute-start | bytes 393224 | tf_op jit(solution)/shard_map/ppermute | solution.py:305
  28.2 7.0 %collective-permute-start.3 = (bf16[256,256]{1,0:T(8,128)(2,1)}, bf16[256,256]{1,0:T(8,128)(2,1)S(1)}, u32[]{:S(2)}, u32[]{:S(2)}) collective-permute-start(bf16[256,256]{1,0:T(8,128)(2,1)} %get-tuple-element.24), channel_id=1, source_target_pairs={{0,32},{8,40},{16,48},{24,56},{32,64},{40,72},{48,80},{56,88},{64,... | collective-permute-start | bytes 393224 | tf_op jit(solution)/shard_map/ppermute | solution.py:305
  35.3 5.6 %collective-permute-start.4 = (bf16[256,256]{1,0:T(8,128)(2,1)}, bf16[256,256]{1,0:T(8,128)(2,1)S(1)}, u32[]{:S(2)}, u32[]{:S(2)}) collective-permute-start(bf16[256,256]{1,0:T(8,128)(2,1)} %get-tuple-element.25), channel_id=1, source_target_pairs={{0,64},{8,72},{16,80},{24,88},{32,96},{40,104},{48,112},{56,120},{... | collective-permute-start | bytes 393224 | tf_op jit(solution)/shard_map/ppermute | solution.py:305
  40.9 3.9 %collective-permute-start.5 = (bf16[256,256]{1,0:T(8,128)(2,1)S(1)}, bf16[256,256]{1,0:T(8,128)(2,1)S(1)}, u32[]{:S(2)}, u32[]{:S(2)}) collective-permute-start(bf16[256,256]{1,0:T(8,128)(2,1)S(1)} %get-tuple-element.26), channel_id=1, source_target_pairs={{0,128},{8,136},{16,144},{24,152},{32,160},{40,168},{48,176},{56,1... | collective-permute-start | bytes 393224 | tf_op jit(solution)/shard_map/ppermute | solution.py:305
  45.0 1.9 %collective-permute-done.5.refs_4_.f4 = bf16[256,256]{1,0:T(8,128)(2,1)S(1)} collective-permute-done((bf16[256,256]{1,0:T(8,128)(2,1)S(1)}, bf16[256,256]{1,0:T(8,128)(2,1)S(1)}, u32[]{:S(2)}, u32[]{:S(2)}) %collective-permute-start.5) | collective-permute-done | bytes 131104 | tf_op jit(solution)/shard_map/ppermute | solution.py:305
  50.8 8.0 %collective-permute-start.11 = (bf16[1024,256]{1,0:T(8,128)(2,1)S(1)}, bf16[1024,256]{1,0:T(8,128)(2,1)S(1)}, u32[]{:S(2)}, u32[]{:S(2)}) collective-permute-start(bf16[1024,256]{1,0:T(8,128)(2,1)S(1)} %get-tuple-element.39), channel_id=1, source_target_pairs={{0,8},{8,0},{16,24},{24,16},{32,40},{40,32},{48,56},{56,48},{64,72... | collective-permute-start | bytes 1572872 | tf_op jit(solution)/shard_map/ppermute | solution.py:339
  58.8 1.5 %collective-permute-done.11.got_ref = bf16[1024,256]{1,0:T(8,128)(2,1)S(1)} collective-permute-done((bf16[1024,256]{1,0:T(8,128)(2,1)S(1)}, bf16[1024,256]{1,0:T(8,128)(2,1)S(1)}, u32[]{:S(2)}, u32[]{:S(2)}) %collective-permute-start.11) | collective-permute-done | bytes 524320 | tf_op jit(solution)/shard_map/ppermute | solution.py:339
  61.2 13.3 %all-to-all-start.1 = ((bf16[32,32,256]{2,1,0:T(8,128)(2,1)}), bf16[32,32,256]{2,1,0:T(8,128)(2,1)S(1)}, u32[]{:S(2)}, u32[]{:S(2)}) async-start(bf16[32,32,256]{2,1,0:T(8,128)(2,1)} %bitcast), calls=%async_computation.1 | async-start | bytes 1048576 | tf_op jit(solution)/shard_map/all_to_all | solution.py:344
  74.5 7.7 %attend.1 = (bf16[512,256]{1,0:T(8,128)(2,1)}, f32[512,256]{1,0:T(8,128)}, f32[512,256]{1,0:T(8,128)}, bf16[768,256]{1,0:T(8,128)(2,1)}, bf16[256,256]{1,0:T(8,1...) custom-call(bf16[512,256]{1,0:T(8,128)(2,1)} %q_hbm.1, ...), custom_call_target="tpu_custom_call" | custom-call | tf_op jit(solution)/shard_map/attend/pallas_call | solution.py:224
  82.2 2.6 %collective-permute-start.6 = (bf16[768,256]{1,0:T(8,128)(2,1)}, bf16[768,256]{1,0:T(8,128)(2,1)S(1)}, u32[]{:S(2)}, u32[]{:S(2)}) collective-permute-start(bf16[768,256]{1,0:T(8,128)(2,1)} %get-tuple-element.31), channel_id=1, source_target_pairs={{8,0},{16,8},{24,16},{32,24},{40,32},{48,40},{56,48},{64,56},{72,6... | collective-permute-start | bytes 1179656 | tf_op jit(solution)/shard_map/ppermute | solution.py:305
  84.8 1.3 %collective-permute-start.7 = (bf16[256,256]{1,0:T(8,128)(2,1)}, bf16[256,256]{1,0:T(8,128)(2,1)S(1)}, u32[]{:S(2)}, u32[]{:S(2)}) collective-permute-start(bf16[256,256]{1,0:T(8,128)(2,1)} %get-tuple-element.32), channel_id=1, source_target_pairs={{16,0},{24,8},{32,16},{40,24},{48,32},{56,40},{64,48},{72,56},{80,... | collective-permute-start | bytes 393224 | tf_op jit(solution)/shard_map/ppermute | solution.py:305
  86.1 1.3 %collective-permute-start.8 = (bf16[256,256]{1,0:T(8,128)(2,1)}, bf16[256,256]{1,0:T(8,128)(2,1)S(1)}, u32[]{:S(2)}, u32[]{:S(2)}) collective-permute-start(bf16[256,256]{1,0:T(8,128)(2,1)} %get-tuple-element.33), channel_id=1, source_target_pairs={{32,0},{40,8},{48,16},{56,24},{64,32},{72,40},{80,48},{88,56},{96,... | collective-permute-start | bytes 393224 | tf_op jit(solution)/shard_map/ppermute | solution.py:305
  87.4 1.3 %collective-permute-start.9 = (bf16[256,256]{1,0:T(8,128)(2,1)}, bf16[256,256]{1,0:T(8,128)(2,1)S(1)}, u32[]{:S(2)}, u32[]{:S(2)}) collective-permute-start(bf16[256,256]{1,0:T(8,128)(2,1)} %get-tuple-element.34), channel_id=1, source_target_pairs={{64,0},{72,8},{80,16},{88,24},{96,32},{104,40},{112,48},{120,56},{... | collective-permute-start | bytes 393224 | tf_op jit(solution)/shard_map/ppermute | solution.py:305
  88.7 1.3 %collective-permute-start.10 = (bf16[256,256]{1,0:T(8,128)(2,1)}, bf16[256,256]{1,0:T(8,128)(2,1)S(1)}, u32[]{:S(2)}, u32[]{:S(2)}) collective-permute-start(bf16[256,256]{1,0:T(8,128)(2,1)} %get-tuple-element.35), channel_id=1, source_target_pairs={{128,0},{136,8},{144,16},{152,24},{160,32},{168,40},{176,48},{184,... | collective-permute-start | bytes 393224 | tf_op jit(solution)/shard_map/ppermute | solution.py:305
  90.0 2.9 %collective-permute-done.7.f1 = bf16[256,256]{1,0:T(8,128)(2,1)S(1)} collective-permute-done((bf16[256,256]{1,0:T(8,128)(2,1)}, bf16[256,256]{1,0:T(8,128)(2,1)S(1)}, u32[]{:S(2)}, u32[]{:S(2)}) %collective-permute-start.7) | collective-permute-done | bytes 131104 | tf_op jit(solution)/shard_map/ppermute | solution.py:305
  92.9 5.6 %collective-permute-done.8.f2 = bf16[256,256]{1,0:T(8,128)(2,1)S(1)} collective-permute-done((bf16[256,256]{1,0:T(8,128)(2,1)}, bf16[256,256]{1,0:T(8,128)(2,1)S(1)}, u32[]{:S(2)}, u32[]{:S(2)}) %collective-permute-start.8) | collective-permute-done | bytes 131104 | tf_op jit(solution)/shard_map/ppermute | solution.py:305
  98.5 1.6 %collective-permute-done.9.f3 = bf16[256,256]{1,0:T(8,128)(2,1)S(1)} collective-permute-done((bf16[256,256]{1,0:T(8,128)(2,1)}, bf16[256,256]{1,0:T(8,128)(2,1)S(1)}, u32[]{:S(2)}, u32[]{:S(2)}) %collective-permute-start.9) | collective-permute-done | bytes 131104 | tf_op jit(solution)/shard_map/ppermute | solution.py:305
  100.1 7.5 %collective-permute-done.10.f4 = bf16[256,256]{1,0:T(8,128)(2,1)S(1)} collective-permute-done((bf16[256,256]{1,0:T(8,128)(2,1)}, bf16[256,256]{1,0:T(8,128)(2,1)S(1)}, u32[]{:S(2)}, u32[]{:S(2)}) %collective-permute-start.10) | collective-permute-done | bytes 131104 | tf_op jit(solution)/shard_map/ppermute | solution.py:305
  109.6 1.6 %finish.1 = (bf16[512,256]{1,0:T(8,128)(2,1)}, bf16[512,256]{1,0:T(8,128)(2,1)}) custom-call(s32[1,5]{1,0:T(1,128)S(1)} %copy-done.8, f32[512,256]{1,0:T(8,128)S(1)} %copy-done.9, f32[512,256]{1,0:T(8,128)S(1)} %copy-done.10, bf16[768,256]{1,0:T(8,128)(2,1)S(1)} %collective-permute-done.6.near_ref, bf16[256,256]{1,0:T(8,128)(2,1)S(1)} %collective-permute-done.7.f1, ...), custom_call_target="tpu_custom_call" | custom-call | flops 5000000000 | bytes 1048576 | tf_op jit(solution)/shard_map/finish/pallas_call | solution.py:290
  (42 shorter events, 11.1 us)
Async XLA Ops:
  0.6 17.2 %collective-permute-start = (bf16[512,256]{1,0:T(8,128)(2,1)}, bf16[512,256]{1,0:T(8,128)(2,1)S(1)}, u32[]{:S(2)}, u32[]{:S(2)}) collective-permute-start(bf16[512,256]{1,0:T(8,128)(2,1)} %a_ref.1), channel_id=1, source_target_pairs={{0,4},{1,5},{2,6},{3,7},{4,0},{5,1},{6,2},{7,3},{8,12},{9,13},{10,... | collective-permute-start | bytes 786440 | tf_op jit(solution)/shard_map/ppermute | solution.py:333
  8.9 1.0 copy-start
  12.9 33.9 %collective-permute-start.1 = (bf16[768,256]{1,0:T(8,128)(2,1)}, bf16[768,256]{1,0:T(8,128)(2,1)}, u32[]{:S(2)}, u32[]{:S(2)}) collective-permute-start(bf16[768,256]{1,0:T(8,128)(2,1)} %get-tuple-element.22), channel_id=1, source_target_pairs={{0,8},{8,16},{16,24},{24,32},{32,40},{40,48},{48,56},{56,64},{64,7... | collective-permute-start | bytes 1179656 | tf_op jit(solution)/shard_map/ppermute | solution.py:305
  17.8 1.0 copy-start.4
  20.2 27.8 %all-to-all-start = ((bf16[4,1024,256]{2,1,0:T(8,128)(2,1)}), bf16[4,1024,256]{2,1,0:T(8,128)(2,1)S(1)}, u32[]{:S(2)}, u32[]{:S(2)}) async-start(bf16[4,1024,256]{2,1,0:T(8,128)(2,1)} %spread.1), calls=%async_computation | async-start | bytes 4194304 | tf_op jit(solution)/shard_map/all_to_all | solution.py:329
  24.2 20.7 %collective-permute-start.2 = (bf16[256,256]{1,0:T(8,128)(2,1)}, bf16[256,256]{1,0:T(8,128)(2,1)S(1)}, u32[]{:S(2)}, u32[]{:S(2)}) collective-permute-start(bf16[256,256]{1,0:T(8,128)(2,1)} %get-tuple-element.23), channel_id=1, source_target_pairs={{0,16},{8,24},{16,32},{24,40},{32,48},{40,56},{48,64},{56,72},{64,... | collective-permute-start | bytes 393224 | tf_op jit(solution)/shard_map/ppermute | solution.py:305
  28.2 16.7 %collective-permute-start.3 = (bf16[256,256]{1,0:T(8,128)(2,1)}, bf16[256,256]{1,0:T(8,128)(2,1)S(1)}, u32[]{:S(2)}, u32[]{:S(2)}) collective-permute-start(bf16[256,256]{1,0:T(8,128)(2,1)} %get-tuple-element.24), channel_id=1, source_target_pairs={{0,32},{8,40},{16,48},{24,56},{32,64},{40,72},{48,80},{56,88},{64,... | collective-permute-start | bytes 393224 | tf_op jit(solution)/shard_map/ppermute | solution.py:305
  35.3 9.7 %collective-permute-start.4 = (bf16[256,256]{1,0:T(8,128)(2,1)}, bf16[256,256]{1,0:T(8,128)(2,1)S(1)}, u32[]{:S(2)}, u32[]{:S(2)}) collective-permute-start(bf16[256,256]{1,0:T(8,128)(2,1)} %get-tuple-element.25), channel_id=1, source_target_pairs={{0,64},{8,72},{16,80},{24,88},{32,96},{40,104},{48,112},{56,120},{... | collective-permute-start | bytes 393224 | tf_op jit(solution)/shard_map/ppermute | solution.py:305
  40.9 7.2 %copy-start.2 = (bf16[2048,256]{1,0:T(8,128)(2,1)S(1)}, bf16[2048,256]{1,0:T(8,128)(2,1)}, u32[]{:S(2)}) copy-start(bf16[2048,256]{1,0:T(8,128)(2,1)} %refs_1_.1) | copy-start | bytes 3145732
  40.9 7.1 %copy-start.3 = (bf16[512,256]{1,0:T(8,128)(2,1)S(1)}, bf16[512,256]{1,0:T(8,128)(2,1)}, u32[]{:S(2)}) copy-start(bf16[512,256]{1,0:T(8,128)(2,1)} %o_hbm.1) | copy-start | bytes 786436
  40.9 5.9 %collective-permute-start.5 = (bf16[256,256]{1,0:T(8,128)(2,1)S(1)}, bf16[256,256]{1,0:T(8,128)(2,1)S(1)}, u32[]{:S(2)}, u32[]{:S(2)}) collective-permute-start(bf16[256,256]{1,0:T(8,128)(2,1)S(1)} %get-tuple-element.26), channel_id=1, source_target_pairs={{0,128},{8,136},{16,144},{24,152},{32,160},{40,168},{48,176},{56,1... | collective-permute-start | bytes 393224 | tf_op jit(solution)/shard_map/ppermute | solution.py:305
  44.9 1.9 %copy-start.11 = (bf16[256,256]{1,0:T(8,128)(2,1)}, bf16[256,256]{1,0:T(8,128)(2,1)S(1)}, u32[]{:S(2)}) copy-start(bf16[256,256]{1,0:T(8,128)(2,1)S(1)} %collective-permute-done.2.refs_1_.f1) | copy-start | bytes 393220
  44.9 1.9 %copy-start.12 = (bf16[256,256]{1,0:T(8,128)(2,1)}, bf16[256,256]{1,0:T(8,128)(2,1)S(1)}, u32[]{:S(2)}) copy-start(bf16[256,256]{1,0:T(8,128)(2,1)S(1)} %collective-permute-done.3.refs_2_.f2) | copy-start | bytes 393220
  45.0 1.9 %copy-start.13 = (bf16[256,256]{1,0:T(8,128)(2,1)}, bf16[256,256]{1,0:T(8,128)(2,1)S(1)}, u32[]{:S(2)}) copy-start(bf16[256,256]{1,0:T(8,128)(2,1)S(1)} %collective-permute-done.4.refs_3_.f3) | copy-start | bytes 393220
  50.8 9.5 %collective-permute-start.11 = (bf16[1024,256]{1,0:T(8,128)(2,1)S(1)}, bf16[1024,256]{1,0:T(8,128)(2,1)S(1)}, u32[]{:S(2)}, u32[]{:S(2)}) collective-permute-start(bf16[1024,256]{1,0:T(8,128)(2,1)S(1)} %get-tuple-element.39), channel_id=1, source_target_pairs={{0,8},{8,0},{16,24},{24,16},{32,40},{40,32},{48,56},{56,48},{64,72... | collective-permute-start | bytes 1572872 | tf_op jit(solution)/shard_map/ppermute | solution.py:339
  60.3 47.2 %copy-start.8 = (s32[1,5]{1,0:T(1,128)S(1)}, s32[1,5]{1,0:T(1,128)}, u32[]{:S(2)}) copy-start(s32[1,5]{1,0:T(1,128)} %pick.3) | copy-start | bytes 64
  61.2 50.0 %all-to-all-start.1 = ((bf16[32,32,256]{2,1,0:T(8,128)(2,1)}), bf16[32,32,256]{2,1,0:T(8,128)(2,1)S(1)}, u32[]{:S(2)}, u32[]{:S(2)}) async-start(bf16[32,32,256]{2,1,0:T(8,128)(2,1)} %bitcast), calls=%async_computation.1 | async-start | bytes 1048576 | tf_op jit(solution)/shard_map/all_to_all | solution.py:344
  82.2 25.3 %collective-permute-start.6 = (bf16[768,256]{1,0:T(8,128)(2,1)}, bf16[768,256]{1,0:T(8,128)(2,1)S(1)}, u32[]{:S(2)}, u32[]{:S(2)}) collective-permute-start(bf16[768,256]{1,0:T(8,128)(2,1)} %get-tuple-element.31), channel_id=1, source_target_pairs={{8,0},{16,8},{24,16},{32,24},{40,32},{48,40},{56,48},{64,56},{72,6... | collective-permute-start | bytes 1179656 | tf_op jit(solution)/shard_map/ppermute | solution.py:305
  84.8 8.1 %collective-permute-start.7 = (bf16[256,256]{1,0:T(8,128)(2,1)}, bf16[256,256]{1,0:T(8,128)(2,1)S(1)}, u32[]{:S(2)}, u32[]{:S(2)}) collective-permute-start(bf16[256,256]{1,0:T(8,128)(2,1)} %get-tuple-element.32), channel_id=1, source_target_pairs={{16,0},{24,8},{32,16},{40,24},{48,32},{56,40},{64,48},{72,56},{80,... | collective-permute-start | bytes 393224 | tf_op jit(solution)/shard_map/ppermute | solution.py:305
  86.1 12.4 %collective-permute-start.8 = (bf16[256,256]{1,0:T(8,128)(2,1)}, bf16[256,256]{1,0:T(8,128)(2,1)S(1)}, u32[]{:S(2)}, u32[]{:S(2)}) collective-permute-start(bf16[256,256]{1,0:T(8,128)(2,1)} %get-tuple-element.33), channel_id=1, source_target_pairs={{32,0},{40,8},{48,16},{56,24},{64,32},{72,40},{80,48},{88,56},{96,... | collective-permute-start | bytes 393224 | tf_op jit(solution)/shard_map/ppermute | solution.py:305
  87.4 12.7 %collective-permute-start.9 = (bf16[256,256]{1,0:T(8,128)(2,1)}, bf16[256,256]{1,0:T(8,128)(2,1)S(1)}, u32[]{:S(2)}, u32[]{:S(2)}) collective-permute-start(bf16[256,256]{1,0:T(8,128)(2,1)} %get-tuple-element.34), channel_id=1, source_target_pairs={{64,0},{72,8},{80,16},{88,24},{96,32},{104,40},{112,48},{120,56},{... | collective-permute-start | bytes 393224 | tf_op jit(solution)/shard_map/ppermute | solution.py:305
  88.7 18.8 %collective-permute-start.10 = (bf16[256,256]{1,0:T(8,128)(2,1)}, bf16[256,256]{1,0:T(8,128)(2,1)S(1)}, u32[]{:S(2)}, u32[]{:S(2)}) collective-permute-start(bf16[256,256]{1,0:T(8,128)(2,1)} %get-tuple-element.35), channel_id=1, source_target_pairs={{128,0},{136,8},{144,16},{152,24},{160,32},{168,40},{176,48},{184,... | collective-permute-start | bytes 393224 | tf_op jit(solution)/shard_map/ppermute | solution.py:305
  107.5 1.0 copy-start.9
  108.6 1.0 copy-start.10
  (5 other events, 3.7 us)

commit v4 on v3

--- a/solution.py
+++ b/solution.py
@@ -9,7 +9,8 @@
 WIN = 256
 BLK = 128
 LEVELS = 5
-GATE_MIB = 60
+FINISH_MIB = 16
+GATE_MIB = 16
 ATTEND_MIB = 60
 BF = jnp.bfloat16
 F32 = jnp.float32
@@ -130,10 +131,11 @@
 
 def attend_kernel(
     q_hbm, k_hbm, v_hbm, o_hbm, do_hbm, near_hbm, f1, f2, f3, f4,
-    dq_ref, own_k, own_v, back_near, b1, b2, b3, b4, token,
+    dq_ref, own_ref, back_near, b1, b2, b3, b4, token,
     q_ref, k_ref, v_ref, o_ref, do_ref, near_ref, f_ref, fk, fv, sems,
 ):
     token[...] = jnp.zeros((8, 128), F32)
+    own_k, own_v = own_ref.at[0:512], own_ref.at[512:1024]
     pairs = [(q_hbm, q_ref), (k_hbm, k_ref), (near_hbm, near_ref)]
     pairs += [(f, f_ref.at[i]) for i, f in enumerate((f1, f2, f3, f4))]
     pairs += [(v_hbm, v_ref), (do_hbm, do_ref), (o_hbm, o_ref)]
@@ -218,18 +220,18 @@
 
 
 def attend(queries, keys, values, outputs, d_out, got):
-    f32s = jax.ShapeDtypeStruct((512, 256), F32)
+    own = jax.ShapeDtypeStruct((1024, 256), F32)
     far = jax.ShapeDtypeStruct((2 * BLK, 256), BF)
     here = pltpu.VMEM((512, 256), BF)
     return pl.pallas_call(
         attend_kernel,
         out_shape=[
-            jax.ShapeDtypeStruct((512, 256), BF), f32s, f32s,
+            jax.ShapeDtypeStruct((512, 256), BF), own,
             jax.ShapeDtypeStruct((2 * WIN + 2 * BLK, 256), BF), far, far, far, far,
             jax.ShapeDtypeStruct((8, 128), F32),
         ],
         in_specs=[ANY] * 10,
-        out_specs=[VMEM] * 9,
+        out_specs=[VMEM] * 8,
         scratch_shapes=[
             here, here, here, here, here,
             pltpu.VMEM((2 * WIN + 2 * BLK, 256), BF),
@@ -273,32 +275,33 @@
     )(part)
 
 
-def finish_kernel(pick, own_k, own_v, near_ref, f1, f2, f3, f4, dk_ref, dv_ref, tk, tv):
-    for ref, acc, at in ((own_k, tk, 0), (own_v, tv, 1)):
-        acc[0:256, :] = ref[0:256, :]
-        acc[256:512, :] = ref[256:512, :] + near_ref[at * WIN : (at + 1) * WIN, :].astype(F32)
+def finish_kernel(pick, own_ref, near_ref, f3, f2, f4, f1, dk_ref, dv_ref, acc):
+    for at, out_ref in ((0, dk_ref), (1, dv_ref)):
+        acc[0:256, :] = own_ref[at * 512 : at * 512 + 256, :]
+        acc[256:512, :] = own_ref[at * 512 + 256 : at * 512 + 512, :] + near_ref[
+            at * WIN : (at + 1) * WIN, :
+        ].astype(F32)
         for level, far in enumerate((near_ref, f1, f2, f3, f4)):
             low = (2 * WIN if level == 0 else 0) + at * BLK
             rows = pl.ds(pl.multiple_of(pick[0, level] * BLK, BLK), BLK)
             acc[rows, :] += far[low : low + BLK, :].astype(F32)
-    dk_ref[...] = tk[...].astype(BF)
-    dv_ref[...] = tv[...].astype(BF)
-
-
-def finish(pick, own_k, own_v, got):
+        out_ref[...] = acc[...].astype(BF)
+
+
+def finish(pick, own, got):
     out = jax.ShapeDtypeStruct((512, 256), BF)
     return pl.pallas_call(
         finish_kernel,
         out_shape=[out, out],
-        in_specs=[SMEM] + [VMEM] * 7,
+        in_specs=[SMEM] + [VMEM] * 6,
         out_specs=[VMEM] * 2,
-        scratch_shapes=[pltpu.VMEM((512, 256), F32)] * 2,
-        compiler_params=params(),
+        scratch_shapes=[pltpu.VMEM((512, 256), F32)],
+        compiler_params=params(FINISH_MIB),
         cost_estimate=pl.CostEstimate(
             flops=5000000000, bytes_accessed=2**20, transcendentals=0
         ),
         name="finish",
-    )(pick, own_k, own_v, *got)
+    )(pick, own, got[0], got[3], got[2], got[4], got[1])
 
 
 def shift(block, distance):
@@ -334,16 +337,16 @@
     packed = pack(block_pick, keys, values)
     got = [shift(b, 2**level) for level, b in enumerate(packed)]
     pieces = [to_row(spread(out_cotangent, other))]
-    ready = gate(got[0], got[1], got[2], got[3], got[4])
+    ready = gate(got[0], got[3], got[2], got[4], got[1])
     d_out, keep, send = project(pieces, out_weight, outputs, ready)
     received = lax.ppermute(send, "tm", [(i, i ^ 1) for i in range(64)])
-    dq, own_k, own_v, *back, token = attend(queries, keys, values, outputs, d_out, got)
+    dq, own, *back, token = attend(queries, keys, values, outputs, d_out, got)
     back = [shift(b, -(2**level)) for level, b in enumerate(back)]
     half = add(keep, received).reshape(NYL * NZ, 32, 256)
     groups = [[2 * i + c for i in range(NYL * NZ)] for c in range(2)]
     part = lax.all_to_all(half, "tm", 0, 0, axis_index_groups=groups)
     weight_grad = total(part)
-    dk, dv = finish(block_pick, own_k, own_v, back)
+    dk, dv = finish(block_pick, own, back)
     return dq, dk, dv, weight_grad
 
 

time: 114 us -> 112 us (0.982)
  the two profiles are of different devices: /device:TPU:1 before, /device:TPU:16 now
where the time goes in v4:
time: 112 us; the launch traced here: 111 us
  starting transfers between devices  63.2 us (56%)
  waiting for transfers between devices  23.8 us (21%)
  Pallas kernels  15.2 us (14%)
  local copies, waits for them, and re-layouts  8.02 us (7%)
    ppermute x10, starting transfers between devices, shift(): lax.ppermute(block, 'tm', [(i, i + distance) for i in range(64) if 0 <= i...  39.8 us
    ppermute x10, waiting for transfers between devices, shift(): lax.ppermute(block, 'tm', [(i, i + distance) for i in range(64) if 0 <= i...  15.8 us
    all_to_all x1, starting transfers between devices, on_device(): part = lax.all_to_all(half, 'tm', 0, 0, axis_index_groups=groups)  10.1 us
    unnamed x28, local copies, waits for them, and re-layouts  8.02 us
    pallas_call x1, Pallas kernels, attend(): pl.pallas_call(attend_kernel, out_shape=[jax.ShapeDtypeStruct((512, 256),...  7.87 us
    ppermute x1, waiting for transfers between devices, on_device(): lax.ppermute(out_cotangent, 'head', [(h, (h + NX) % (2 * NX)) for h in ra...  6.12 us
    ppermute x1, starting transfers between devices, on_device(): lax.ppermute(out_cotangent, 'head', [(h, (h + NX) % (2 * NX)) for h in ra...  5.94 us
    all_to_all x1, starting transfers between devices, to_row(): return lax.all_to_all(blocks, 'head', 0, 0, axis_index_groups=rows)  5.44 us
  transfers between devices with their start and end apart: 14, of which 6 were waited for; matrix products, arithmetic and copies ran while one was open for 0% of the time, Pallas kernels for 11%

profile of v4, /device:TPU:16, one launch (start us, length us, event | category | flops | bytes accessed | tf_op | source)
XLA Modules:
  0.0 111.0 jit_solution(15875808016903708814)
XLA Ops:
  0.6 5.9 %collective-permute-start = (bf16[512,256]{1,0:T(8,128)(2,1)}, bf16[512,256]{1,0:T(8,128)(2,1)S(1)}, u32[]{:S(2)}, u32[]{:S(2)}) collective-permute-start(bf16[512,256]{1,0:T(8,128)(2,1)} %a_ref.1), channel_id=1, source_target_pairs={{0,4},{1,5},{2,6},{3,7},{4,0},{5,1},{6,2},{7,3},{8,12},{9,13},{10,... | collective-permute-start | bytes 786440 | tf_op jit(solution)/shard_map/ppermute | solution.py:336
  9.1 1.5 %pack.1 = (bf16[768,256]{1,0:T(8,128)(2,1)}, bf16[256,256]{1,0:T(8,128)(2,1)S(1)}, bf16[256,256]{1,0:T(8,128)(2,1)}, bf16[256,256]{1,0:T(8,128)(2,1)}, bf16[256,256]{1,0:T(8,128)(2,1)}) custom-call(s32[1,5]{1,0:T(1,128)S(1)} %copy-done.10, bf16[512,256]{1,0:T(8,128)(2,1)S(1)} %copy-done, bf16[512,256]{1,0:T(8,128)(2,1)S(1)} %copy-done.1), custom_call_target="tpu_custom_call" | custom-call | tf_op jit(solution)/shard_map/pack/pallas_call | solution.py:43
  11.2 1.9 %collective-permute-start.1 = (bf16[768,256]{1,0:T(8,128)(2,1)}, bf16[768,256]{1,0:T(8,128)(2,1)}, u32[]{:S(2)}, u32[]{:S(2)}) collective-permute-start(bf16[768,256]{1,0:T(8,128)(2,1)} %get-tuple-element.21), channel_id=1, source_target_pairs={{0,8},{8,16},{16,24},{24,32},{32,40},{40,48},{48,56},{56,64},{64,7... | collective-permute-start | bytes 1179656 | tf_op jit(solution)/shard_map/ppermute | solution.py:308
  13.2 6.1 %collective-permute-done.b_ref = bf16[512,256]{1,0:T(8,128)(2,1)S(1)} collective-permute-done((bf16[512,256]{1,0:T(8,128)(2,1)}, bf16[512,256]{1,0:T(8,128)(2,1)S(1)}, u32[]{:S(2)}, u32[]{:S(2)}) %collective-permute-start) | collective-permute-done | bytes 262176 | tf_op jit(solution)/shard_map/ppermute | solution.py:336
  20.2 1.5 %spread.1 = bf16[4,1024,256]{2,1,0:T(8,128)(2,1)} custom-call(bf16[512,256]{1,0:T(8,128)(2,1)S(1)} %copy-done.4, bf16[512,256]{1,0:T(8,128)(2,1)S(1)} %collective-permute-done.b_ref), custom_call_target="tpu_custom_call" | custom-call | tf_op jit(solution)/shard_map/spread/pallas_call | solution.py:320
  21.7 5.4 %all-to-all-start = ((bf16[4,1024,256]{2,1,0:T(8,128)(2,1)}), bf16[4,1024,256]{2,1,0:T(8,128)(2,1)S(1)}, u32[]{:S(2)}, u32[]{:S(2)}) async-start(bf16[4,1024,256]{2,1,0:T(8,128)(2,1)} %spread.1), calls=%async_computation | async-start | bytes 4194304 | tf_op jit(solution)/shard_map/all_to_all | solution.py:332
  27.1 10.9 %collective-permute-start.2 = (bf16[256,256]{1,0:T(8,128)(2,1)}, bf16[256,256]{1,0:T(8,128)(2,1)S(1)}, u32[]{:S(2)}, u32[]{:S(2)}) collective-permute-start(bf16[256,256]{1,0:T(8,128)(2,1)} %get-tuple-element.22), channel_id=1, source_target_pairs={{0,64},{8,72},{16,80},{24,88},{32,96},{40,104},{48,112},{56,120},{... | collective-permute-start | bytes 393224 | tf_op jit(solution)/shard_map/ppermute | solution.py:308
  38.1 4.3 %collective-permute-start.3 = (bf16[256,256]{1,0:T(8,128)(2,1)}, bf16[256,256]{1,0:T(8,128)(2,1)S(1)}, u32[]{:S(2)}, u32[]{:S(2)}) collective-permute-start(bf16[256,256]{1,0:T(8,128)(2,1)} %get-tuple-element.23), channel_id=1, source_target_pairs={{0,32},{8,40},{16,48},{24,56},{32,64},{40,72},{48,80},{56,88},{64,... | collective-permute-start | bytes 393224 | tf_op jit(solution)/shard_map/ppermute | solution.py:308
  42.4 2.6 %collective-permute-start.4 = (bf16[256,256]{1,0:T(8,128)(2,1)}, bf16[256,256]{1,0:T(8,128)(2,1)S(1)}, u32[]{:S(2)}, u32[]{:S(2)}) collective-permute-start(bf16[256,256]{1,0:T(8,128)(2,1)} %get-tuple-element.24), channel_id=1, source_target_pairs={{0,128},{8,136},{16,144},{24,152},{32,160},{40,168},{48,176},{56,1... | collective-permute-start | bytes 393224 | tf_op jit(solution)/shard_map/ppermute | solution.py:308
  45.0 3.5 %collective-permute-start.5 = (bf16[256,256]{1,0:T(8,128)(2,1)}, bf16[256,256]{1,0:T(8,128)(2,1)S(1)}, u32[]{:S(2)}, u32[]{:S(2)}) collective-permute-start(bf16[256,256]{1,0:T(8,128)(2,1)} %copy-done.13), channel_id=1, source_target_pairs={{0,16},{8,24},{16,32},{24,40},{32,48},{40,56},{48,64},{56,72},{64,... | collective-permute-start | bytes 393224 | tf_op jit(solution)/shard_map/ppermute | solution.py:308
  48.5 2.1 %collective-permute-done.3.refs_2_.f2 = bf16[256,256]{1,0:T(8,128)(2,1)S(1)} collective-permute-done((bf16[256,256]{1,0:T(8,128)(2,1)}, bf16[256,256]{1,0:T(8,128)(2,1)S(1)}, u32[]{:S(2)}, u32[]{:S(2)}) %collective-permute-start.3) | collective-permute-done | bytes 131104 | tf_op jit(solution)/shard_map/ppermute | solution.py:308
  50.6 3.7 %collective-permute-done.5.refs_4_.f1 = bf16[256,256]{1,0:T(8,128)(2,1)S(1)} collective-permute-done((bf16[256,256]{1,0:T(8,128)(2,1)}, bf16[256,256]{1,0:T(8,128)(2,1)S(1)}, u32[]{:S(2)}, u32[]{:S(2)}) %collective-permute-start.5) | collective-permute-done | bytes 131104 | tf_op jit(solution)/shard_map/ppermute | solution.py:308
  58.3 1.9 %collective-permute-start.11 = (bf16[1024,256]{1,0:T(8,128)(2,1)S(1)}, bf16[1024,256]{1,0:T(8,128)(2,1)S(1)}, u32[]{:S(2)}, u32[]{:S(2)}) collective-permute-start(bf16[1024,256]{1,0:T(8,128)(2,1)S(1)} %get-tuple-element.37), channel_id=1, source_target_pairs={{0,8},{8,0},{16,24},{24,16},{32,40},{40,32},{48,56},{56,48},{64,72... | collective-permute-start | bytes 1572872 | tf_op jit(solution)/shard_map/ppermute | solution.py:342
  60.2 1.9 %collective-permute-done.11.got_ref = bf16[1024,256]{1,0:T(8,128)(2,1)S(1)} collective-permute-done((bf16[1024,256]{1,0:T(8,128)(2,1)S(1)}, bf16[1024,256]{1,0:T(8,128)(2,1)S(1)}, u32[]{:S(2)}, u32[]{:S(2)}) %collective-permute-start.11) | collective-permute-done | bytes 524320 | tf_op jit(solution)/shard_map/ppermute | solution.py:342
  63.0 10.1 %all-to-all-start.1 = ((bf16[32,32,256]{2,1,0:T(8,128)(2,1)}), bf16[32,32,256]{2,1,0:T(8,128)(2,1)S(1)}, u32[]{:S(2)}, u32[]{:S(2)}) async-start(bf16[32,32,256]{2,1,0:T(8,128)(2,1)} %bitcast), calls=%async_computation.1 | async-start | bytes 1048576 | tf_op jit(solution)/shard_map/all_to_all | solution.py:347
  73.1 7.9 %attend.1 = (bf16[512,256]{1,0:T(8,128)(2,1)}, f32[1024,256]{1,0:T(8,128)}, bf16[768,256]{1,0:T(8,128)(2,1)}, bf16[256,256]{1,0:T(8,128)(2,1)}, bf16[256,256]{1,...) custom-call(bf16[512,256]{1,0:T(8,128)(2,1)} %q_hbm.1, ...), custom_call_target="tpu_custom_call" | custom-call | tf_op jit(solution)/shard_map/attend/pallas_call | solution.py:226
  81.0 3.8 %collective-permute-start.6 = (bf16[768,256]{1,0:T(8,128)(2,1)}, bf16[768,256]{1,0:T(8,128)(2,1)S(1)}, u32[]{:S(2)}, u32[]{:S(2)}) collective-permute-start(bf16[768,256]{1,0:T(8,128)(2,1)} %get-tuple-element.29), channel_id=1, source_target_pairs={{8,0},{16,8},{24,16},{32,24},{40,32},{48,40},{56,48},{64,56},{72,6... | collective-permute-start | bytes 1179656 | tf_op jit(solution)/shard_map/ppermute | solution.py:308
  84.7 5.4 %collective-permute-start.7 = (bf16[256,256]{1,0:T(8,128)(2,1)}, bf16[256,256]{1,0:T(8,128)(2,1)S(1)}, u32[]{:S(2)}, u32[]{:S(2)}) collective-permute-start(bf16[256,256]{1,0:T(8,128)(2,1)} %get-tuple-element.30), channel_id=1, source_target_pairs={{64,0},{72,8},{80,16},{88,24},{96,32},{104,40},{112,48},{120,56},{... | collective-permute-start | bytes 393224 | tf_op jit(solution)/shard_map/ppermute | solution.py:308
  90.2 2.5 %collective-permute-start.8 = (bf16[256,256]{1,0:T(8,128)(2,1)}, bf16[256,256]{1,0:T(8,128)(2,1)S(1)}, u32[]{:S(2)}, u32[]{:S(2)}) collective-permute-start(bf16[256,256]{1,0:T(8,128)(2,1)} %get-tuple-element.31), channel_id=1, source_target_pairs={{32,0},{40,8},{48,16},{56,24},{64,32},{72,40},{80,48},{88,56},{96,... | collective-permute-start | bytes 393224 | tf_op jit(solution)/shard_map/ppermute | solution.py:308
  92.6 2.5 %collective-permute-start.9 = (bf16[256,256]{1,0:T(8,128)(2,1)}, bf16[256,256]{1,0:T(8,128)(2,1)S(1)}, u32[]{:S(2)}, u32[]{:S(2)}) collective-permute-start(bf16[256,256]{1,0:T(8,128)(2,1)} %get-tuple-element.32), channel_id=1, source_target_pairs={{128,0},{136,8},{144,16},{152,24},{160,32},{168,40},{176,48},{184,... | collective-permute-start | bytes 393224 | tf_op jit(solution)/shard_map/ppermute | solution.py:308
  95.1 2.5 %collective-permute-start.10 = (bf16[256,256]{1,0:T(8,128)(2,1)}, bf16[256,256]{1,0:T(8,128)(2,1)S(1)}, u32[]{:S(2)}, u32[]{:S(2)}) collective-permute-start(bf16[256,256]{1,0:T(8,128)(2,1)} %get-tuple-element.33), channel_id=1, source_target_pairs={{16,0},{24,8},{32,16},{40,24},{48,32},{56,40},{64,48},{72,56},{80,... | collective-permute-start | bytes 393224 | tf_op jit(solution)/shard_map/ppermute | solution.py:308
  97.6 8.1 %collective-permute-done.8.f2 = bf16[256,256]{1,0:T(8,128)(2,1)S(1)} collective-permute-done((bf16[256,256]{1,0:T(8,128)(2,1)}, bf16[256,256]{1,0:T(8,128)(2,1)S(1)}, u32[]{:S(2)}, u32[]{:S(2)}) %collective-permute-start.8) | collective-permute-done | bytes 131104 | tf_op jit(solution)/shard_map/ppermute | solution.py:308
  105.7 1.9 %collective-permute-done.10.f1 = bf16[256,256]{1,0:T(8,128)(2,1)S(1)} collective-permute-done((bf16[256,256]{1,0:T(8,128)(2,1)}, bf16[256,256]{1,0:T(8,128)(2,1)S(1)}, u32[]{:S(2)}, u32[]{:S(2)}) %collective-permute-start.10) | collective-permute-done | bytes 131104 | tf_op jit(solution)/shard_map/ppermute | solution.py:308
  108.8 1.5 %finish.1 = (bf16[512,256]{1,0:T(8,128)(2,1)}, bf16[512,256]{1,0:T(8,128)(2,1)}) custom-call(s32[1,5]{1,0:T(1,128)S(1)} %copy-done.11, f32[1024,256]{1,0:T(8,128)S(1)} %copy-done.12, bf16[768,256]{1,0:T(8,128)(2,1)S(1)} %collective-permute-done.6.near_ref, bf16[256,256]{1,0:T(8,128)(2,1)S(1)} %collective-permute-done.7.f3, ...), custom_call_target="tpu_custom_call" | custom-call | flops 5000000000 | bytes 1048576 | tf_op jit(solution)/shard_map/finish/pallas_call | solution.py:293
  (40 shorter events, 11.0 us)
Async XLA Ops:
  0.6 18.6 %collective-permute-start = (bf16[512,256]{1,0:T(8,128)(2,1)}, bf16[512,256]{1,0:T(8,128)(2,1)S(1)}, u32[]{:S(2)}, u32[]{:S(2)}) collective-permute-start(bf16[512,256]{1,0:T(8,128)(2,1)} %a_ref.1), channel_id=1, source_target_pairs={{0,4},{1,5},{2,6},{3,7},{4,0},{5,1},{6,2},{7,3},{8,12},{9,13},{10,... | collective-permute-start | bytes 786440 | tf_op jit(solution)/shard_map/ppermute | solution.py:336
  6.6 1.0 copy-start
  7.5 0.9 copy-start.1
  8.5 0.7 copy-start.10
  11.2 43.1 %collective-permute-start.1 = (bf16[768,256]{1,0:T(8,128)(2,1)}, bf16[768,256]{1,0:T(8,128)(2,1)}, u32[]{:S(2)}, u32[]{:S(2)}) collective-permute-start(bf16[768,256]{1,0:T(8,128)(2,1)} %get-tuple-element.21), channel_id=1, source_target_pairs={{0,8},{8,16},{16,24},{24,32},{32,40},{40,48},{48,56},{56,64},{64,7... | collective-permute-start | bytes 1179656 | tf_op jit(solution)/shard_map/ppermute | solution.py:308
  19.3 1.0 copy-start.4
  21.7 34.6 %all-to-all-start = ((bf16[4,1024,256]{2,1,0:T(8,128)(2,1)}), bf16[4,1024,256]{2,1,0:T(8,128)(2,1)S(1)}, u32[]{:S(2)}, u32[]{:S(2)}) async-start(bf16[4,1024,256]{2,1,0:T(8,128)(2,1)} %spread.1), calls=%async_computation | async-start | bytes 4194304 | tf_op jit(solution)/shard_map/all_to_all | solution.py:332
  27.1 21.4 %collective-permute-start.2 = (bf16[256,256]{1,0:T(8,128)(2,1)}, bf16[256,256]{1,0:T(8,128)(2,1)S(1)}, u32[]{:S(2)}, u32[]{:S(2)}) collective-permute-start(bf16[256,256]{1,0:T(8,128)(2,1)} %get-tuple-element.22), channel_id=1, source_target_pairs={{0,64},{8,72},{16,80},{24,88},{32,96},{40,104},{48,112},{56,120},{... | collective-permute-start | bytes 393224 | tf_op jit(solution)/shard_map/ppermute | solution.py:308
  38.1 12.6 %collective-permute-start.3 = (bf16[256,256]{1,0:T(8,128)(2,1)}, bf16[256,256]{1,0:T(8,128)(2,1)S(1)}, u32[]{:S(2)}, u32[]{:S(2)}) collective-permute-start(bf16[256,256]{1,0:T(8,128)(2,1)} %get-tuple-element.23), channel_id=1, source_target_pairs={{0,32},{8,40},{16,48},{24,56},{32,64},{40,72},{48,80},{56,88},{64,... | collective-permute-start | bytes 393224 | tf_op jit(solution)/shard_map/ppermute | solution.py:308
  42.4 8.3 %collective-permute-start.4 = (bf16[256,256]{1,0:T(8,128)(2,1)}, bf16[256,256]{1,0:T(8,128)(2,1)S(1)}, u32[]{:S(2)}, u32[]{:S(2)}) collective-permute-start(bf16[256,256]{1,0:T(8,128)(2,1)} %get-tuple-element.24), channel_id=1, source_target_pairs={{0,128},{8,136},{16,144},{24,152},{32,160},{40,168},{48,176},{56,1... | collective-permute-start | bytes 393224 | tf_op jit(solution)/shard_map/ppermute | solution.py:308
  45.0 11.3 %copy-start.2 = (bf16[2048,256]{1,0:T(8,128)(2,1)S(1)}, bf16[2048,256]{1,0:T(8,128)(2,1)}, u32[]{:S(2)}) copy-start(bf16[2048,256]{1,0:T(8,128)(2,1)} %refs_1_.1) | copy-start | bytes 3145732
  45.0 11.3 %copy-start.3 = (bf16[512,256]{1,0:T(8,128)(2,1)S(1)}, bf16[512,256]{1,0:T(8,128)(2,1)}, u32[]{:S(2)}) copy-start(bf16[512,256]{1,0:T(8,128)(2,1)} %o_hbm.1) | copy-start | bytes 786436
  45.0 9.3 %collective-permute-start.5 = (bf16[256,256]{1,0:T(8,128)(2,1)}, bf16[256,256]{1,0:T(8,128)(2,1)S(1)}, u32[]{:S(2)}, u32[]{:S(2)}) collective-permute-start(bf16[256,256]{1,0:T(8,128)(2,1)} %copy-done.13), channel_id=1, source_target_pairs={{0,16},{8,24},{16,32},{24,40},{32,48},{40,56},{48,64},{56,72},{64,... | collective-permute-start | bytes 393224 | tf_op jit(solution)/shard_map/ppermute | solution.py:308
  48.5 5.8 %copy-start.6 = (bf16[256,256]{1,0:T(8,128)(2,1)}, bf16[256,256]{1,0:T(8,128)(2,1)S(1)}, u32[]{:S(2)}) copy-start(bf16[256,256]{1,0:T(8,128)(2,1)S(1)} %collective-permute-done.2.refs_1_.f3) | copy-start | bytes 393220
  57.6 0.7 copy-start.5
  58.3 3.8 %collective-permute-start.11 = (bf16[1024,256]{1,0:T(8,128)(2,1)S(1)}, bf16[1024,256]{1,0:T(8,128)(2,1)S(1)}, u32[]{:S(2)}, u32[]{:S(2)}) collective-permute-start(bf16[1024,256]{1,0:T(8,128)(2,1)S(1)} %get-tuple-element.37), channel_id=1, source_target_pairs={{0,8},{8,0},{16,24},{24,16},{32,40},{40,32},{48,56},{56,48},{64,72... | collective-permute-start | bytes 1572872 | tf_op jit(solution)/shard_map/ppermute | solution.py:342
  62.1 45.5 %copy-start.11 = (s32[1,5]{1,0:T(1,128)S(1)}, s32[1,5]{1,0:T(1,128)}, u32[]{:S(2)}) copy-start(s32[1,5]{1,0:T(1,128)} %pick.3) | copy-start | bytes 64
  63.0 47.3 %all-to-all-start.1 = ((bf16[32,32,256]{2,1,0:T(8,128)(2,1)}), bf16[32,32,256]{2,1,0:T(8,128)(2,1)S(1)}, u32[]{:S(2)}, u32[]{:S(2)}) async-start(bf16[32,32,256]{2,1,0:T(8,128)(2,1)} %bitcast), calls=%async_computation.1 | async-start | bytes 1048576 | tf_op jit(solution)/shard_map/all_to_all | solution.py:347
  81.0 26.6 %collective-permute-start.6 = (bf16[768,256]{1,0:T(8,128)(2,1)}, bf16[768,256]{1,0:T(8,128)(2,1)S(1)}, u32[]{:S(2)}, u32[]{:S(2)}) collective-permute-start(bf16[768,256]{1,0:T(8,128)(2,1)} %get-tuple-element.29), channel_id=1, source_target_pairs={{8,0},{16,8},{24,16},{32,24},{40,32},{48,40},{56,48},{64,56},{72,6... | collective-permute-start | bytes 1179656 | tf_op jit(solution)/shard_map/ppermute | solution.py:308
  84.7 12.9 %collective-permute-start.7 = (bf16[256,256]{1,0:T(8,128)(2,1)}, bf16[256,256]{1,0:T(8,128)(2,1)S(1)}, u32[]{:S(2)}, u32[]{:S(2)}) collective-permute-start(bf16[256,256]{1,0:T(8,128)(2,1)} %get-tuple-element.30), channel_id=1, source_target_pairs={{64,0},{72,8},{80,16},{88,24},{96,32},{104,40},{112,48},{120,56},{... | collective-permute-start | bytes 393224 | tf_op jit(solution)/shard_map/ppermute | solution.py:308
  90.2 15.6 %collective-permute-start.8 = (bf16[256,256]{1,0:T(8,128)(2,1)}, bf16[256,256]{1,0:T(8,128)(2,1)S(1)}, u32[]{:S(2)}, u32[]{:S(2)}) collective-permute-start(bf16[256,256]{1,0:T(8,128)(2,1)} %get-tuple-element.31), channel_id=1, source_target_pairs={{32,0},{40,8},{48,16},{56,24},{64,32},{72,40},{80,48},{88,56},{96,... | collective-permute-start | bytes 393224 | tf_op jit(solution)/shard_map/ppermute | solution.py:308
  92.6 13.1 %collective-permute-start.9 = (bf16[256,256]{1,0:T(8,128)(2,1)}, bf16[256,256]{1,0:T(8,128)(2,1)S(1)}, u32[]{:S(2)}, u32[]{:S(2)}) collective-permute-start(bf16[256,256]{1,0:T(8,128)(2,1)} %get-tuple-element.32), channel_id=1, source_target_pairs={{128,0},{136,8},{144,16},{152,24},{160,32},{168,40},{176,48},{184,... | collective-permute-start | bytes 393224 | tf_op jit(solution)/shard_map/ppermute | solution.py:308
  95.1 12.5 %collective-permute-start.10 = (bf16[256,256]{1,0:T(8,128)(2,1)}, bf16[256,256]{1,0:T(8,128)(2,1)S(1)}, u32[]{:S(2)}, u32[]{:S(2)}) collective-permute-start(bf16[256,256]{1,0:T(8,128)(2,1)} %get-tuple-element.33), channel_id=1, source_target_pairs={{16,0},{24,8},{32,16},{40,24},{48,32},{56,40},{64,48},{72,56},{80,... | collective-permute-start | bytes 393224 | tf_op jit(solution)/shard_map/ppermute | solution.py:308
  107.6 1.2 %copy-start.12 = (f32[1024,256]{1,0:T(8,128)S(1)}, f32[1024,256]{1,0:T(8,128)}, u32[]{:S(2)}) copy-start(f32[1024,256]{1,0:T(8,128)} %get-tuple-element.28.own_ref) | copy-start | bytes 3145732
  (4 other events, 2.6 us)

commit v5 on v4

--- a/solution.py
+++ b/solution.py
@@ -109,7 +109,7 @@
         acc = acc + dot(cot, w_ref[pl.ds(pl.multiple_of(src * 256, 256), 256), :], 1, 0)
         term = dot(cot, o, 0, 0).astype(BF)
         for sub in range(4):
-            rows = pl.ds(pl.multiple_of(src * 128 + sub * 32, 32), 32)
+            rows = pl.ds(pl.multiple_of((src % 2 * 4 + sub) * 128 + src // 2 * 32, 32), 32)
             low = term[sub * 64 : sub * 64 + 32, :]
             high = term[sub * 64 + 32 : sub * 64 + 64, :]
             keep_ref[rows, :] = jnp.where(core == 0, low, high)
@@ -260,6 +260,21 @@
     )(keep, received)
 
 
+def part_kernel(half_ref, out_ref):
+    out_ref[...] = jnp.sum(half_ref[...].astype(F32), axis=0).astype(BF)
+
+
+def part_sum(half):
+    return pl.pallas_call(
+        part_kernel,
+        out_shape=jax.ShapeDtypeStruct((NYL, 32, 256), BF),
+        in_specs=[VMEM],
+        out_specs=VMEM,
+        compiler_params=params(),
+        name="part_sum",
+    )(half)
+
+
 def total_kernel(part_ref, out_ref):
     out_ref[...] = jnp.sum(part_ref[...].astype(F32), axis=0) * (512 * 64) ** (-0.5)
 
@@ -342,9 +357,11 @@
     received = lax.ppermute(send, "tm", [(i, i ^ 1) for i in range(64)])
     dq, own, *back, token = attend(queries, keys, values, outputs, d_out, got)
     back = [shift(b, -(2**level)) for level, b in enumerate(back)]
-    half = add(keep, received).reshape(NYL * NZ, 32, 256)
-    groups = [[2 * i + c for i in range(NYL * NZ)] for c in range(2)]
-    part = lax.all_to_all(half, "tm", 0, 0, axis_index_groups=groups)
+    half = add(keep, received).reshape(NZ, NYL, 32, 256)
+    z_groups = [[yl * 16 + z * 2 + c for z in range(NZ)] for yl in range(NYL) for c in range(2)]
+    half = lax.all_to_all(half, "tm", 0, 0, axis_index_groups=z_groups)
+    y_groups = [[yl * 16 + zc for yl in range(NYL)] for zc in range(16)]
+    part = lax.all_to_all(part_sum(half), "tm", 0, 0, axis_index_groups=y_groups)
     weight_grad = total(part)
     dk, dv = finish(block_pick, own, back)
     return dq, dk, dv, weight_grad

time: 112 us -> 109 us (0.973)
  the two profiles are of different devices: /device:TPU:16 before, /device:TPU:1 now
where the time goes in v5:
time: 109 us
  starting transfers between devices  73.7 us (68%)
  Pallas kernels  15.8 us (14%)
  waiting for transfers between devices  10.1 us (9%)
  local copies, waits for them, and re-layouts  8.02 us (7%)
    ppermute x10, starting transfers between devices, shift(): lax.ppermute(block, 'tm', [(i, i + distance) for i in range(64) if 0 <= i...  32.5 us
    all_to_all x1, starting transfers between devices, on_device(): lax.all_to_all(part_sum(half), 'tm', 0, 0, axis_index_groups=y_groups)  14.6 us
    ppermute x1, starting transfers between devices, on_device(): lax.ppermute(out_cotangent, 'head', [(h, (h + NX) % (2 * NX)) for h in ra...  8.28 us
    unnamed x28, local copies, waits for them, and re-layouts  8.02 us
    ppermute x1, starting transfers between devices, on_device(): received = lax.ppermute(send, 'tm', [(i, i ^ 1) for i in range(64)])  8.02 us
    pallas_call x1, Pallas kernels, attend(): pl.pallas_call(attend_kernel, out_shape=[jax.ShapeDtypeStruct((512, 256),...  7.88 us
    all_to_all x1, starting transfers between devices, on_device(): half = lax.all_to_all(half, 'tm', 0, 0, axis_index_groups=z_groups)  6.21 us
    all_to_all x1, waiting for transfers between devices, on_device(): lax.all_to_all(part_sum(half), 'tm', 0, 0, axis_index_groups=y_groups)  4.11 us
  transfers between devices with their start and end apart: 15, of which 4 were waited for; matrix products, arithmetic and copies ran while one was open for 0% of the time, Pallas kernels for 12%

profile of v5, /device:TPU:1, one launch (start us, length us, event | category | flops | bytes accessed | tf_op | source)
XLA Modules:
  0.0 108.5 jit_solution(3933282432753126553)
XLA Ops:
  0.6 8.3 %collective-permute-start = (bf16[512,256]{1,0:T(8,128)(2,1)}, bf16[512,256]{1,0:T(8,128)(2,1)S(1)}, u32[]{:S(2)}, u32[]{:S(2)}) collective-permute-start(bf16[512,256]{1,0:T(8,128)(2,1)} %a_ref.1), channel_id=1, source_target_pairs={{0,4},{1,5},{2,6},{3,7},{4,0},{5,1},{6,2},{7,3},{8,12},{9,13},{10,... | collective-permute-start | bytes 786440 | tf_op jit(solution)/shard_map/ppermute | solution.py:351
  11.5 1.5 %pack.1 = (bf16[768,256]{1,0:T(8,128)(2,1)}, bf16[256,256]{1,0:T(8,128)(2,1)S(1)}, bf16[256,256]{1,0:T(8,128)(2,1)}, bf16[256,256]{1,0:T(8,128)(2,1)}, bf16[256,256]{1,0:T(8,128)(2,1)}) custom-call(s32[1,5]{1,0:T(1,128)S(1)} %copy-done.10, bf16[512,256]{1,0:T(8,128)(2,1)S(1)} %copy-done, bf16[512,256]{1,0:T(8,128)(2,1)S(1)} %copy-done.1), custom_call_target="tpu_custom_call" | custom-call | tf_op jit(solution)/shard_map/pack/pallas_call | solution.py:43
  13.6 4.8 %collective-permute-start.1 = (bf16[768,256]{1,0:T(8,128)(2,1)}, bf16[768,256]{1,0:T(8,128)(2,1)}, u32[]{:S(2)}, u32[]{:S(2)}) collective-permute-start(bf16[768,256]{1,0:T(8,128)(2,1)} %get-tuple-element.21), channel_id=1, source_target_pairs={{0,8},{8,16},{16,24},{24,32},{32,40},{40,48},{48,56},{56,64},{64,7... | collective-permute-start | bytes 1179656 | tf_op jit(solution)/shard_map/ppermute | solution.py:323
  19.4 1.5 %spread.1 = bf16[4,1024,256]{2,1,0:T(8,128)(2,1)} custom-call(bf16[512,256]{1,0:T(8,128)(2,1)S(1)} %copy-done.4, bf16[512,256]{1,0:T(8,128)(2,1)S(1)} %collective-permute-done.b_ref), custom_call_target="tpu_custom_call" | custom-call | tf_op jit(solution)/shard_map/spread/pallas_call | solution.py:335
  20.9 4.0 %all-to-all-start = ((bf16[4,1024,256]{2,1,0:T(8,128)(2,1)}), bf16[4,1024,256]{2,1,0:T(8,128)(2,1)S(1)}, u32[]{:S(2)}, u32[]{:S(2)}) async-start(bf16[4,1024,256]{2,1,0:T(8,128)(2,1)} %spread.1), calls=%async_computation | async-start | bytes 4194304 | tf_op jit(solution)/shard_map/all_to_all | solution.py:347
  24.9 9.7 %collective-permute-start.2 = (bf16[256,256]{1,0:T(8,128)(2,1)}, bf16[256,256]{1,0:T(8,128)(2,1)S(1)}, u32[]{:S(2)}, u32[]{:S(2)}) collective-permute-start(bf16[256,256]{1,0:T(8,128)(2,1)} %get-tuple-element.22), channel_id=1, source_target_pairs={{0,64},{8,72},{16,80},{24,88},{32,96},{40,104},{48,112},{56,120},{... | collective-permute-start | bytes 393224 | tf_op jit(solution)/shard_map/ppermute | solution.py:323
  34.6 4.0 %collective-permute-start.3 = (bf16[256,256]{1,0:T(8,128)(2,1)}, bf16[256,256]{1,0:T(8,128)(2,1)S(1)}, u32[]{:S(2)}, u32[]{:S(2)}) collective-permute-start(bf16[256,256]{1,0:T(8,128)(2,1)} %get-tuple-element.23), channel_id=1, source_target_pairs={{0,32},{8,40},{16,48},{24,56},{32,64},{40,72},{48,80},{56,88},{64,... | collective-permute-start | bytes 393224 | tf_op jit(solution)/shard_map/ppermute | solution.py:323
  38.6 3.0 %collective-permute-start.4 = (bf16[256,256]{1,0:T(8,128)(2,1)}, bf16[256,256]{1,0:T(8,128)(2,1)S(1)}, u32[]{:S(2)}, u32[]{:S(2)}) collective-permute-start(bf16[256,256]{1,0:T(8,128)(2,1)} %get-tuple-element.24), channel_id=1, source_target_pairs={{0,128},{8,136},{16,144},{24,152},{32,160},{40,168},{48,176},{56,1... | collective-permute-start | bytes 393224 | tf_op jit(solution)/shard_map/ppermute | solution.py:323
  41.7 3.2 %collective-permute-start.5 = (bf16[256,256]{1,0:T(8,128)(2,1)}, bf16[256,256]{1,0:T(8,128)(2,1)S(1)}, u32[]{:S(2)}, u32[]{:S(2)}) collective-permute-start(bf16[256,256]{1,0:T(8,128)(2,1)} %copy-done.13), channel_id=1, source_target_pairs={{0,16},{8,24},{16,32},{24,40},{32,48},{40,56},{48,64},{56,72},{64,... | collective-permute-start | bytes 393224 | tf_op jit(solution)/shard_map/ppermute | solution.py:323
  44.9 2.2 %collective-permute-done.5.refs_4_.f1 = bf16[256,256]{1,0:T(8,128)(2,1)S(1)} collective-permute-done((bf16[256,256]{1,0:T(8,128)(2,1)}, bf16[256,256]{1,0:T(8,128)(2,1)S(1)}, u32[]{:S(2)}, u32[]{:S(2)}) %collective-permute-start.5) | collective-permute-done | bytes 131104 | tf_op jit(solution)/shard_map/ppermute | solution.py:323
  49.1 1.3 %project.1 = (bf16[512,256]{1,0:T(8,128)(2,1)S(1)}, bf16[1024,256]{1,0:T(8,128)(2,1)S(1)}, bf16[1024,256]{1,0:T(8,128)(2,1)S(1)}) custom-call(bf16[4,1024,256]{2,1,0:T(8,128)(2,1)S(1)} %all-to-all-done.refs_0_, bf16[2048,256]{1,0:T(8,128)(2,1)S(1)} %copy-done.2, bf16[512,256]{1,0:T(8,128)(2,1)S(1)} %copy-done.3, f32[8,128]{1,0:T(8,128)S(1)} %gate.1.refs_3_), custom_call_target="tpu_custom_call" | custom-call | tf_op jit(solution)/shard_map/project/pallas_call | solution.py:122
  51.1 8.0 %collective-permute-start.11 = (bf16[1024,256]{1,0:T(8,128)(2,1)S(1)}, bf16[1024,256]{1,0:T(8,128)(2,1)S(1)}, u32[]{:S(2)}, u32[]{:S(2)}) collective-permute-start(bf16[1024,256]{1,0:T(8,128)(2,1)S(1)} %get-tuple-element.37), channel_id=1, source_target_pairs={{0,8},{8,0},{16,24},{24,16},{32,40},{40,32},{48,56},{56,48},{64,72... | collective-permute-start | bytes 1572872 | tf_op jit(solution)/shard_map/ppermute | solution.py:357
  59.1 1.5 %collective-permute-done.11.got_ref = bf16[1024,256]{1,0:T(8,128)(2,1)S(1)} collective-permute-done((bf16[1024,256]{1,0:T(8,128)(2,1)S(1)}, bf16[1024,256]{1,0:T(8,128)(2,1)S(1)}, u32[]{:S(2)}, u32[]{:S(2)}) %collective-permute-start.11) | collective-permute-done | bytes 524320 | tf_op jit(solution)/shard_map/ppermute | solution.py:357
  61.6 6.2 %all-to-all-start.1 = ((bf16[8,4,32,256]{3,2,1,0:T(8,128)(2,1)}), bf16[8,4,32,256]{3,2,1,0:T(8,128)(2,1)S(1)}, u32[]{:S(2)}, u32[]{:S(2)}) async-start(bf16[8,4,32,256]{3,2,1,0:T(8,128)(2,1)} %bitcast), calls=%async_computation.1 | async-start | bytes 1048576 | tf_op jit(solution)/shard_map/all_to_all | solution.py:362
  67.8 7.9 %attend.1 = (bf16[512,256]{1,0:T(8,128)(2,1)}, f32[1024,256]{1,0:T(8,128)}, bf16[768,256]{1,0:T(8,128)(2,1)}, bf16[256,256]{1,0:T(8,128)(2,1)}, bf16[256,256]{1,...) custom-call(bf16[512,256]{1,0:T(8,128)(2,1)} %q_hbm.1, ...), custom_call_target="tpu_custom_call" | custom-call | tf_op jit(solution)/shard_map/attend/pallas_call | solution.py:226
  75.7 2.6 %collective-permute-start.6 = (bf16[768,256]{1,0:T(8,128)(2,1)}, bf16[768,256]{1,0:T(8,128)(2,1)S(1)}, u32[]{:S(2)}, u32[]{:S(2)}) collective-permute-start(bf16[768,256]{1,0:T(8,128)(2,1)} %get-tuple-element.29), channel_id=1, source_target_pairs={{8,0},{16,8},{24,16},{32,24},{40,32},{48,40},{56,48},{64,56},{72,6... | collective-permute-start | bytes 1179656 | tf_op jit(solution)/shard_map/ppermute | solution.py:323
  78.2 1.3 %collective-permute-start.7 = (bf16[256,256]{1,0:T(8,128)(2,1)}, bf16[256,256]{1,0:T(8,128)(2,1)S(1)}, u32[]{:S(2)}, u32[]{:S(2)}) collective-permute-start(bf16[256,256]{1,0:T(8,128)(2,1)} %get-tuple-element.30), channel_id=1, source_target_pairs={{64,0},{72,8},{80,16},{88,24},{96,32},{104,40},{112,48},{120,56},{... | collective-permute-start | bytes 393224 | tf_op jit(solution)/shard_map/ppermute | solution.py:323
  79.5 1.3 %collective-permute-start.8 = (bf16[256,256]{1,0:T(8,128)(2,1)}, bf16[256,256]{1,0:T(8,128)(2,1)S(1)}, u32[]{:S(2)}, u32[]{:S(2)}) collective-permute-start(bf16[256,256]{1,0:T(8,128)(2,1)} %get-tuple-element.31), channel_id=1, source_target_pairs={{32,0},{40,8},{48,16},{56,24},{64,32},{72,40},{80,48},{88,56},{96,... | collective-permute-start | bytes 393224 | tf_op jit(solution)/shard_map/ppermute | solution.py:323
  80.8 1.3 %collective-permute-start.9 = (bf16[256,256]{1,0:T(8,128)(2,1)}, bf16[256,256]{1,0:T(8,128)(2,1)S(1)}, u32[]{:S(2)}, u32[]{:S(2)}) collective-permute-start(bf16[256,256]{1,0:T(8,128)(2,1)} %get-tuple-element.32), channel_id=1, source_target_pairs={{128,0},{136,8},{144,16},{152,24},{160,32},{168,40},{176,48},{184,... | collective-permute-start | bytes 393224 | tf_op jit(solution)/shard_map/ppermute | solution.py:323
  82.1 1.3 %collective-permute-start.10 = (bf16[256,256]{1,0:T(8,128)(2,1)}, bf16[256,256]{1,0:T(8,128)(2,1)S(1)}, u32[]{:S(2)}, u32[]{:S(2)}) collective-permute-start(bf16[256,256]{1,0:T(8,128)(2,1)} %get-tuple-element.33), channel_id=1, source_target_pairs={{16,0},{24,8},{32,16},{40,24},{48,32},{56,40},{64,48},{72,56},{80,... | collective-permute-start | bytes 393224 | tf_op jit(solution)/shard_map/ppermute | solution.py:323
  83.4 2.3 %all-to-all-done.1.half_ref = bf16[8,4,32,256]{3,2,1,0:T(8,128)(2,1)S(1)} async-done(((bf16[8,4,32,256]{3,2,1,0:T(8,128)(2,1)}), bf16[8,4,32,256]{3,2,1,0:T(8,128)(2,1)S(1)}, u32[]{:S(2)}, u32[]{:S(2)}) %all-to-all-start.1) | async-done | bytes 524320 | tf_op jit(solution)/shard_map/all_to_all | solution.py:362
  86.4 14.6 %all-to-all-start.2 = ((bf16[4,32,256]{2,1,0:T(8,128)(2,1)}), bf16[4,32,256]{2,1,0:T(8,128)(2,1)S(1)}, u32[]{:S(2)}, u32[]{:S(2)}) async-start(bf16[4,32,256]{2,1,0:T(8,128)(2,1)} %part_sum.1), calls=%async_computation.2 | async-start | bytes 131072 | tf_op jit(solution)/shard_map/all_to_all | solution.py:364
  102.3 1.5 %finish.1 = (bf16[512,256]{1,0:T(8,128)(2,1)}, bf16[512,256]{1,0:T(8,128)(2,1)}) custom-call(s32[1,5]{1,0:T(1,128)S(1)} %copy-done.11, f32[1024,256]{1,0:T(8,128)S(1)} %copy-done.12, bf16[768,256]{1,0:T(8,128)(2,1)S(1)} %collective-permute-done.6.near_ref, bf16[256,256]{1,0:T(8,128)(2,1)S(1)} %collective-permute-done.7.f3, ...), custom_call_target="tpu_custom_call" | custom-call | flops 5000000000 | bytes 1048576 | tf_op jit(solution)/shard_map/finish/pallas_call | solution.py:308
  103.8 4.1 %all-to-all-done.2.part_ref = bf16[4,32,256]{2,1,0:T(8,128)(2,1)S(1)} async-done(((bf16[4,32,256]{2,1,0:T(8,128)(2,1)}), bf16[4,32,256]{2,1,0:T(8,128)(2,1)S(1)}, u32[]{:S(2)}, u32[]{:S(2)}) %all-to-all-start.2) | async-done | bytes 65568 | tf_op jit(solution)/shard_map/all_to_all | solution.py:364
  (43 shorter events, 10.3 us)
Async XLA Ops:
  0.6 17.8 %collective-permute-start = (bf16[512,256]{1,0:T(8,128)(2,1)}, bf16[512,256]{1,0:T(8,128)(2,1)S(1)}, u32[]{:S(2)}, u32[]{:S(2)}) collective-permute-start(bf16[512,256]{1,0:T(8,128)(2,1)} %a_ref.1), channel_id=1, source_target_pairs={{0,4},{1,5},{2,6},{3,7},{4,0},{5,1},{6,2},{7,3},{8,12},{9,13},{10,... | collective-permute-start | bytes 786440 | tf_op jit(solution)/shard_map/ppermute | solution.py:351
  8.9 1.0 copy-start
  9.9 0.9 copy-start.1
  13.6 33.5 %collective-permute-start.1 = (bf16[768,256]{1,0:T(8,128)(2,1)}, bf16[768,256]{1,0:T(8,128)(2,1)}, u32[]{:S(2)}, u32[]{:S(2)}) collective-permute-start(bf16[768,256]{1,0:T(8,128)(2,1)} %get-tuple-element.21), channel_id=1, source_target_pairs={{0,8},{8,16},{16,24},{24,32},{32,40},{40,48},{48,56},{56,64},{64,7... | collective-permute-start | bytes 1179656 | tf_op jit(solution)/shard_map/ppermute | solution.py:323
  18.4 1.0 copy-start.4
  20.9 28.2 %all-to-all-start = ((bf16[4,1024,256]{2,1,0:T(8,128)(2,1)}), bf16[4,1024,256]{2,1,0:T(8,128)(2,1)S(1)}, u32[]{:S(2)}, u32[]{:S(2)}) async-start(bf16[4,1024,256]{2,1,0:T(8,128)(2,1)} %spread.1), calls=%async_computation | async-start | bytes 4194304 | tf_op jit(solution)/shard_map/all_to_all | solution.py:347
  24.9 20.0 %collective-permute-start.2 = (bf16[256,256]{1,0:T(8,128)(2,1)}, bf16[256,256]{1,0:T(8,128)(2,1)S(1)}, u32[]{:S(2)}, u32[]{:S(2)}) collective-permute-start(bf16[256,256]{1,0:T(8,128)(2,1)} %get-tuple-element.22), channel_id=1, source_target_pairs={{0,64},{8,72},{16,80},{24,88},{32,96},{40,104},{48,112},{56,120},{... | collective-permute-start | bytes 393224 | tf_op jit(solution)/shard_map/ppermute | solution.py:323
  34.6 10.3 %collective-permute-start.3 = (bf16[256,256]{1,0:T(8,128)(2,1)}, bf16[256,256]{1,0:T(8,128)(2,1)S(1)}, u32[]{:S(2)}, u32[]{:S(2)}) collective-permute-start(bf16[256,256]{1,0:T(8,128)(2,1)} %get-tuple-element.23), channel_id=1, source_target_pairs={{0,32},{8,40},{16,48},{24,56},{32,64},{40,72},{48,80},{56,88},{64,... | collective-permute-start | bytes 393224 | tf_op jit(solution)/shard_map/ppermute | solution.py:323
  38.6 6.3 %collective-permute-start.4 = (bf16[256,256]{1,0:T(8,128)(2,1)}, bf16[256,256]{1,0:T(8,128)(2,1)S(1)}, u32[]{:S(2)}, u32[]{:S(2)}) collective-permute-start(bf16[256,256]{1,0:T(8,128)(2,1)} %get-tuple-element.24), channel_id=1, source_target_pairs={{0,128},{8,136},{16,144},{24,152},{32,160},{40,168},{48,176},{56,1... | collective-permute-start | bytes 393224 | tf_op jit(solution)/shard_map/ppermute | solution.py:323
  41.6 7.5 %copy-start.2 = (bf16[2048,256]{1,0:T(8,128)(2,1)S(1)}, bf16[2048,256]{1,0:T(8,128)(2,1)}, u32[]{:S(2)}) copy-start(bf16[2048,256]{1,0:T(8,128)(2,1)} %refs_1_.1) | copy-start | bytes 3145732
  41.6 7.5 %copy-start.3 = (bf16[512,256]{1,0:T(8,128)(2,1)S(1)}, bf16[512,256]{1,0:T(8,128)(2,1)}, u32[]{:S(2)}) copy-start(bf16[512,256]{1,0:T(8,128)(2,1)} %o_hbm.1) | copy-start | bytes 786436
  41.7 5.5 %collective-permute-start.5 = (bf16[256,256]{1,0:T(8,128)(2,1)}, bf16[256,256]{1,0:T(8,128)(2,1)S(1)}, u32[]{:S(2)}, u32[]{:S(2)}) collective-permute-start(bf16[256,256]{1,0:T(8,128)(2,1)} %copy-done.13), channel_id=1, source_target_pairs={{0,16},{8,24},{16,32},{24,40},{32,48},{40,56},{48,64},{56,72},{64,... | collective-permute-start | bytes 393224 | tf_op jit(solution)/shard_map/ppermute | solution.py:323
  44.9 2.2 %copy-start.6 = (bf16[256,256]{1,0:T(8,128)(2,1)}, bf16[256,256]{1,0:T(8,128)(2,1)S(1)}, u32[]{:S(2)}) copy-start(bf16[256,256]{1,0:T(8,128)(2,1)S(1)} %collective-permute-done.2.refs_1_.f3) | copy-start | bytes 393220
  50.4 0.7 copy-start.5
  51.1 9.5 %collective-permute-start.11 = (bf16[1024,256]{1,0:T(8,128)(2,1)S(1)}, bf16[1024,256]{1,0:T(8,128)(2,1)S(1)}, u32[]{:S(2)}, u32[]{:S(2)}) collective-permute-start(bf16[1024,256]{1,0:T(8,128)(2,1)S(1)} %get-tuple-element.37), channel_id=1, source_target_pairs={{0,8},{8,0},{16,24},{24,16},{32,40},{40,32},{48,56},{56,48},{64,72... | collective-permute-start | bytes 1572872 | tf_op jit(solution)/shard_map/ppermute | solution.py:357
  61.6 39.5 %copy-start.11 = (s32[1,5]{1,0:T(1,128)S(1)}, s32[1,5]{1,0:T(1,128)}, u32[]{:S(2)}) copy-start(s32[1,5]{1,0:T(1,128)} %pick.3) | copy-start | bytes 64
  61.6 24.2 %all-to-all-start.1 = ((bf16[8,4,32,256]{3,2,1,0:T(8,128)(2,1)}), bf16[8,4,32,256]{3,2,1,0:T(8,128)(2,1)S(1)}, u32[]{:S(2)}, u32[]{:S(2)}) async-start(bf16[8,4,32,256]{3,2,1,0:T(8,128)(2,1)} %bitcast), calls=%async_computation.1 | async-start | bytes 1048576 | tf_op jit(solution)/shard_map/all_to_all | solution.py:362
  75.7 25.4 %collective-permute-start.6 = (bf16[768,256]{1,0:T(8,128)(2,1)}, bf16[768,256]{1,0:T(8,128)(2,1)S(1)}, u32[]{:S(2)}, u32[]{:S(2)}) collective-permute-start(bf16[768,256]{1,0:T(8,128)(2,1)} %get-tuple-element.29), channel_id=1, source_target_pairs={{8,0},{16,8},{24,16},{32,24},{40,32},{48,40},{56,48},{64,56},{72,6... | collective-permute-start | bytes 1179656 | tf_op jit(solution)/shard_map/ppermute | solution.py:323
  78.2 22.8 %collective-permute-start.7 = (bf16[256,256]{1,0:T(8,128)(2,1)}, bf16[256,256]{1,0:T(8,128)(2,1)S(1)}, u32[]{:S(2)}, u32[]{:S(2)}) collective-permute-start(bf16[256,256]{1,0:T(8,128)(2,1)} %get-tuple-element.30), channel_id=1, source_target_pairs={{64,0},{72,8},{80,16},{88,24},{96,32},{104,40},{112,48},{120,56},{... | collective-permute-start | bytes 393224 | tf_op jit(solution)/shard_map/ppermute | solution.py:323
  79.5 21.5 %collective-permute-start.8 = (bf16[256,256]{1,0:T(8,128)(2,1)}, bf16[256,256]{1,0:T(8,128)(2,1)S(1)}, u32[]{:S(2)}, u32[]{:S(2)}) collective-permute-start(bf16[256,256]{1,0:T(8,128)(2,1)} %get-tuple-element.31), channel_id=1, source_target_pairs={{32,0},{40,8},{48,16},{56,24},{64,32},{72,40},{80,48},{88,56},{96,... | collective-permute-start | bytes 393224 | tf_op jit(solution)/shard_map/ppermute | solution.py:323
  80.8 20.2 %collective-permute-start.9 = (bf16[256,256]{1,0:T(8,128)(2,1)}, bf16[256,256]{1,0:T(8,128)(2,1)S(1)}, u32[]{:S(2)}, u32[]{:S(2)}) collective-permute-start(bf16[256,256]{1,0:T(8,128)(2,1)} %get-tuple-element.32), channel_id=1, source_target_pairs={{128,0},{136,8},{144,16},{152,24},{160,32},{168,40},{176,48},{184,... | collective-permute-start | bytes 393224 | tf_op jit(solution)/shard_map/ppermute | solution.py:323
  82.1 18.9 %collective-permute-start.10 = (bf16[256,256]{1,0:T(8,128)(2,1)}, bf16[256,256]{1,0:T(8,128)(2,1)S(1)}, u32[]{:S(2)}, u32[]{:S(2)}) collective-permute-start(bf16[256,256]{1,0:T(8,128)(2,1)} %get-tuple-element.33), channel_id=1, source_target_pairs={{16,0},{24,8},{32,16},{40,24},{48,32},{56,40},{64,48},{72,56},{80,... | collective-permute-start | bytes 393224 | tf_op jit(solution)/shard_map/ppermute | solution.py:323
  86.4 21.5 %all-to-all-start.2 = ((bf16[4,32,256]{2,1,0:T(8,128)(2,1)}), bf16[4,32,256]{2,1,0:T(8,128)(2,1)S(1)}, u32[]{:S(2)}, u32[]{:S(2)}) async-start(bf16[4,32,256]{2,1,0:T(8,128)(2,1)} %part_sum.1), calls=%async_computation.2 | async-start | bytes 131072 | tf_op jit(solution)/shard_map/all_to_all | solution.py:364
  101.1 1.2 %copy-start.12 = (f32[1024,256]{1,0:T(8,128)S(1)}, f32[1024,256]{1,0:T(8,128)}, u32[]{:S(2)}) copy-start(f32[1024,256]{1,0:T(8,128)} %get-tuple-element.28.own_ref) | copy-start | bytes 3145732
  (5 other events, 3.3 us)

commit v6 on v5

--- a/solution.py
+++ b/solution.py
@@ -10,7 +10,7 @@
 BLK = 128
 LEVELS = 5
 FINISH_MIB = 16
-GATE_MIB = 16
+GATE_MIB = 60
 ATTEND_MIB = 60
 BF = jnp.bfloat16
 F32 = jnp.float32
@@ -81,15 +81,15 @@
 
 
 def gate_kernel(*refs):
-    refs[-1][...] = jnp.zeros((8, 128), F32)
+    refs[-1][0, 0] = jnp.int32(0)
 
 
 def gate(*got):
     return pl.pallas_call(
         gate_kernel,
-        out_shape=jax.ShapeDtypeStruct((8, 128), F32),
+        out_shape=jax.ShapeDtypeStruct((1, 128), jnp.int32),
         in_specs=[ANY] * len(got),
-        out_specs=VMEM,
+        out_specs=SMEM,
         compiler_params=params(GATE_MIB),
         cost_estimate=pl.CostEstimate(
             flops=13000000000, bytes_accessed=2**20, transcendentals=0
@@ -122,7 +122,7 @@
     return pl.pallas_call(
         project_kernel,
         out_shape=[jax.ShapeDtypeStruct((512, 256), BF), half, half],
-        in_specs=[VMEM] * (PIECES + 2) + [ANY],
+        in_specs=[VMEM] * (PIECES + 2) + [SMEM],
         out_specs=[VMEM] * 3,
         compiler_params=params(),
         name="project",

time: 109 us -> 111 us (1.018)
  starting transfers between devices: 73.7 us -> 75.3 us
  local copies, waits for them, and re-layouts: 8.02 us -> 6.73 us
    unnamed x28, local copies, waits for them, and re-layouts: 8.02 us -> 6.73 us
where the time goes in v6:
time: 111 us; the launch traced here: 110 us
  starting transfers between devices  75.3 us (68%)
  Pallas kernels  16.9 us (15%)
  waiting for transfers between devices  9.8 us (9%)
  local copies, waits for them, and re-layouts  6.73 us (6%)
    ppermute x10, starting transfers between devices, shift(): lax.ppermute(block, 'tm', [(i, i + distance) for i in range(64) if 0 <= i...  33.2 us
    all_to_all x1, starting transfers between devices, on_device(): lax.all_to_all(part_sum(half), 'tm', 0, 0, axis_index_groups=y_groups)  15.2 us
    ppermute x1, starting transfers between devices, on_device(): lax.ppermute(out_cotangent, 'head', [(h, (h + NX) % (2 * NX)) for h in ra...  8.28 us
    ppermute x1, starting transfers between devices, on_device(): received = lax.ppermute(send, 'tm', [(i, i ^ 1) for i in range(64)])  8.02 us
    pallas_call x1, Pallas kernels, attend(): pl.pallas_call(attend_kernel, out_shape=[jax.ShapeDtypeStruct((512, 256),...  7.86 us
    unnamed x28, local copies, waits for them, and re-layouts  6.73 us
    all_to_all x1, starting transfers between devices, on_device(): half = lax.all_to_all(half, 'tm', 0, 0, axis_index_groups=z_groups)  6.63 us
    all_to_all x1, waiting for transfers between devices, on_device(): lax.all_to_all(part_sum(half), 'tm', 0, 0, axis_index_groups=y_groups)  4.07 us
  transfers between devices with their start and end apart: 15, of which 4 were waited for; matrix products, arithmetic and copies ran while one was open for 0% of the time, Pallas kernels for 12%

profile of v6, /device:TPU:1, one launch (start us, length us, event | category | flops | bytes accessed | tf_op | source)
XLA Modules:
  0.0 109.7 jit_solution(9088603942546897263)
XLA Ops:
  0.6 8.3 %collective-permute-start = (bf16[512,256]{1,0:T(8,128)(2,1)}, bf16[512,256]{1,0:T(8,128)(2,1)S(1)}, u32[]{:S(2)}, u32[]{:S(2)}) collective-permute-start(bf16[512,256]{1,0:T(8,128)(2,1)} %a_ref.1), channel_id=1, source_target_pairs={{0,4},{1,5},{2,6},{3,7},{4,0},{5,1},{6,2},{7,3},{8,12},{9,13},{10,... | collective-permute-start | bytes 786440 | tf_op jit(solution)/shard_map/ppermute | solution.py:351
  11.5 1.5 %pack.1 = (bf16[768,256]{1,0:T(8,128)(2,1)}, bf16[256,256]{1,0:T(8,128)(2,1)S(1)}, bf16[256,256]{1,0:T(8,128)(2,1)}, bf16[256,256]{1,0:T(8,128)(2,1)}, bf16[256,256]{1,0:T(8,128)(2,1)}) custom-call(s32[1,5]{1,0:T(1,128)S(1)} %copy-done.6, bf16[512,256]{1,0:T(8,128)(2,1)S(1)} %copy-done.1, bf16[512,256]{1,0:T(8,128)(2,1)S(1)} %copy-done.2), custom_call_target="tpu_custom_call" | custom-call | tf_op jit(solution)/shard_map/pack/pallas_call | solution.py:43
  12.9 4.8 %collective-permute-start.1 = (bf16[768,256]{1,0:T(8,128)(2,1)}, bf16[768,256]{1,0:T(8,128)(2,1)}, u32[]{:S(2)}, u32[]{:S(2)}) collective-permute-start(bf16[768,256]{1,0:T(8,128)(2,1)} %get-tuple-element.21), channel_id=1, source_target_pairs={{0,8},{8,16},{16,24},{24,32},{32,40},{40,48},{48,56},{56,64},{64,7... | collective-permute-start | bytes 1179656 | tf_op jit(solution)/shard_map/ppermute | solution.py:323
  18.7 1.5 %spread.1 = bf16[4,1024,256]{2,1,0:T(8,128)(2,1)} custom-call(bf16[512,256]{1,0:T(8,128)(2,1)S(1)} %copy-done.4, bf16[512,256]{1,0:T(8,128)(2,1)S(1)} %collective-permute-done.b_ref), custom_call_target="tpu_custom_call" | custom-call | tf_op jit(solution)/shard_map/spread/pallas_call | solution.py:335
  20.2 4.0 %all-to-all-start = ((bf16[4,1024,256]{2,1,0:T(8,128)(2,1)}), bf16[4,1024,256]{2,1,0:T(8,128)(2,1)S(1)}, u32[]{:S(2)}, u32[]{:S(2)}) async-start(bf16[4,1024,256]{2,1,0:T(8,128)(2,1)} %spread.1), calls=%async_computation | async-start | bytes 4194304 | tf_op jit(solution)/shard_map/all_to_all | solution.py:347
  24.2 9.7 %collective-permute-start.2 = (bf16[256,256]{1,0:T(8,128)(2,1)}, bf16[256,256]{1,0:T(8,128)(2,1)S(1)}, u32[]{:S(2)}, u32[]{:S(2)}) collective-permute-start(bf16[256,256]{1,0:T(8,128)(2,1)} %get-tuple-element.22), channel_id=1, source_target_pairs={{0,64},{8,72},{16,80},{24,88},{32,96},{40,104},{48,112},{56,120},{... | collective-permute-start | bytes 393224 | tf_op jit(solution)/shard_map/ppermute | solution.py:323
  34.0 4.0 %collective-permute-start.3 = (bf16[256,256]{1,0:T(8,128)(2,1)}, bf16[256,256]{1,0:T(8,128)(2,1)S(1)}, u32[]{:S(2)}, u32[]{:S(2)}) collective-permute-start(bf16[256,256]{1,0:T(8,128)(2,1)} %get-tuple-element.23), channel_id=1, source_target_pairs={{0,32},{8,40},{16,48},{24,56},{32,64},{40,72},{48,80},{56,88},{64,... | collective-permute-start | bytes 393224 | tf_op jit(solution)/shard_map/ppermute | solution.py:323
  38.0 3.6 %collective-permute-start.4 = (bf16[256,256]{1,0:T(8,128)(2,1)}, bf16[256,256]{1,0:T(8,128)(2,1)S(1)}, u32[]{:S(2)}, u32[]{:S(2)}) collective-permute-start(bf16[256,256]{1,0:T(8,128)(2,1)} %get-tuple-element.24), channel_id=1, source_target_pairs={{0,128},{8,136},{16,144},{24,152},{32,160},{40,168},{48,176},{56,1... | collective-permute-start | bytes 393224 | tf_op jit(solution)/shard_map/ppermute | solution.py:323
  41.7 3.2 %collective-permute-start.5 = (bf16[256,256]{1,0:T(8,128)(2,1)S(1)}, bf16[256,256]{1,0:T(8,128)(2,1)S(1)}, u32[]{:S(2)}, u32[]{:S(2)}) collective-permute-start(bf16[256,256]{1,0:T(8,128)(2,1)S(1)} %get-tuple-element.25), channel_id=1, source_target_pairs={{0,16},{8,24},{16,32},{24,40},{32,48},{40,56},{48,64},{56,72},{64,... | collective-permute-start | bytes 393224 | tf_op jit(solution)/shard_map/ppermute | solution.py:323
  45.0 1.9 %collective-permute-done.5.refs_4_.f1 = bf16[256,256]{1,0:T(8,128)(2,1)S(1)} collective-permute-done((bf16[256,256]{1,0:T(8,128)(2,1)S(1)}, bf16[256,256]{1,0:T(8,128)(2,1)S(1)}, u32[]{:S(2)}, u32[]{:S(2)}) %collective-permute-start.5) | collective-permute-done | bytes 131104 | tf_op jit(solution)/shard_map/ppermute | solution.py:323
  48.7 1.8 %project.1 = (bf16[512,256]{1,0:T(8,128)(2,1)S(1)}, bf16[1024,256]{1,0:T(8,128)(2,1)S(1)}, bf16[1024,256]{1,0:T(8,128)(2,1)S(1)}) custom-call(bf16[4,1024,256]{2,1,0:T(8,128)(2,1)S(1)} %all-to-all-done.refs_0_, bf16[2048,256]{1,0:T(8,128)(2,1)S(1)} %copy-done.3, bf16[512,256]{1,0:T(8,128)(2,1)S(1)} %copy-done, s32[1,128]{1,0:T(1,128)S(1)} %copy-done.8), custom_call_target="tpu_custom_call" | custom-call | tf_op jit(solution)/shard_map/project/pallas_call | solution.py:122
  51.2 8.0 %collective-permute-start.11 = (bf16[1024,256]{1,0:T(8,128)(2,1)S(1)}, bf16[1024,256]{1,0:T(8,128)(2,1)S(1)}, u32[]{:S(2)}, u32[]{:S(2)}) collective-permute-start(bf16[1024,256]{1,0:T(8,128)(2,1)S(1)} %get-tuple-element.37), channel_id=1, source_target_pairs={{0,8},{8,0},{16,24},{24,16},{32,40},{40,32},{48,56},{56,48},{64,72... | collective-permute-start | bytes 1572872 | tf_op jit(solution)/shard_map/ppermute | solution.py:357
  59.3 1.5 %collective-permute-done.11.got_ref = bf16[1024,256]{1,0:T(8,128)(2,1)S(1)} collective-permute-done((bf16[1024,256]{1,0:T(8,128)(2,1)S(1)}, bf16[1024,256]{1,0:T(8,128)(2,1)S(1)}, u32[]{:S(2)}, u32[]{:S(2)}) %collective-permute-start.11) | collective-permute-done | bytes 524320 | tf_op jit(solution)/shard_map/ppermute | solution.py:357
  61.7 6.6 %all-to-all-start.1 = ((bf16[8,4,32,256]{3,2,1,0:T(8,128)(2,1)}), bf16[8,4,32,256]{3,2,1,0:T(8,128)(2,1)S(1)}, u32[]{:S(2)}, u32[]{:S(2)}) async-start(bf16[8,4,32,256]{3,2,1,0:T(8,128)(2,1)} %bitcast), calls=%async_computation.1 | async-start | bytes 1048576 | tf_op jit(solution)/shard_map/all_to_all | solution.py:362
  68.3 7.9 %attend.1 = (bf16[512,256]{1,0:T(8,128)(2,1)}, f32[1024,256]{1,0:T(8,128)}, bf16[768,256]{1,0:T(8,128)(2,1)}, bf16[256,256]{1,0:T(8,128)(2,1)}, bf16[256,256]{1,...) custom-call(bf16[512,256]{1,0:T(8,128)(2,1)} %q_hbm.1, ...), custom_call_target="tpu_custom_call" | custom-call | tf_op jit(solution)/shard_map/attend/pallas_call | solution.py:226
  76.2 2.6 %collective-permute-start.6 = (bf16[768,256]{1,0:T(8,128)(2,1)}, bf16[768,256]{1,0:T(8,128)(2,1)S(1)}, u32[]{:S(2)}, u32[]{:S(2)}) collective-permute-start(bf16[768,256]{1,0:T(8,128)(2,1)} %get-tuple-element.29), channel_id=1, source_target_pairs={{8,0},{16,8},{24,16},{32,24},{40,32},{48,40},{56,48},{64,56},{72,6... | collective-permute-start | bytes 1179656 | tf_op jit(solution)/shard_map/ppermute | solution.py:323
  78.7 1.3 %collective-permute-start.7 = (bf16[256,256]{1,0:T(8,128)(2,1)}, bf16[256,256]{1,0:T(8,128)(2,1)S(1)}, u32[]{:S(2)}, u32[]{:S(2)}) collective-permute-start(bf16[256,256]{1,0:T(8,128)(2,1)} %get-tuple-element.30), channel_id=1, source_target_pairs={{64,0},{72,8},{80,16},{88,24},{96,32},{104,40},{112,48},{120,56},{... | collective-permute-start | bytes 393224 | tf_op jit(solution)/shard_map/ppermute | solution.py:323
  80.0 1.3 %collective-permute-start.8 = (bf16[256,256]{1,0:T(8,128)(2,1)}, bf16[256,256]{1,0:T(8,128)(2,1)S(1)}, u32[]{:S(2)}, u32[]{:S(2)}) collective-permute-start(bf16[256,256]{1,0:T(8,128)(2,1)} %get-tuple-element.31), channel_id=1, source_target_pairs={{32,0},{40,8},{48,16},{56,24},{64,32},{72,40},{80,48},{88,56},{96,... | collective-permute-start | bytes 393224 | tf_op jit(solution)/shard_map/ppermute | solution.py:323
  81.3 1.3 %collective-permute-start.9 = (bf16[256,256]{1,0:T(8,128)(2,1)}, bf16[256,256]{1,0:T(8,128)(2,1)S(1)}, u32[]{:S(2)}, u32[]{:S(2)}) collective-permute-start(bf16[256,256]{1,0:T(8,128)(2,1)} %get-tuple-element.32), channel_id=1, source_target_pairs={{128,0},{136,8},{144,16},{152,24},{160,32},{168,40},{176,48},{184,... | collective-permute-start | bytes 393224 | tf_op jit(solution)/shard_map/ppermute | solution.py:323
  82.6 1.3 %collective-permute-start.10 = (bf16[256,256]{1,0:T(8,128)(2,1)}, bf16[256,256]{1,0:T(8,128)(2,1)S(1)}, u32[]{:S(2)}, u32[]{:S(2)}) collective-permute-start(bf16[256,256]{1,0:T(8,128)(2,1)} %get-tuple-element.33), channel_id=1, source_target_pairs={{16,0},{24,8},{32,16},{40,24},{48,32},{56,40},{64,48},{72,56},{80,... | collective-permute-start | bytes 393224 | tf_op jit(solution)/shard_map/ppermute | solution.py:323
  83.9 2.3 %all-to-all-done.1.half_ref = bf16[8,4,32,256]{3,2,1,0:T(8,128)(2,1)S(1)} async-done(((bf16[8,4,32,256]{3,2,1,0:T(8,128)(2,1)}), bf16[8,4,32,256]{3,2,1,0:T(8,128)(2,1)S(1)}, u32[]{:S(2)}, u32[]{:S(2)}) %all-to-all-start.1) | async-done | bytes 524320 | tf_op jit(solution)/shard_map/all_to_all | solution.py:362
  87.0 15.2 %all-to-all-start.2 = ((bf16[4,32,256]{2,1,0:T(8,128)(2,1)}), bf16[4,32,256]{2,1,0:T(8,128)(2,1)S(1)}, u32[]{:S(2)}, u32[]{:S(2)}) async-start(bf16[4,32,256]{2,1,0:T(8,128)(2,1)} %part_sum.1), calls=%async_computation.2 | async-start | bytes 131072 | tf_op jit(solution)/shard_map/all_to_all | solution.py:364
  103.5 1.5 %finish.1 = (bf16[512,256]{1,0:T(8,128)(2,1)}, bf16[512,256]{1,0:T(8,128)(2,1)}) custom-call(s32[1,5]{1,0:T(1,128)S(1)} %copy-done.7, f32[1024,256]{1,0:T(8,128)S(1)} %copy-done.9, bf16[768,256]{1,0:T(8,128)(2,1)S(1)} %collective-permute-done.6.near_ref, bf16[256,256]{1,0:T(8,128)(2,1)S(1)} %collective-permute-done.7.f3, ...), custom_call_target="tpu_custom_call" | custom-call | flops 5000000000 | bytes 1048576 | tf_op jit(solution)/shard_map/finish/pallas_call | solution.py:308
  105.0 4.1 %all-to-all-done.2.part_ref = bf16[4,32,256]{2,1,0:T(8,128)(2,1)S(1)} async-done(((bf16[4,32,256]{2,1,0:T(8,128)(2,1)}), bf16[4,32,256]{2,1,0:T(8,128)(2,1)S(1)}, u32[]{:S(2)}, u32[]{:S(2)}) %all-to-all-start.2) | async-done | bytes 65568 | tf_op jit(solution)/shard_map/all_to_all | solution.py:364
  (43 shorter events, 9.5 us)
Async XLA Ops:
  0.6 17.2 %collective-permute-start = (bf16[512,256]{1,0:T(8,128)(2,1)}, bf16[512,256]{1,0:T(8,128)(2,1)S(1)}, u32[]{:S(2)}, u32[]{:S(2)}) collective-permute-start(bf16[512,256]{1,0:T(8,128)(2,1)} %a_ref.1), channel_id=1, source_target_pairs={{0,4},{1,5},{2,6},{3,7},{4,0},{5,1},{6,2},{7,3},{8,12},{9,13},{10,... | collective-permute-start | bytes 786440 | tf_op jit(solution)/shard_map/ppermute | solution.py:351
  8.9 1.0 copy-start.1
  12.9 33.9 %collective-permute-start.1 = (bf16[768,256]{1,0:T(8,128)(2,1)}, bf16[768,256]{1,0:T(8,128)(2,1)}, u32[]{:S(2)}, u32[]{:S(2)}) collective-permute-start(bf16[768,256]{1,0:T(8,128)(2,1)} %get-tuple-element.21), channel_id=1, source_target_pairs={{0,8},{8,16},{16,24},{24,32},{32,40},{40,48},{48,56},{56,64},{64,7... | collective-permute-start | bytes 1179656 | tf_op jit(solution)/shard_map/ppermute | solution.py:323
  17.8 1.0 copy-start.4
  20.2 27.8 %all-to-all-start = ((bf16[4,1024,256]{2,1,0:T(8,128)(2,1)}), bf16[4,1024,256]{2,1,0:T(8,128)(2,1)S(1)}, u32[]{:S(2)}, u32[]{:S(2)}) async-start(bf16[4,1024,256]{2,1,0:T(8,128)(2,1)} %spread.1), calls=%async_computation | async-start | bytes 4194304 | tf_op jit(solution)/shard_map/all_to_all | solution.py:347
  24.2 20.7 %collective-permute-start.2 = (bf16[256,256]{1,0:T(8,128)(2,1)}, bf16[256,256]{1,0:T(8,128)(2,1)S(1)}, u32[]{:S(2)}, u32[]{:S(2)}) collective-permute-start(bf16[256,256]{1,0:T(8,128)(2,1)} %get-tuple-element.22), channel_id=1, source_target_pairs={{0,64},{8,72},{16,80},{24,88},{32,96},{40,104},{48,112},{56,120},{... | collective-permute-start | bytes 393224 | tf_op jit(solution)/shard_map/ppermute | solution.py:323
  34.0 10.9 %collective-permute-start.3 = (bf16[256,256]{1,0:T(8,128)(2,1)}, bf16[256,256]{1,0:T(8,128)(2,1)S(1)}, u32[]{:S(2)}, u32[]{:S(2)}) collective-permute-start(bf16[256,256]{1,0:T(8,128)(2,1)} %get-tuple-element.23), channel_id=1, source_target_pairs={{0,32},{8,40},{16,48},{24,56},{32,64},{40,72},{48,80},{56,88},{64,... | collective-permute-start | bytes 393224 | tf_op jit(solution)/shard_map/ppermute | solution.py:323
  38.0 6.9 %collective-permute-start.4 = (bf16[256,256]{1,0:T(8,128)(2,1)}, bf16[256,256]{1,0:T(8,128)(2,1)S(1)}, u32[]{:S(2)}, u32[]{:S(2)}) collective-permute-start(bf16[256,256]{1,0:T(8,128)(2,1)} %get-tuple-element.24), channel_id=1, source_target_pairs={{0,128},{8,136},{16,144},{24,152},{32,160},{40,168},{48,176},{56,1... | collective-permute-start | bytes 393224 | tf_op jit(solution)/shard_map/ppermute | solution.py:323
  41.6 6.4 %copy-start = (bf16[512,256]{1,0:T(8,128)(2,1)S(1)}, bf16[512,256]{1,0:T(8,128)(2,1)}, u32[]{:S(2)}) copy-start(bf16[512,256]{1,0:T(8,128)(2,1)} %o_hbm.1) | copy-start | bytes 786436
  41.6 6.4 %copy-start.3 = (bf16[2048,256]{1,0:T(8,128)(2,1)S(1)}, bf16[2048,256]{1,0:T(8,128)(2,1)}, u32[]{:S(2)}) copy-start(bf16[2048,256]{1,0:T(8,128)(2,1)} %refs_1_.1) | copy-start | bytes 3145732
  41.7 5.2 %collective-permute-start.5 = (bf16[256,256]{1,0:T(8,128)(2,1)S(1)}, bf16[256,256]{1,0:T(8,128)(2,1)S(1)}, u32[]{:S(2)}, u32[]{:S(2)}) collective-permute-start(bf16[256,256]{1,0:T(8,128)(2,1)S(1)} %get-tuple-element.25), channel_id=1, source_target_pairs={{0,16},{8,24},{16,32},{24,40},{32,48},{40,56},{48,64},{56,72},{64,... | collective-permute-start | bytes 393224 | tf_op jit(solution)/shard_map/ppermute | solution.py:323
  44.9 1.9 %copy-start.10 = (bf16[256,256]{1,0:T(8,128)(2,1)}, bf16[256,256]{1,0:T(8,128)(2,1)S(1)}, u32[]{:S(2)}) copy-start(bf16[256,256]{1,0:T(8,128)(2,1)S(1)} %collective-permute-done.2.refs_1_.f3) | copy-start | bytes 393220
  44.9 1.9 %copy-start.11 = (bf16[256,256]{1,0:T(8,128)(2,1)}, bf16[256,256]{1,0:T(8,128)(2,1)S(1)}, u32[]{:S(2)}) copy-start(bf16[256,256]{1,0:T(8,128)(2,1)S(1)} %collective-permute-done.3.refs_2_.f2) | copy-start | bytes 393220
  45.0 1.9 %copy-start.12 = (bf16[256,256]{1,0:T(8,128)(2,1)}, bf16[256,256]{1,0:T(8,128)(2,1)S(1)}, u32[]{:S(2)}) copy-start(bf16[256,256]{1,0:T(8,128)(2,1)S(1)} %collective-permute-done.4.refs_3_.f4) | copy-start | bytes 393220
  51.2 9.5 %collective-permute-start.11 = (bf16[1024,256]{1,0:T(8,128)(2,1)S(1)}, bf16[1024,256]{1,0:T(8,128)(2,1)S(1)}, u32[]{:S(2)}, u32[]{:S(2)}) collective-permute-start(bf16[1024,256]{1,0:T(8,128)(2,1)S(1)} %get-tuple-element.37), channel_id=1, source_target_pairs={{0,8},{8,0},{16,24},{24,16},{32,40},{40,32},{48,56},{56,48},{64,72... | collective-permute-start | bytes 1572872 | tf_op jit(solution)/shard_map/ppermute | solution.py:357
  61.7 40.6 %copy-start.7 = (s32[1,5]{1,0:T(1,128)S(1)}, s32[1,5]{1,0:T(1,128)}, u32[]{:S(2)}) copy-start(s32[1,5]{1,0:T(1,128)} %pick.3) | copy-start | bytes 64
  61.7 24.6 %all-to-all-start.1 = ((bf16[8,4,32,256]{3,2,1,0:T(8,128)(2,1)}), bf16[8,4,32,256]{3,2,1,0:T(8,128)(2,1)S(1)}, u32[]{:S(2)}, u32[]{:S(2)}) async-start(bf16[8,4,32,256]{3,2,1,0:T(8,128)(2,1)} %bitcast), calls=%async_computation.1 | async-start | bytes 1048576 | tf_op jit(solution)/shard_map/all_to_all | solution.py:362
  76.2 26.0 %collective-permute-start.6 = (bf16[768,256]{1,0:T(8,128)(2,1)}, bf16[768,256]{1,0:T(8,128)(2,1)S(1)}, u32[]{:S(2)}, u32[]{:S(2)}) collective-permute-start(bf16[768,256]{1,0:T(8,128)(2,1)} %get-tuple-element.29), channel_id=1, source_target_pairs={{8,0},{16,8},{24,16},{32,24},{40,32},{48,40},{56,48},{64,56},{72,6... | collective-permute-start | bytes 1179656 | tf_op jit(solution)/shard_map/ppermute | solution.py:323
  78.7 23.5 %collective-permute-start.7 = (bf16[256,256]{1,0:T(8,128)(2,1)}, bf16[256,256]{1,0:T(8,128)(2,1)S(1)}, u32[]{:S(2)}, u32[]{:S(2)}) collective-permute-start(bf16[256,256]{1,0:T(8,128)(2,1)} %get-tuple-element.30), channel_id=1, source_target_pairs={{64,0},{72,8},{80,16},{88,24},{96,32},{104,40},{112,48},{120,56},{... | collective-permute-start | bytes 393224 | tf_op jit(solution)/shard_map/ppermute | solution.py:323
  80.0 22.2 %collective-permute-start.8 = (bf16[256,256]{1,0:T(8,128)(2,1)}, bf16[256,256]{1,0:T(8,128)(2,1)S(1)}, u32[]{:S(2)}, u32[]{:S(2)}) collective-permute-start(bf16[256,256]{1,0:T(8,128)(2,1)} %get-tuple-element.31), channel_id=1, source_target_pairs={{32,0},{40,8},{48,16},{56,24},{64,32},{72,40},{80,48},{88,56},{96,... | collective-permute-start | bytes 393224 | tf_op jit(solution)/shard_map/ppermute | solution.py:323
  81.3 20.9 %collective-permute-start.9 = (bf16[256,256]{1,0:T(8,128)(2,1)}, bf16[256,256]{1,0:T(8,128)(2,1)S(1)}, u32[]{:S(2)}, u32[]{:S(2)}) collective-permute-start(bf16[256,256]{1,0:T(8,128)(2,1)} %get-tuple-element.32), channel_id=1, source_target_pairs={{128,0},{136,8},{144,16},{152,24},{160,32},{168,40},{176,48},{184,... | collective-permute-start | bytes 393224 | tf_op jit(solution)/shard_map/ppermute | solution.py:323
  82.6 19.6 %collective-permute-start.10 = (bf16[256,256]{1,0:T(8,128)(2,1)}, bf16[256,256]{1,0:T(8,128)(2,1)S(1)}, u32[]{:S(2)}, u32[]{:S(2)}) collective-permute-start(bf16[256,256]{1,0:T(8,128)(2,1)} %get-tuple-element.33), channel_id=1, source_target_pairs={{16,0},{24,8},{32,16},{40,24},{48,32},{56,40},{64,48},{72,56},{80,... | collective-permute-start | bytes 393224 | tf_op jit(solution)/shard_map/ppermute | solution.py:323
  87.0 22.1 %all-to-all-start.2 = ((bf16[4,32,256]{2,1,0:T(8,128)(2,1)}), bf16[4,32,256]{2,1,0:T(8,128)(2,1)S(1)}, u32[]{:S(2)}, u32[]{:S(2)}) async-start(bf16[4,32,256]{2,1,0:T(8,128)(2,1)} %part_sum.1), calls=%async_computation.2 | async-start | bytes 131072 | tf_op jit(solution)/shard_map/all_to_all | solution.py:364
  102.2 1.2 %copy-start.9 = (f32[1024,256]{1,0:T(8,128)S(1)}, f32[1024,256]{1,0:T(8,128)}, u32[]{:S(2)}) copy-start(f32[1024,256]{1,0:T(8,128)} %get-tuple-element.28.own_ref) | copy-start | bytes 3145732
  (5 other events, 3.6 us)
